TPU v7x, 128 devices: a whole 4x4x4 slice. The times are simulated.
128 devices in a mesh: section: 4 (over z), branch: 32 (over y, x, core).
Axes of the slice: x: 4, y: 4, z: 4, core: 2. Of those that a mesh axis runs over, the one named last changes fastest.
Arguments:
- layer_input: bfloat16 [4, 2, 4096, 4096], P('section', None, 'branch'), may hold values from -6 to 6
- cotangent: bfloat16 [2, 4096, 4096], P(None, 'branch'), may hold values from -6 to 6
- state_in: float32 [4, 2, 4096, 64], P('section', None, 'branch'), may hold values from -2 to 2
- state_out: float32 [4, 2, 4096, 64], P('section', None, 'branch'), may hold values from -2 to 2
- step_size: float32 [4, 2, 4096, 64], P('section', None, 'branch'), may hold values from 0.01 to 0.1
- saved_states: float32 [4, 2, 32, 64, 64, 64], P('section', None, 'branch'), may hold values from -6 to 6
- decay_rate: float32 [4, 64], P('section'), may hold values from 0.001 to 0.3
- skip_gain: float32 [4, 64], P('section'), may hold values from 0.5 to 1.5
- lengths: int32 [2, 16], replicated, may hold values from 32 to 128, as said below
Outputs:
- input_grad: bfloat16 [4, 2, 4096, 4096], P('section', None, 'branch')
- grad_state_in: float32 [4, 2, 4096, 64], P('section', None, 'branch')
- grad_state_out: float32 [4, 2, 4096, 64], P('section', None, 'branch')
- grad_step: float32 [4, 2, 4096, 64], P('section', None, 'branch')
- grad_decay: float32 [4, 64], P('section')
- grad_skip: float32 [4, 64], P('section')
Inputs may be any that keep to these rules, and one draw needn't show every extreme that they name: lengths[m, j] counts the live tokens of completion j of family m; every family has a completion of exactly 128.
All inputs are finite; a program needn't handle non-finite values.
Results may differ from a plain program's by a relative error of at most 0.0058.
Values may be sent and summed in bfloat16 or wider, within the bound.
No kernel may reach another device: no remote copies, remote signals or barrier semaphores. Data moves between devices by JAX's collectives and lax.ppermute only.
A program may use at most 384 MiB of HBM per device.

v0:
```python
import math

import jax
import jax.numpy as jnp
from jax import lax
from jax.sharding import PartitionSpec as P

HIGH = lax.Precision.HIGHEST


def from_behind(x, axis, by):
    count = lax.axis_size(axis)
    pairs = [(i, i + by) for i in range(count) if 0 <= i + by < count]
    return lax.ppermute(x, axis, pairs)


def prefix(value, axis, join, neutral):
    count, mine = (lax.axis_size(axis), lax.axis_index(axis))
    pieces = jax.tree.map(lambda part: lax.all_gather(part, axis), value)
    pieces = jax.tree.map(lambda part: part[::-1], pieces)
    mine = count - 1 - mine
    running = jax.tree.map(
        lambda part, zero: jnp.full_like(part, 0) + jnp.asarray(zero, part.dtype), value, neutral
    )

    def turn(position, running):
        longer = join(running, jax.tree.map(lambda part: part[position], pieces))
        return jax.tree.map(lambda new, old: jnp.where(position < mine, new, old), longer, running)

    return lax.fori_loop(0, count - 1, turn, running)


def decay_logs(step_rows, decay_vec):
    return jnp.cumsum(-decay_vec[None, :] * step_rows, axis=0)


def start_grad(upstream, out_rows, logdec):
    carried = jnp.exp(logdec)
    begin_grad = jnp.einsum("thp,tn->hpn", upstream * carried[:, :, None], out_rows, precision=HIGH)
    return (jnp.exp(logdec[-1]), begin_grad)


def local_terms(layer_x, upstream, in_rows, out_rows, step_rows, logdec):
    row_count = layer_x.shape[0]
    causal = jnp.arange(row_count)[:, None] >= jnp.arange(row_count)[None, :]
    lograte = logdec.T
    spread = lograte[:, :, None] - lograte[:, None, :]
    kernel = jnp.where(causal[None], jnp.exp(jnp.where(causal[None], spread, 0.0)), 0.0)
    affinity = jnp.dot(out_rows, in_rows.T, precision=HIGH)
    weighted = kernel * affinity[None]
    pair_grad = jnp.einsum("thp,uhp->htu", upstream, layer_x, precision=HIGH)
    scaled = kernel * pair_grad * step_rows.T[:, None, :]
    back_x = jnp.einsum("htu,thp->uhp", weighted, upstream, precision=HIGH)
    back_in = jnp.einsum("htu,tn->un", scaled, out_rows, precision=HIGH)
    back_out = jnp.einsum("htu,un->tn", scaled, in_rows, precision=HIGH)
    mixed_terms = scaled * affinity[None]
    back_log = (jnp.sum(mixed_terms, axis=2) - jnp.sum(mixed_terms, axis=1)).T
    return (back_x, back_in, back_out, back_log)


def first_part(upstream, in_rows, step_rows, logdec, gain_vec, end_grad, back_x):
    remain = jnp.exp(logdec[-1][None, :] - logdec)
    end_in = jnp.einsum("un,hpn->uhp", in_rows, end_grad, precision=HIGH)
    state_pull = back_x + remain[:, :, None] * end_in
    input_grad = gain_vec[None, :, None] * upstream + step_rows[:, :, None] * state_pull
    return (input_grad, state_pull, end_in)


def rest_part(
    layer_x,
    upstream,
    out_rows,
    step_rows,
    logdec,
    decay_vec,
    saved_state,
    end_grad,
    local_part,
    state_pull,
    end_in,
):
    back_in, back_out, back_log = (local_part[1], local_part[2], local_part[3])
    row_count = layer_x.shape[0]
    carried = jnp.exp(logdec)
    remain = jnp.exp(logdec[-1][None, :] - logdec)
    end_x = jnp.einsum("uhp,hpn->uhn", layer_x, end_grad, precision=HIGH)
    grad_in = back_in + jnp.einsum("uh,uhn->un", step_rows * remain, end_x, precision=HIGH)
    up_saved = jnp.einsum("thp,hpn->thn", upstream, saved_state, precision=HIGH)
    grad_out = back_out + jnp.einsum("th,thn->tn", carried, up_saved, precision=HIGH)
    read_saved = jnp.einsum("tn,hpn->thp", out_rows, saved_state, precision=HIGH)
    end_flow = step_rows * remain * jnp.sum(layer_x * end_in, axis=2)
    last_term = jnp.exp(logdec[-1]) * jnp.sum(end_grad * saved_state, axis=(1, 2)) + jnp.sum(
        end_flow, axis=0
    )
    is_last = jnp.arange(row_count) == row_count - 1
    grad_log = back_log + carried * jnp.sum(upstream * read_saved, axis=2) - end_flow
    grad_log = grad_log + jnp.where(is_last[:, None], last_term[None, :], 0.0)
    grad_rate = jnp.cumsum(grad_log[::-1], axis=0)[::-1]
    grad_step = jnp.sum(layer_x * state_pull, axis=2) - decay_vec[None, :] * grad_rate
    decay_part = jnp.sum(-step_rows * grad_rate, axis=0)
    skip_part = jnp.sum(layer_x * upstream, axis=(0, 2))
    return (grad_in, grad_out, grad_step, decay_part, skip_part)


def combine(earlier, later):
    return (later[0] * earlier[0], later[0][:, None, None] * earlier[1] + later[1])


def pass_down(sent_grad):
    return from_behind(sent_grad, "section", -1)


def shards(
    layer_input,
    cotangent,
    state_in,
    state_out,
    step_size,
    saved_states,
    decay_rate,
    skip_gain,
    lengths,
):
    section_count = lax.axis_size("section")
    branches = lax.axis_size("branch")
    half_branch = branches // 2
    section_at = lax.axis_index("section")
    branch_at = lax.axis_index("branch")
    micro_count = layer_input.shape[1]
    row_count = layer_input.shape[2]
    feature_count = layer_input.shape[3]
    head_count = decay_rate.shape[1]
    head_size = feature_count // head_count
    state_count = state_in.shape[3]
    is_completion = branch_at >= half_branch
    comp_slot = jnp.clip(branch_at - half_branch, 0, half_branch - 1)
    grad_scale = 1.0 / math.sqrt(micro_count * row_count * branches * head_size)
    decay_vec = decay_rate[0]
    gain_vec = skip_gain[0]
    row_ids = jnp.arange(row_count)
    unit_decay = jnp.ones((head_count,), jnp.float32)
    zero_state = jnp.zeros((head_count, head_size, state_count), jnp.float32)
    zero_rows = jnp.zeros((row_count, head_count, head_size), jnp.float32)
    zero_proj = jnp.zeros((row_count, state_count), jnp.float32)
    zero_step = jnp.zeros((row_count, head_count), jnp.float32)
    zero_head = jnp.zeros((head_count,), jnp.float32)
    received = jnp.zeros((row_count, feature_count), jnp.bfloat16)
    all_input = jnp.zeros((micro_count, row_count, feature_count), jnp.bfloat16)
    all_in = jnp.zeros((micro_count, row_count, state_count), jnp.float32)
    all_out = jnp.zeros((micro_count, row_count, state_count), jnp.float32)
    all_step = jnp.zeros((micro_count, row_count, head_count), jnp.float32)
    decay_sum = zero_head
    skip_sum = zero_head
    tick_count = section_count + micro_count - 1
    for moment in range(tick_count):
        position = moment - (section_count - 1 - section_at)
        active = (position >= 0) & (position < micro_count)
        chosen = jnp.clip(position, 0, micro_count - 1)
        limit = jnp.where(is_completion, lengths[chosen, comp_slot], row_count)
        top_grad = jnp.where((row_ids < limit)[:, None], cotangent[chosen].astype(jnp.float32), 0.0)
        upstream = jnp.where(
            section_at == section_count - 1, top_grad, received.astype(jnp.float32)
        )
        upstream = upstream.reshape(row_count, head_count, head_size)
        layer_x = (
            layer_input[0, chosen].astype(jnp.float32).reshape(row_count, head_count, head_size)
        )
        in_rows = state_in[0, chosen]
        out_rows = state_out[0, chosen]
        step_rows = step_size[0, chosen]
        saved_state = saved_states[0, chosen, 0]
        logdec = decay_logs(step_rows, decay_vec)
        decay_total, begin_grad = lax.cond(
            active, lambda: start_grad(upstream, out_rows, logdec), lambda: (zero_head, zero_state)
        )
        element = (jnp.where(is_completion, 1.0, decay_total), begin_grad)
        reach_decay, end_grad = prefix(element, "branch", combine, (unit_decay, zero_state))
        end_grad = jnp.where(is_completion, 0.0, end_grad)
        local_part = lax.cond(
            active,
            lambda: local_terms(layer_x, upstream, in_rows, out_rows, step_rows, logdec),
            lambda: (zero_rows, zero_proj, zero_proj, zero_step),
        )

        def finish_all():
            first = first_part(
                upstream, in_rows, step_rows, logdec, gain_vec, end_grad, local_part[0]
            )
            rest = rest_part(
                layer_x,
                upstream,
                out_rows,
                step_rows,
                logdec,
                decay_vec,
                saved_state,
                end_grad,
                local_part,
                first[1],
                first[2],
            )
            return (first[0],) + rest

        results = lax.cond(
            active,
            finish_all,
            lambda: (zero_rows, zero_proj, zero_proj, zero_step, zero_head, zero_head),
        )
        sent_grad = results[0].reshape(row_count, feature_count).astype(jnp.bfloat16)
        rest = results[1:]
        if moment < tick_count - 1:
            received = pass_down(sent_grad)
        all_input = all_input.at[chosen].set(jnp.where(active, sent_grad, all_input[chosen]))
        all_in = all_in.at[chosen].set(jnp.where(active, rest[0], all_in[chosen]))
        all_out = all_out.at[chosen].set(jnp.where(active, rest[1], all_out[chosen]))
        all_step = all_step.at[chosen].set(jnp.where(active, rest[2], all_step[chosen]))
        decay_sum = decay_sum + rest[3]
        skip_sum = skip_sum + rest[4]
    decay_sum, skip_sum = lax.psum((decay_sum, skip_sum), "branch")
    return (
        all_input[None],
        all_in[None],
        all_out[None],
        all_step[None],
        (decay_sum * grad_scale)[None],
        (skip_sum * grad_scale)[None],
    )


def solution(mesh):
    placed = (
        P("section", None, "branch", None),
        P(None, "branch", None),
        P("section", None, "branch", None),
        P("section", None, "branch", None),
        P("section", None, "branch", None),
        P("section", None, "branch", None, None, None),
        P("section", None),
        P("section", None),
        P(),
    )
    return jax.shard_map(
        shards,
        mesh=mesh,
        in_specs=placed,
        out_specs=(
            P("section", None, "branch", None),
            P("section", None, "branch", None),
            P("section", None, "branch", None),
            P("section", None, "branch", None),
            P("section", None),
            P("section", None),
        ),
        check_vma=False,
    )
```

profile of v0, /device:TPU:0, one launch (start us, length us, event | category | flops | bytes accessed | tf_op | source)
XLA Modules:
  0.0 2194.9 jit_solution(7350356176887559500)
XLA Ops:
  9.5 5.3 constant_dynamic-slice_fusion.9
  24.7 69.8 %all-reduce = f32[2048]{0:T(1024)S(1)} all-reduce(f32[2048]{0:T(1024)S(1)} %fusion.206), channel_id=2, replica_groups=mesh['section'=4,'branch'=32] {'branch'}, use_global_device_ids=true, to_apply=%add | all-reduce | flops 2048 | bytes 16384
  94.5 7.0 dynamic-slice_convert_fusion
  106.2 124.5 %all-gather.16.cloned.1.call-done = f32[2048,64,64]{2,1,0:T(8,128)} async-done(((f32[64,64,64]{2,1,0:T(8,128)}), f32[2048,64,64]{2,1,0:T(8,128)}) %all-gather.16.cloned.1.call-update) | async-done | bytes 33554448 | tf_op jit(solution)/shard_map/all_gather | solution.py:19
  230.7 43.7 %rev.71 = f32[32,64,64,64]{3,2,1,0:T(8,128)} reverse(f32[32,64,64,64]{3,2,1,0:T(8,128)} %bitcast.112), dimensions={0} | reverse | bytes 67108864 | tf_op jit(solution)/shard_map/rev | solution.py:20
  274.4 65.8 %while.90 = (s32[]{:T(128)}, f32[64,64,64]{2,1,0:T(8,128)S(1)}, s32[]{:T(128)}, f32[32,64]{1,0:T(8,128)S(1)}, f32[32,64,64,64]{3,2,1,0:T(8,128)}, /*index=5*/s32[]{:T(128)}, s32[]{:T(128)}) while((s32[]{:T(128)}, f32[64,64,64]{2,1,0:T(8,128)S(1)}, s32[]{:T(128)}, f32[32,64]{1,0:T(8,128)S(1)}, f32[32,64,64,64]{3,2,1,0:T(8,128)}, ...), condition=%wide.region_10.11_spmd.clone, body=%wide.region_9.10_spmd.clone.sunk | while | flops 1048580 | bytes 3146601 | solution.py:30
  348.9 23.1 %collective-permute-done = bf16[128,4096]{0,1:T(8,128)(2,1)} collective-permute-done((bf16[128,4096]{0,1:T(8,128)(2,1)}, bf16[128,4096]{0,1:T(8,128)(2,1)}, u32[]{:S(2)}, u32[]{:S(2)}) %collective-permute-start) | collective-permute-done | bytes 1048608 | tf_op jit(solution)/shard_map/ppermute | solution.py:14
  379.8 66.3 %all-reduce.1 = f32[2048]{0:T(1024)S(1)} all-reduce(f32[2048]{0:T(1024)S(1)} %fusion.207), channel_id=4, replica_groups=mesh['section'=4,'branch'=32] {'branch'}, use_global_device_ids=true, to_apply=%add.1 | all-reduce | flops 2048 | bytes 16384
  448.3 165.8 %all-gather.18.cloned.1.call-done = f32[2048,64,64]{2,1,0:T(8,128)} async-done(((f32[64,64,64]{2,1,0:T(8,128)}), f32[2048,64,64]{2,1,0:T(8,128)}) %all-gather.18.cloned.1.call-update) | async-done | bytes 33554448 | tf_op jit(solution)/shard_map/all_gather | solution.py:19
  614.1 43.7 %rev.73 = f32[32,64,64,64]{3,2,1,0:T(8,128)} reverse(f32[32,64,64,64]{3,2,1,0:T(8,128)} %bitcast.122), dimensions={0} | reverse | bytes 67108864 | tf_op jit(solution)/shard_map/rev | solution.py:20
  657.8 119.5 %while.91 = (s32[]{:T(128)}, f32[64,64,64]{2,1,0:T(8,128)}, s32[]{:T(128)}, f32[32,64]{1,0:T(8,128)S(1)}, f32[32,64,64,64]{3,2,1,0:T(8,128)}, /*index=5*/s32[]{:T(128)}, s32[]{:T(128)}) while((s32[]{:T(128)}, f32[64,64,64]{2,1,0:T(8,128)}, s32[]{:T(128)}, f32[32,64]{1,0:T(8,128)S(1)}, f32[32,64,64,64]{3,2,1,0:T(8,128)}, ...), condition=%wide.region_31.32_spmd.clone, body=%wide.region_30.31_spmd.clone.sunk | while | flops 1048580 | bytes 3146601 | solution.py:30
  661.1 3.9 fusion.303
  665.0 3.9 fusion.303
  668.8 3.9 fusion.303
  672.7 3.9 fusion.303
  676.6 3.9 fusion.303
  684.3 3.9 fusion.303
  688.2 3.9 fusion.303
  692.1 3.9 fusion.303
  696.0 3.9 fusion.303
  699.8 3.9 fusion.303
  711.5 3.9 fusion.303
  715.3 3.9 fusion.303
  719.2 3.9 fusion.303
  723.1 3.9 fusion.303
  734.7 3.9 fusion.303
  738.6 3.9 fusion.303
  742.5 3.9 fusion.303
  746.3 3.9 fusion.303
  777.3 5.7 conditional.20
  787.5 23.1 %collective-permute-done.1 = bf16[128,4096]{0,1:T(8,128)(2,1)} collective-permute-done((bf16[128,4096]{0,1:T(8,128)(2,1)}, bf16[128,4096]{0,1:T(8,128)(2,1)}, u32[]{:S(2)}, u32[]{:S(2)}) %collective-permute-start.1) | collective-permute-done | bytes 1048608 | tf_op jit(solution)/shard_map/ppermute | solution.py:14
  818.5 66.6 %all-reduce.2 = f32[2048]{0:T(1024)S(1)} all-reduce(f32[2048]{0:T(1024)S(1)} %fusion.208), channel_id=6, replica_groups=mesh['section'=4,'branch'=32] {'branch'}, use_global_device_ids=true, to_apply=%add.2 | all-reduce | flops 2048 | bytes 16384
  885.2 17.4 conditional.22
  902.6 144.9 %all-gather.20.cloned.1.call-done = f32[2048,64,64]{2,1,0:T(8,128)} async-done(((f32[64,64,64]{2,1,0:T(8,128)}), f32[2048,64,64]{2,1,0:T(8,128)}) %all-gather.20.cloned.1.call-update) | async-done | bytes 33554448 | tf_op jit(solution)/shard_map/all_gather | solution.py:19
  1047.4 43.6 %rev.75 = f32[32,64,64,64]{3,2,1,0:T(8,128)} reverse(f32[32,64,64,64]{3,2,1,0:T(8,128)} %bitcast.133), dimensions={0} | reverse | bytes 67108864 | tf_op jit(solution)/shard_map/rev | solution.py:20
  1091.1 119.5 %while.92 = (s32[]{:T(128)}, f32[64,64,64]{2,1,0:T(8,128)}, s32[]{:T(128)}, f32[32,64]{1,0:T(8,128)S(1)}, f32[32,64,64,64]{3,2,1,0:T(8,128)}, /*index=5*/s32[]{:T(128)}, s32[]{:T(128)}) while((s32[]{:T(128)}, f32[64,64,64]{2,1,0:T(8,128)}, s32[]{:T(128)}, f32[32,64]{1,0:T(8,128)S(1)}, f32[32,64,64,64]{3,2,1,0:T(8,128)}, ...), condition=%wide.region_52.53_spmd.clone, body=%wide.region_51.52_spmd.clone.sunk | while | flops 1048580 | bytes 3146601 | solution.py:30
  1217.8 53.9 %collective-permute-done.2 = bf16[128,4096]{0,1:T(8,128)(2,1)} collective-permute-done((bf16[128,4096]{0,1:T(8,128)(2,1)}, bf16[128,4096]{0,1:T(8,128)(2,1)}, u32[]{:S(2)}, u32[]{:S(2)}) %collective-permute-start.2) | collective-permute-done | bytes 1048608 | tf_op jit(solution)/shard_map/ppermute | solution.py:14
  1274.9 4.8 conditional.24
  1275.0 4.7 fusion.56
  1282.8 67.4 %all-reduce.3 = f32[2048]{0:T(1024)S(1)} all-reduce(f32[2048]{0:T(1024)S(1)} %fusion.209), channel_id=8, replica_groups=mesh['section'=4,'branch'=32] {'branch'}, use_global_device_ids=true, to_apply=%add.3 | all-reduce | flops 2048 | bytes 16384
  1350.4 18.1 conditional.25
  1351.0 11.0 multiply_reduce_fusion.6
  1362.4 6.0 fusion.52
  1368.5 110.6 %all-gather.22.cloned.1.call-done = f32[2048,64,64]{2,1,0:T(8,128)} async-done(((f32[64,64,64]{2,1,0:T(8,128)}), f32[2048,64,64]{2,1,0:T(8,128)}) %all-gather.22.cloned.1.call-update) | async-done | bytes 33554448 | tf_op jit(solution)/shard_map/all_gather | solution.py:19
  1479.1 43.6 %rev.77 = f32[32,64,64,64]{3,2,1,0:T(8,128)} reverse(f32[32,64,64,64]{3,2,1,0:T(8,128)} %bitcast.144), dimensions={0} | reverse | bytes 67108864 | tf_op jit(solution)/shard_map/rev | solution.py:20
  1522.6 119.5 %while.93 = (s32[]{:T(128)}, f32[64,64,64]{2,1,0:T(8,128)}, s32[]{:T(128)}, f32[32,64]{1,0:T(8,128)S(1)}, f32[32,64,64,64]{3,2,1,0:T(8,128)}, /*index=5*/s32[]{:T(128)}, s32[]{:T(128)}) while((s32[]{:T(128)}, f32[64,64,64]{2,1,0:T(8,128)}, s32[]{:T(128)}, f32[32,64]{1,0:T(8,128)S(1)}, f32[32,64,64,64]{3,2,1,0:T(8,128)}, ...), condition=%wide.region_73.74_spmd.clone, body=%wide.region_72.73_spmd.clone.sunk | while | flops 1048580 | bytes 3146601 | solution.py:30
  1642.1 33.4 %conditional.26 = (f32[64]{0:T(128)S(1)}, f32[64]{0:T(128)S(1)}, bf16[128,4096]{0,1:T(8,128)(2,1)}, bf16[128,4096]{1,0:T(8,128)(2,1)}, f32[128,64]{0,1:T(8,128)S...) conditional(s32[]{:T(128)} %convert_element_type.172, () %tuple.319, (f32[128,64]{1,0:T(8,128)S(1)}, ...), branch_computations={%region_74.75_spmd, %region_75.84_spmd} | conditional | flops 1621983232 | bytes 64164024 | solution.py:204
  1642.3 5.7 copy.267
  1654.4 6.8 multiply_reduce_fusion.23
  1668.1 4.5 fusion.155
  1680.1 23.0 %collective-permute-done.3 = bf16[128,4096]{0,1:T(8,128)(2,1)} collective-permute-done((bf16[128,4096]{0,1:T(8,128)(2,1)}, bf16[128,4096]{0,1:T(8,128)(2,1)}, u32[]{:S(2)}, u32[]{:S(2)}) %collective-permute-start.3) | collective-permute-done | bytes 1048608 | tf_op jit(solution)/shard_map/ppermute | solution.py:14
  1706.3 4.8 conditional.27
  1706.4 4.7 fusion.71
  1733.9 67.4 %all-reduce.4 = f32[2048]{0:T(1024)S(1)} all-reduce(f32[2048]{0:T(1024)S(1)} %fusion.210), channel_id=10, replica_groups=mesh['section'=4,'branch'=32] {'branch'}, use_global_device_ids=true, to_apply=%add.4 | all-reduce | flops 2048 | bytes 16384
  1801.4 18.0 conditional.28
  1802.0 10.9 multiply_reduce_fusion.8
  1813.3 6.0 fusion.67
  1819.4 90.1 %all-gather.24.cloned.1.call-done = f32[2048,64,64]{2,1,0:T(8,128)} async-done(((f32[64,64,64]{2,1,0:T(8,128)}), f32[2048,64,64]{2,1,0:T(8,128)}) %all-gather.24.cloned.1.call-update) | async-done | bytes 33554448 | tf_op jit(solution)/shard_map/all_gather | solution.py:19
  1909.5 43.6 %rev.79 = f32[32,64,64,64]{3,2,1,0:T(8,128)} reverse(f32[32,64,64,64]{3,2,1,0:T(8,128)} %bitcast.156), dimensions={0} | reverse | bytes 67108864 | tf_op jit(solution)/shard_map/rev | solution.py:20
  1953.1 119.3 %while.94 = (s32[]{:T(128)}, f32[64,64,64]{2,1,0:T(8,128)}, s32[]{:T(128)}, f32[32,64]{1,0:T(8,128)S(1)}, f32[32,64,64,64]{3,2,1,0:T(8,128)}, /*index=5*/s32[]{:T(128)}, s32[]{:T(128)}) while((s32[]{:T(128)}, f32[64,64,64]{2,1,0:T(8,128)}, s32[]{:T(128)}, f32[32,64]{1,0:T(8,128)S(1)}, f32[32,64,64,64]{3,2,1,0:T(8,128)}, ...), condition=%wide.region_94.95_spmd.clone, body=%wide.region_93.94_spmd.clone.sunk | while | flops 1048580 | bytes 3146601 | solution.py:30
  2072.4 41.6 %conditional.29 = (f32[64]{0:T(128)S(1)}, f32[64]{0:T(128)S(1)}, bf16[128,4096]{1,0:T(8,128)(2,1)S(1)}, f32[128,64]{0,1:T(8,128)S(1)}, f32[128,64]{0,1:T(8,128)S(1)}, /*index=5*/f32[128,64]{0,1:T(8,128)S(1)}) conditional(s32[]{:T(128)} %convert_element_type.178, () %tuple.326, (f32[128,64]{1,0:T(8,128)S(1)}, f32[128,64]{0,1:T(8,128)S(1)}, ...), branch_computations={%region_95.96_spmd, %region_96.105_spmd} | conditional | flops 1621983232 | bytes 69540360 | solution.py:204
  2073.2 5.6 copy.280
  2085.2 6.6 multiply_reduce_fusion.27
  2115.3 64.8 %all-reduce.5 = (f32[64]{0:T(128)S(1)}, f32[64]{0:T(128)S(1)}) all-reduce(f32[64]{0:T(128)S(1)} %add_add_fusion.1, f32[64]{0:T(128)S(1)} %add_add_fusion), channel_id=1, replica_groups=mesh['section'=4,'branch'=32] {'branch'}, use_global_device_ids=true, to_apply=%region_105.106 | all-reduce | flops 128 | bytes 1024 | tf_op jit(solution)/shard_map/psum | solution.py:219
  (667 shorter events, 631.6 us)
Async XLA Ops:
  7.2 223.5 %all-gather.16.cloned.1.call-start = ((), (), s32[]{:S(2)}) async-start(), calls=%async_computation | async-start | bytes 69206016 | tf_op jit(solution)/shard_map/all_gather | solution.py:19
  14.7 1.8 copy-start.63
  14.7 1.8 copy-start.36
  14.7 2.9 copy-start.37
  14.7 2.9 copy-start.38
  23.2 590.9 %all-gather.18.cloned.1.call-start = ((), (), s32[]{:S(2)}) async-start(), calls=%async_computation.1 | async-start | bytes 69206016 | tf_op jit(solution)/shard_map/all_gather | solution.py:19
  344.4 30.7 %copy-start.54 = (f32[128,64]{0,1:T(8,128)}, f32[128,64]{0,1:T(8,128)S(1)}, u32[]{:S(2)}) copy-start(f32[128,64]{0,1:T(8,128)S(1)} %get-tuple-element.1902) | copy-start | bytes 98308
  344.4 30.7 %copy-start.56 = (f32[128,64]{0,1:T(8,128)}, f32[128,64]{0,1:T(8,128)S(1)}, u32[]{:S(2)}) copy-start(f32[128,64]{0,1:T(8,128)S(1)} %get-tuple-element.1903) | copy-start | bytes 98308
  344.4 30.7 %copy-start.58 = (f32[128,64]{0,1:T(8,128)}, f32[128,64]{0,1:T(8,128)S(1)}, u32[]{:S(2)}) copy-start(f32[128,64]{0,1:T(8,128)S(1)} %get-tuple-element.1904) | copy-start | bytes 98308
  344.4 30.7 %copy-start.66 = (f32[64]{0:T(128)}, f32[64]{0:T(128)S(1)}, u32[]{:S(2)}) copy-start(f32[64]{0:T(128)S(1)} %get-tuple-element.1441) | copy-start | bytes 772
  344.5 30.7 %copy-start.68 = (f32[64]{0:T(128)}, f32[64]{0:T(128)S(1)}, u32[]{:S(2)}) copy-start(f32[64]{0:T(128)S(1)} %get-tuple-element.1446) | copy-start | bytes 772
  344.5 27.5 %collective-permute-start = (bf16[128,4096]{0,1:T(8,128)(2,1)}, bf16[128,4096]{0,1:T(8,128)(2,1)}, u32[]{:S(2)}, u32[]{:S(2)}) collective-permute-start(bf16[128,4096]{0,1:T(8,128)(2,1)} %get-tuple-element.1393), channel_id=1, source_target_pairs={{32,0},{64,32},{96,64},{33,1},{65,33},{97,65},{34,2},{66,34},{98,6... | collective-permute-start | bytes 3145736 | tf_op jit(solution)/shard_map/ppermute | solution.py:14
  376.8 670.7 %all-gather.20.cloned.1.call-start = ((), (), s32[]{:S(2)}) async-start(), calls=%async_computation.2 | async-start | bytes 69206016 | tf_op jit(solution)/shard_map/all_gather | solution.py:19
  783.0 30.8 %copy-start.41 = (f32[128,64]{0,1:T(8,128)}, f32[128,64]{0,1:T(8,128)S(1)}, u32[]{:S(2)}) copy-start(f32[128,64]{0,1:T(8,128)S(1)} %get-tuple-element.1906) | copy-start | bytes 98308
  783.0 30.8 %copy-start.43 = (f32[128,64]{0,1:T(8,128)}, f32[128,64]{0,1:T(8,128)S(1)}, u32[]{:S(2)}) copy-start(f32[128,64]{0,1:T(8,128)S(1)} %get-tuple-element.1907) | copy-start | bytes 98308
  783.0 30.8 %copy-start.45 = (f32[128,64]{0,1:T(8,128)}, f32[128,64]{0,1:T(8,128)S(1)}, u32[]{:S(2)}) copy-start(f32[128,64]{0,1:T(8,128)S(1)} %get-tuple-element.1908) | copy-start | bytes 98308
  783.1 30.7 %copy-start.69 = (f32[64]{0:T(128)}, f32[64]{0:T(128)S(1)}, u32[]{:S(2)}) copy-start(f32[64]{0:T(128)S(1)} %get-tuple-element.1442) | copy-start | bytes 772
  783.1 30.7 %copy-start.70 = (f32[64]{0:T(128)}, f32[64]{0:T(128)S(1)}, u32[]{:S(2)}) copy-start(f32[64]{0:T(128)S(1)} %get-tuple-element.1447) | copy-start | bytes 772
  783.1 4.2 copy-start.62
  783.1 27.5 %collective-permute-start.1 = (bf16[128,4096]{0,1:T(8,128)(2,1)}, bf16[128,4096]{0,1:T(8,128)(2,1)}, u32[]{:S(2)}, u32[]{:S(2)}) collective-permute-start(bf16[128,4096]{0,1:T(8,128)(2,1)} %get-tuple-element.1401), channel_id=1, source_target_pairs={{32,0},{64,32},{96,64},{33,1},{65,33},{97,65},{34,2},{66,34},{98,6... | collective-permute-start | bytes 3145736 | tf_op jit(solution)/shard_map/ppermute | solution.py:14
  787.5 26.3 %copy-start.29 = (f32[128,64]{0,1:T(8,128)S(1)}, f32[128,64]{0,1:T(8,128)}, u32[]{:S(2)}) copy-start(f32[128,64]{0,1:T(8,128)} %get-tuple-element.2100) | copy-start | bytes 98308
  815.4 663.6 %all-gather.22.cloned.1.call-start = ((), (), s32[]{:S(2)}) async-start(), calls=%async_computation.3 | async-start | bytes 69206016 | tf_op jit(solution)/shard_map/all_gather | solution.py:19
  815.5 69.7 %copy-start.32 = (f32[128,64]{0,1:T(8,128)S(1)}, f32[128,64]{0,1:T(8,128)}, u32[]{:S(2)}) copy-start(f32[128,64]{0,1:T(8,128)} %get-tuple-element.2081) | copy-start | bytes 98308
  815.5 69.7 %copy-start.35 = (f32[1,1,128,64]{2,3,1,0:T(8,128)S(1)}, f32[1,1,128,64]{2,3,1,0:T(8,128)}, u32[]{:S(2)}) copy-start(f32[1,1,128,64]{2,3,1,0:T(8,128)} %get-tuple-element.2075) | copy-start | bytes 98308
  1213.3 61.6 %copy-start.71 = (f32[64]{0:T(128)}, f32[64]{0:T(128)S(1)}, u32[]{:S(2)}) copy-start(f32[64]{0:T(128)S(1)} %get-tuple-element.1443) | copy-start | bytes 772
  1213.3 61.5 %copy-start.72 = (f32[64]{0:T(128)}, f32[64]{0:T(128)S(1)}, u32[]{:S(2)}) copy-start(f32[64]{0:T(128)S(1)} %get-tuple-element.1448) | copy-start | bytes 772
  1213.3 4.2 copy-start.61
  1213.3 58.4 %collective-permute-start.2 = (bf16[128,4096]{0,1:T(8,128)(2,1)}, bf16[128,4096]{0,1:T(8,128)(2,1)}, u32[]{:S(2)}, u32[]{:S(2)}) collective-permute-start(bf16[128,4096]{0,1:T(8,128)(2,1)} %get-tuple-element.1409), channel_id=1, source_target_pairs={{32,0},{64,32},{96,64},{33,1},{65,33},{97,65},{34,2},{66,34},{98,6... | collective-permute-start | bytes 3145736 | tf_op jit(solution)/shard_map/ppermute | solution.py:14
  1217.8 57.0 %copy-start.28 = (f32[128,64]{0,1:T(8,128)S(1)}, f32[128,64]{0,1:T(8,128)}, u32[]{:S(2)}) copy-start(f32[128,64]{0,1:T(8,128)} %get-tuple-element.2097) | copy-start | bytes 98308
  1279.7 629.8 %all-gather.24.cloned.1.call-start = ((), (), s32[]{:S(2)}) async-start(), calls=%async_computation.4 | async-start | bytes 69206016 | tf_op jit(solution)/shard_map/all_gather | solution.py:19
  1279.8 70.6 %copy-start.31 = (f32[128,64]{0,1:T(8,128)S(1)}, f32[128,64]{0,1:T(8,128)}, u32[]{:S(2)}) copy-start(f32[128,64]{0,1:T(8,128)} %get-tuple-element.2084) | copy-start | bytes 98308
  1279.8 70.6 %copy-start.34 = (f32[1,1,128,64]{2,3,1,0:T(8,128)S(1)}, f32[1,1,128,64]{2,3,1,0:T(8,128)}, u32[]{:S(2)}) copy-start(f32[1,1,128,64]{2,3,1,0:T(8,128)} %get-tuple-element.2077) | copy-start | bytes 98308
  1350.9 11.5 copy-start.7
  1650.9 3.0 copy-start.8
  1650.9 3.5 copy-start.24
  1653.9 7.3 copy-start.18
  1654.4 7.0 copy-start.13
  1675.6 4.3 copy-start.73
  1675.6 30.7 %copy-start.74 = (f32[64]{0:T(128)}, f32[64]{0:T(128)S(1)}, u32[]{:S(2)}) copy-start(f32[64]{0:T(128)S(1)} %get-tuple-element.1449) | copy-start | bytes 772
  1675.6 4.2 copy-start.60
  1675.6 27.5 %collective-permute-start.3 = (bf16[128,4096]{0,1:T(8,128)(2,1)}, bf16[128,4096]{0,1:T(8,128)(2,1)}, u32[]{:S(2)}, u32[]{:S(2)}) collective-permute-start(bf16[128,4096]{0,1:T(8,128)(2,1)} %get-tuple-element.1417), channel_id=1, source_target_pairs={{32,0},{64,32},{96,64},{33,1},{65,33},{97,65},{34,2},{66,34},{98,6... | collective-permute-start | bytes 3145736 | tf_op jit(solution)/shard_map/ppermute | solution.py:14
  1680.1 26.2 %copy-start.27 = (f32[128,64]{0,1:T(8,128)S(1)}, f32[128,64]{0,1:T(8,128)}, u32[]{:S(2)}) copy-start(f32[128,64]{0,1:T(8,128)} %get-tuple-element.2101) | copy-start | bytes 98308
  1711.2 3.0 copy-start.65
  1711.2 4.5 copy-start.59
  1711.2 5.2 copy-start.57
  1711.2 5.9 copy-start.55
  1718.0 2.5 copy-start.42
  1731.7 2.1 copy-start.9
  1731.7 69.7 %copy-start.30 = (f32[128,64]{0,1:T(8,128)S(1)}, f32[128,64]{0,1:T(8,128)}, u32[]{:S(2)}) copy-start(f32[128,64]{0,1:T(8,128)} %get-tuple-element.2080) | copy-start | bytes 98308
  1731.7 69.7 %copy-start.33 = (f32[1,1,128,64]{2,3,1,0:T(8,128)S(1)}, f32[1,1,128,64]{2,3,1,0:T(8,128)}, u32[]{:S(2)}) copy-start(f32[1,1,128,64]{2,3,1,0:T(8,128)} %get-tuple-element.2028) | copy-start | bytes 98308
  1802.0 11.3 copy-start.1
  2072.4 42.3 %copy-start.67 = (f32[64]{0:T(128)S(1)}, f32[64]{0:T(128)}, u32[]{:S(2)}) copy-start(f32[64]{0:T(128)} %copy-done.66) | copy-start | bytes 772
  2072.4 6.4 copy-start.49
  2072.4 6.4 copy-start.51
  2072.4 6.4 copy-start.52
  2081.7 3.0 copy-start.2
  2081.7 3.5 copy-start.21
  2081.7 3.5 copy-start.40
  2084.7 7.1 copy-start.19
  2085.2 6.8 copy-start.14
  2092.0 3.5 copy-start.53
  2096.2 9.4 copy-start.39
  2096.2 13.0 copy-start.20
  2109.2 4.0 copy-start.50
  (11 other events, 12.7 us)
Sparse Core Ops, SparseCore 0:
  23.3 207.3 all-gather.15
  376.9 237.1 all-gather.17
  815.6 231.8 all-gather.19
  1279.8 199.1 all-gather.21
  1711.3 198.1 all-gather.23
where the time goes:
time: 2200 us; the launch traced here: 2190 us
  waiting for transfers between devices  759 us (34%)
  other arithmetic  608 us (28%)
  blocking collectives  402 us (18%)
  local copies, waits for them, and re-layouts  301 us (14%)
  matrix products  77.9 us (4%)
  loops' own time  23.1 us (1%)
    all_gather x5, waiting for transfers between devices, prefix(): pieces = jax.tree.map(lambda part: lax.all_gather(part, axis), value)  636 us
    select_n x155, other arithmetic, turn(): jnp.where(position < mine, new, old)  541 us
    unnamed x5, blocking collectives  338 us
    rev x10, local copies, waits for them, and re-layouts, prefix(): pieces = jax.tree.map(lambda part: part[::-1], pieces)  218 us
    ppermute x4, waiting for transfers between devices, from_behind(): return lax.ppermute(x, axis, pairs)  123 us
    psum x1, blocking collectives, shards(): decay_sum, skip_sum = lax.psum((decay_sum, skip_sum), 'branch')  64.8 us
  transfers between devices with their start and end apart: 9, of which 9 were waited for; matrix products, arithmetic and copies ran while one was open for 4% of the time, Pallas kernels for 0%

commit v1 on v0

v1 whole, which is shorter than its diff:
```python
import functools
import math

import jax
import jax.numpy as jnp
from jax import lax
from jax.experimental import pallas as pl
from jax.experimental.pallas import tpu as pltpu
from jax.sharding import PartitionSpec as P

F32 = jnp.float32
BF16 = jnp.bfloat16

SECTIONS = 4
FAMILIES = 2
ROWS = 128
STATE = 64
HEADDIM = 64
GROUP = 16
COLS = GROUP * HEADDIM
LANES = 128
CHUNK = 256
BRANCHES = 32
SEND_ROWS = 112
PACK_ROWS = FAMILIES * ROWS + 4 * GROUP
GRAD_ROWS = FAMILIES * (ROWS + GROUP)
VMEM_LIMIT = 48 * 1024 * 1024

NN = (((1,), (0,)), ((), ()))
NT = (((1,), (1,)), ((), ()))
TN = (((0,), (0,)), ((), ()))


def dot(a, b, dims):
    return lax.dot_general(a, b, dims, preferred_element_type=F32)


def split(a):
    high = a.astype(BF16)
    return high, (a - high.astype(F32)).astype(BF16)


def dot3(a, b, dims):
    return dot(a[0], b[0], dims) + dot(a[1], b[0], dims) + dot(a[0], b[1], dims)


def dot2(a, b, dims):
    return dot(a[0], b, dims) + dot(a[1], b, dims)


def lane_ids(shape):
    return lax.broadcasted_iota(jnp.int32, shape, len(shape) - 1)


def half(rolled, plain, side):
    lanes = lane_ids(plain.shape)
    if side == 0:
        return jnp.where(lanes < STATE, plain, 0.0)
    return jnp.where(lanes >= STATE, rolled, 0.0)


def expander():
    row = lax.broadcasted_iota(jnp.int32, (2 * GROUP, COLS), 0) & (GROUP - 1)
    col = lax.broadcasted_iota(jnp.int32, (2 * GROUP, COLS), 1) >> 6
    return jnp.where(row == col, 1.0, 0.0).astype(BF16)


def stack_split(a):
    high = a.astype(BF16).astype(F32)
    return jnp.concatenate([high, a - high], axis=0).astype(BF16)


class Layer:
    def __init__(self, pack_ref, layer, family):
        base = FAMILIES * ROWS
        both = pack_ref[layer, family * ROWS : (family + 1) * ROWS, :]
        turned = pltpu.roll(both, STATE, 1)
        self.b = (half(both, both, 0), half(turned, turned, 1))
        self.c = (half(turned, turned, 0), half(both, both, 1))
        self.step = pack_ref[layer, base + family * GROUP : base + (family + 1) * GROUP, :]
        self.decay = pack_ref[layer, base + 2 * GROUP : base + 3 * GROUP, :]
        gain = pack_ref[layer, base + 3 * GROUP : base + 4 * GROUP, :]
        row = lax.broadcasted_iota(jnp.int32, (ROWS, ROWS), 0)
        col = lax.broadcasted_iota(jnp.int32, (ROWS, ROWS), 1)
        self.row, self.col = row, col
        upper = jnp.where(row <= col, 1.0, 0.0).astype(BF16)
        drop = -self.decay * self.step
        first = drop.astype(BF16)
        rest = drop - first.astype(F32)
        second = rest.astype(BF16)
        third = (rest - second.astype(F32)).astype(BF16)
        logs = dot(first, upper, NN) + dot(second, upper, NN) + dot(third, upper, NN)
        carried = jnp.exp(logs)
        scale = self.step * jnp.exp(-logs)
        total = jnp.sum(jnp.where(lane_ids(carried.shape) == ROWS - 1, carried, 0.0), axis=1, keepdims=True)
        self.total = jnp.broadcast_to(total, (GROUP, LANES))
        self.carried2 = stack_split(carried)
        self.scale2 = stack_split(scale)
        self.gain2 = stack_split(gain)
        pulled = dot3(split(self.b[0]), split(self.c[0]), NT)
        self.pull = split(jnp.where(row <= col, pulled, 0.0))


def phase_a(family, upper_at, high, low, expand, send_ref):
    c_pair = split(jnp.concatenate([high.c[0], low.c[1]], axis=0))
    c_both = split(low.c[0] + low.c[1])
    b_both = high.b[0] + high.b[1]
    b_tile = jnp.concatenate([b_both] * (CHUNK // LANES), axis=1)
    lanes = lane_ids((STATE // 2, LANES))
    for chunk in range(COLS // CHUNK):
        cols = slice(chunk * CHUNK, (chunk + 1) * CHUNK)
        spread = expand[:, cols]
        carried = dot(high.carried2, spread, TN)
        scale = dot(high.scale2, spread, TN)
        gain = dot(high.gain2, spread, TN)
        low_carried = dot(low.carried2, spread, TN)
        upstream = upper_at(cols)
        hat = carried * upstream
        hat2 = split(hat)
        pulled = dot3(high.pull, hat2, NN)
        low_hat = low_carried * (gain * upstream + scale * pulled)
        low_hat2 = split(low_hat)
        both = tuple(jnp.concatenate([a, b], axis=0) for a, b in zip(hat2, low_hat2))
        begin = dot3(both, c_pair, TN).astype(BF16)
        response = split(low_carried * scale * b_tile)
        move = dot3(response, c_both, TN)
        for inner in range(CHUNK // HEADDIM):
            head = family * GROUP + chunk * (CHUNK // HEADDIM) + inner
            top = inner * HEADDIM
            send_ref[head, 0:HEADDIM, :] = begin[top : top + HEADDIM, :]
            first = move[top : top + 32, :]
            second = move[top + 32 : top + 64, :]
            send_ref[head, HEADDIM : HEADDIM + 32, :] = jnp.where(lanes < STATE, first, second).astype(BF16)
    totals = jnp.where(lane_ids((GROUP, LANES)) < STATE, high.total, low.total)
    total_high = totals.astype(BF16).astype(F32)
    total_low = totals - total_high
    place = lax.broadcasted_iota(jnp.int32, (16, LANES), 0)
    for inner in range(GROUP):
        one = jnp.broadcast_to(total_high[inner : inner + 1, :], (16, LANES))
        two = jnp.broadcast_to(total_low[inner : inner + 1, :], (16, LANES))
        block = jnp.where(place == 0, one, jnp.where(place == 1, two, 0.0))
        send_ref[family * GROUP + inner, 96:112, :] = block.astype(BF16)


def phase_b(family, side, upper_at, x_ref, s_ref, end_ref, layer, expand, put_grad):
    b, c = layer.b[side], layer.c[side]
    b2 = split(b)
    b_one, c_one = b2[0], c.astype(BF16)
    read = dot(c_one, b_one, NT)
    read = jnp.where(layer.row >= layer.col, read, 0.0).astype(BF16)
    pairs = jnp.zeros((ROWS, ROWS), F32)
    grad_out = jnp.zeros((ROWS, LANES), F32)
    grad_in = jnp.zeros((ROWS, LANES), F32)
    flow = jnp.zeros((GROUP, ROWS), F32)
    worth = jnp.zeros((GROUP, ROWS), F32)
    ending = jnp.zeros((GROUP, ROWS), F32)
    skips = jnp.zeros((GROUP, ROWS), F32)
    lanes = lane_ids((CHUNK, LANES))
    for chunk in range(COLS // CHUNK):
        cols = slice(chunk * CHUNK, (chunk + 1) * CHUNK)
        spread = expand[:, cols]
        one = spread[0:GROUP]
        carried = dot(layer.carried2, spread, TN)
        scale = dot(layer.scale2, spread, TN)
        gain = dot(layer.gain2, spread, TN)
        upstream = upper_at(cols)
        x = x_ref[family, :, cols].astype(F32)
        hat = carried * upstream
        hat2 = split(hat)
        hat_one = hat2[0]
        x_hat = scale * x
        x_one = x_hat.astype(BF16)
        per_chunk = CHUNK // HEADDIM
        first = family * GROUP + chunk * per_chunk
        ends = end_ref[first : first + per_chunk].reshape(CHUNK, LANES)
        top = (chunk % 2) * CHUNK
        packed = s_ref[family, top : top + CHUNK, :].astype(F32)
        if (chunk < 2) != (side == 0):
            packed = pltpu.roll(packed, STATE, 1)
        saved = jnp.where((lanes < STATE) == (side == 0), packed, 0.0)
        saved_one = saved.astype(BF16)
        end_in = dot2(b2, ends, NT)
        pulled = dot3(layer.pull, hat2, NN) + end_in
        put_grad(cols, (gain * upstream + scale * pulled).astype(BF16))
        forward = dot(read, x_one, NN) + dot(c_one, saved_one, NT)
        pairs = pairs + dot(hat_one, x_one, NT)
        grad_out = grad_out + dot(hat_one, saved_one, NN)
        grad_in = grad_in + dot(x_one, ends, NN)
        x_pulled = x_hat * pulled
        worth = worth + dot(one, x_pulled.astype(BF16), NT)
        flow = flow + dot(one, (hat * forward - x_pulled).astype(BF16), NT)
        ending = ending + dot(one, (x_hat * end_in).astype(BF16), NT)
        ending = ending + dot(one, (ends.astype(F32) * saved).astype(BF16), NN)
        skips = skips + dot(one, (x * upstream).astype(BF16), NT)
    pairs = jnp.where(layer.row >= layer.col, pairs, 0.0).astype(BF16)
    grad_out = grad_out + dot(pairs, b_one, NN)
    grad_in = grad_in + dot(pairs, c_one, TN)
    lanes = lane_ids((ROWS, LANES))
    if side == 0:
        grads = jnp.where(lanes < STATE, grad_in, pltpu.roll(grad_out, STATE, 1))
    else:
        grads = jnp.where(lanes < STATE, pltpu.roll(grad_in, STATE, 1), grad_out)
    later = jnp.where(layer.row >= layer.col, 1.0, 0.0).astype(BF16)
    rate = dot2(split(flow), later, NN) + jnp.sum(ending, axis=1, keepdims=True)
    grad_step = worth / layer.step - layer.decay * rate
    decay_part = jnp.sum(-layer.step * rate, axis=1, keepdims=True)
    skip_part = jnp.sum(skips, axis=1, keepdims=True)
    place = lane_ids((GROUP, LANES))
    small = jnp.where(place == 0, decay_part, jnp.where(place == 1, skip_part, 0.0))
    return grads, grad_step, small


def first_kernel(high_at, lengths_ref, cot_ref, pack_ref, send_ref, up_ref, cot_buf, sem):
    mine = lax.axis_index("section")
    branch = lax.axis_index("branch")
    at = pl.multiple_of(mine * COLS, COLS)
    copy = pltpu.make_async_copy(cot_ref.at[:, :, pl.ds(at, COLS)], cot_buf, sem)
    copy.start()
    expand = expander()
    copy.wait()
    for family in range(FAMILIES):
        slot = jnp.clip(branch - BRANCHES // 2, 0, BRANCHES // 2 - 1)
        limit = jnp.where(branch >= BRANCHES // 2, lengths_ref[family, slot], ROWS)

        def upper_at(cols):
            rows = lax.broadcasted_iota(jnp.int32, (ROWS, CHUNK), 0)
            value = jnp.where(rows < limit, cot_buf[family, :, cols].astype(F32), 0.0)
            up_ref[family, :, cols] = value.astype(BF16)
            return value

        high = Layer(pack_ref, high_at, family)
        low = Layer(pack_ref, high_at - 1, family)
        phase_a(family, upper_at, high, low, expand, send_ref)


def later_kernel(high_at, goes_on, *refs):
    pack_ref, up_ref, end_ref, own_x = refs[:4]
    x_refs, s_refs = refs[4:7], refs[7:11]
    outs = refs[11:]
    grad_refs, part_refs, small_ref = outs[0:4], outs[4:8], outs[8]
    rest = outs[9:]
    if goes_on:
        send_ref, next_ref = rest[0:2]
        rest = rest[2:]
    x_buf, s_buf, grad_buf, part_buf, x_sem, s_sem, grad_sem, part_sem = rest
    mine = lax.axis_index("section")
    at = pl.multiple_of(mine * COLS, COLS)
    sources = (own_x.at[0, :, :, pl.ds(at, COLS)],) + tuple(x_refs)
    for side in range(2):
        layer_at = high_at - side
        away = lax.rem(mine - layer_at + SECTIONS, SECTIONS)
        for k in range(SECTIONS):

            @pl.when(away == k)
            def _():
                pltpu.make_async_copy(sources[k], x_buf.at[side], x_sem.at[side]).start()
                pltpu.make_async_copy(s_refs[k], s_buf.at[side], s_sem.at[side]).start()

    expand = expander()
    for side in range(2):
        layer_at = high_at - side
        pltpu.make_async_copy(x_refs[0], x_buf.at[side], x_sem.at[side]).wait()
        pltpu.make_async_copy(s_refs[0], s_buf.at[side], s_sem.at[side]).wait()
        smalls = jnp.zeros((GROUP, LANES), F32)
        for family in range(FAMILIES):

            def upper_at(cols):
                if side == 0:
                    return up_ref[family, :, cols].astype(F32)
                return grad_buf[0, family, :, cols].astype(F32)

            def put_grad(cols, value):
                grad_buf[side, family, :, cols] = value

            layer = Layer(pack_ref, layer_at, family)
            grads, grad_step, small = phase_b(
                family, side, upper_at, x_buf.at[side], s_buf.at[side], end_ref, layer, expand, put_grad
            )
            part_buf[side, family * ROWS : (family + 1) * ROWS, :] = grads.astype(BF16)
            below = FAMILIES * ROWS + family * GROUP
            part_buf[side, below : below + GROUP, :] = grad_step.astype(BF16)
            smalls = smalls + small
        small_ref[side, :, :] = smalls
        ahead = lax.rem(layer_at - mine + SECTIONS, SECTIONS)
        for k in range(SECTIONS):

            @pl.when(ahead == k)
            def _():
                pltpu.make_async_copy(grad_buf.at[side], grad_refs[k], grad_sem.at[side]).start()
                pltpu.make_async_copy(part_buf.at[side], part_refs[k], part_sem.at[side]).start()

    if goes_on:
        next_ref[...] = grad_buf[1]
        for family in range(FAMILIES):

            def upper_at(cols):
                return grad_buf[1, family, :, cols].astype(F32)

            high = Layer(pack_ref, high_at - 2, family)
            low = Layer(pack_ref, high_at - 3, family)
            phase_a(family, upper_at, high, low, expand, send_ref)
    for side in range(2):
        pltpu.make_async_copy(grad_buf.at[side], grad_refs[0], grad_sem.at[side]).wait()
        pltpu.make_async_copy(part_buf.at[side], part_refs[0], part_sem.at[side]).wait()


def chain_kernel(got_ref, end_ref):
    lanes = lane_ids((STATE // 2, LANES))
    prompt = BRANCHES // 2
    fork = jnp.zeros((HEADDIM, LANES), F32)
    for at in range(prompt, BRANCHES):
        fork = fork + got_ref[at, 0:HEADDIM, :].astype(F32)
    plain, extra = fork, jnp.zeros((HEADDIM, LANES), F32)
    blank = jnp.zeros((STATE, LANES), F32)
    for at in range(prompt - 1, -1, -1):
        tail = got_ref[at, 96:112, :].astype(F32)
        total = tail[0:1, :] + tail[1:2, :]
        plain = total * plain
        extra = total * extra
        end_ref[at, :, :] = (plain + extra).astype(BF16)
        if at == 0:
            break
        packed = got_ref[at, HEADDIM : HEADDIM + 32, :].astype(F32)
        turned = pltpu.roll(packed, STATE, 1)
        move = jnp.concatenate(
            [jnp.where(lanes >= STATE, turned, 0.0), jnp.where(lanes >= STATE, packed, 0.0), blank], axis=0
        ).astype(BF16)
        extra = extra + dot2(split(plain), move, NN)
        plain = plain + got_ref[at, 0:HEADDIM, :].astype(F32)
    for at in range(prompt, BRANCHES):
        end_ref[at, :, :] = jnp.zeros((HEADDIM, LANES), BF16)


def pack_kernel(in_ref, out_ref, step_ref, decay_ref, gain_ref, pack_ref):
    base = FAMILIES * ROWS
    decay = jnp.transpose(jnp.broadcast_to(decay_ref[...], (LANES, SECTIONS * GROUP)))
    gain = jnp.transpose(jnp.broadcast_to(gain_ref[...], (LANES, SECTIONS * GROUP)))
    steps = [jnp.transpose(step_ref[0, family]) for family in range(FAMILIES)]
    both = [
        jnp.concatenate([in_ref[0, family], out_ref[0, family]], axis=1) for family in range(FAMILIES)
    ]
    for to in range(SECTIONS):
        heads = slice(to * GROUP, (to + 1) * GROUP)
        for family in range(FAMILIES):
            pack_ref[to, family * ROWS : (family + 1) * ROWS, :] = both[family]
            pack_ref[to, base + family * GROUP : base + (family + 1) * GROUP, :] = steps[family][heads]
        pack_ref[to, base + 2 * GROUP : base + 3 * GROUP, :] = decay[heads]
        pack_ref[to, base + 3 * GROUP : base + 4 * GROUP, :] = gain[heads]


def sort_kernel(at_ref, x1, x2, x3, s0, s1, s2, s3, o1, o2, o3, p0, p1, p2, p3):
    for x_ref, o_ref in ((x1, o1), (x2, o2), (x3, o3)):
        o_ref[0] = x_ref[0, 0]
    for s_ref, p_ref in ((s0, p0), (s1, p1), (s2, p2), (s3, p3)):
        whole = s_ref[0, 0, 0].reshape(COLS, STATE)
        p_ref[0] = jnp.concatenate([whole[: COLS // 2], whole[COLS // 2 :]], axis=1).astype(BF16)


def home_kernel(*refs):
    early_grads, late_grads = refs[0:4], refs[4:8]
    early_parts, late_parts = refs[8:12], refs[12:16]
    grad_ref, in_ref, out_ref, step_ref, part_buf, grad_sem, part_sem = refs[16:]
    mine = lax.axis_index("section")
    for is_early, grads, parts in ((True, early_grads, early_parts), (False, late_grads, late_parts)):

        @pl.when((mine >= 2) == is_early)
        def _():
            for k in range(SECTIONS):
                source = lax.rem(mine - k + SECTIONS, SECTIONS)
                at = pl.multiple_of(source * COLS, COLS)
                pltpu.make_async_copy(parts[k], part_buf.at[source], part_sem.at[k]).start()
                pltpu.make_async_copy(grads[k], grad_ref.at[0, :, :, pl.ds(at, COLS)], grad_sem.at[k]).start()

    for k in range(SECTIONS):
        pltpu.make_async_copy(early_parts[k], part_buf.at[k], part_sem.at[k]).wait()
    for family in range(FAMILIES):
        rows = slice(family * ROWS, (family + 1) * ROWS)
        total = part_buf[0, rows, :].astype(F32)
        for k in range(1, SECTIONS):
            total = total + part_buf[k, rows, :].astype(F32)
        in_ref[0, family] = total[:, 0:STATE]
        out_ref[0, family] = total[:, STATE:]
        below = FAMILIES * ROWS + family * GROUP
        steps = jnp.concatenate(
            [part_buf[k, below : below + GROUP, :].astype(F32) for k in range(SECTIONS)], axis=0
        )
        step_ref[0, family] = jnp.transpose(steps)
    for k in range(SECTIONS):
        pltpu.make_async_copy(early_grads[k], grad_ref.at[0, :, :, pl.ds(0, COLS)], grad_sem.at[k]).wait()


VM = pl.BlockSpec(memory_space=pltpu.VMEM)
SM = pl.BlockSpec(memory_space=pltpu.SMEM)
ANY = pl.BlockSpec(memory_space=pl.ANY)
PARAMS = pltpu.CompilerParams(vmem_limit_bytes=VMEM_LIMIT)


def shape(dims, dtype):
    return jax.ShapeDtypeStruct(dims, dtype)


def pack_small(state_in, state_out, step_size, decay_rate, skip_gain):
    return pl.pallas_call(
        pack_kernel,
        out_shape=shape((SECTIONS, PACK_ROWS, LANES), F32),
        in_specs=[VM] * 5,
        out_specs=VM,
        compiler_params=PARAMS,
        name="pack_small",
    )(state_in, state_out, step_size, decay_rate, skip_gain)


def sort_heads(layer_input, saved_states):
    mine = jnp.full((1,), lax.axis_index("section"), jnp.int32)

    def x_spec(k):
        return pl.BlockSpec(
            (1, 1, ROWS, COLS), lambda f, at: (0, f, 0, lax.rem(at[0] + k, SECTIONS))
        )

    def s_spec(k):
        return pl.BlockSpec(
            (1, 1, 1, GROUP, HEADDIM, STATE), lambda f, at: (0, f, 0, lax.rem(at[0] + k, SECTIONS), 0, 0)
        )

    x_out = pl.BlockSpec((1, ROWS, COLS), lambda f, at: (f, 0, 0))
    s_out = pl.BlockSpec((1, COLS // 2, LANES), lambda f, at: (f, 0, 0))
    outs = pl.pallas_call(
        sort_kernel,
        grid_spec=pltpu.PrefetchScalarGridSpec(
            num_scalar_prefetch=1,
            grid=(FAMILIES,),
            in_specs=[x_spec(1), x_spec(2), x_spec(3)] + [s_spec(k) for k in range(SECTIONS)],
            out_specs=[x_out] * 3 + [s_out] * 4,
        ),
        out_shape=[shape((FAMILIES, ROWS, COLS), BF16)] * 3 + [shape((FAMILIES, COLS // 2, LANES), BF16)] * 4,
        compiler_params=PARAMS,
        name="sort_heads",
    )(mine, layer_input, layer_input, layer_input, *([saved_states] * 4))
    return outs[:3], outs[3:]


def first_phase(high_at, lengths, cotangent, packs):
    return pl.pallas_call(
        functools.partial(first_kernel, high_at),
        out_shape=[
            shape((BRANCHES, SEND_ROWS, LANES), BF16),
            shape((FAMILIES, ROWS, COLS), BF16),
        ],
        in_specs=[SM, ANY, VM],
        out_specs=[VM, VM],
        scratch_shapes=[pltpu.VMEM((FAMILIES, ROWS, COLS), BF16), pltpu.SemaphoreType.DMA],
        compiler_params=PARAMS,
        name="first_phase",
    )(lengths, cotangent, packs)


def later_phase(high_at, goes_on, packs, upstream, ends, layer_input, xs, states):
    outs = [shape((FAMILIES, ROWS, COLS), BF16)] * 4
    outs += [shape((GRAD_ROWS, LANES), BF16)] * 4
    outs += [shape((2, GROUP, LANES), F32)]
    specs = [ANY] * 8 + [VM]
    if goes_on:
        outs += [shape((BRANCHES, SEND_ROWS, LANES), BF16), shape((FAMILIES, ROWS, COLS), BF16)]
        specs += [VM, VM]
    pair = pltpu.SemaphoreType.DMA((2,))
    return pl.pallas_call(
        functools.partial(later_kernel, high_at, goes_on),
        out_shape=outs,
        in_specs=[VM, VM, VM] + [ANY] * 8,
        out_specs=specs,
        scratch_shapes=[
            pltpu.VMEM((2, FAMILIES, ROWS, COLS), BF16),
            pltpu.VMEM((2, FAMILIES, COLS // 2, LANES), BF16),
            pltpu.VMEM((2, FAMILIES, ROWS, COLS), BF16),
            pltpu.VMEM((2, GRAD_ROWS, LANES), BF16),
            pair,
            pair,
            pair,
            pair,
        ],
        compiler_params=PARAMS,
        name="later_phase",
    )(packs, upstream, ends, layer_input, *xs, *states)


def chain(got):
    return pl.pallas_call(
        chain_kernel,
        out_shape=shape((BRANCHES, HEADDIM, LANES), BF16),
        in_specs=[VM],
        out_specs=VM,
        compiler_params=PARAMS,
        name="chain",
    )(got)


def home(early_grads, late_grads, early_parts, late_parts):
    return pl.pallas_call(
        home_kernel,
        out_shape=[
            shape((1, FAMILIES, ROWS, SECTIONS * COLS), BF16),
            shape((1, FAMILIES, ROWS, STATE), F32),
            shape((1, FAMILIES, ROWS, STATE), F32),
            shape((1, FAMILIES, ROWS, SECTIONS * GROUP), F32),
        ],
        in_specs=[ANY] * 16,
        out_specs=[ANY, VM, VM, VM],
        scratch_shapes=[
            pltpu.VMEM((SECTIONS, GRAD_ROWS, LANES), BF16),
            pltpu.SemaphoreType.DMA((SECTIONS,)),
            pltpu.SemaphoreType.DMA((SECTIONS,)),
        ],
        compiler_params=PARAMS,
        name="home",
    )(*early_grads, *late_grads, *early_parts, *late_parts)


def swap(value, axis):
    return lax.all_to_all(value, axis, 0, 0, tiled=True)


def send_on(value, k, targets):
    pairs = [(i, (i + k) % SECTIONS) for i in range(SECTIONS) if (i + k) % SECTIONS in targets]
    return lax.ppermute(value, "section", pairs)


def send_home(later, targets):
    grads = [later[0]] + [send_on(later[k], k, targets) for k in range(1, SECTIONS)]
    parts = [later[4]] + [send_on(later[4 + k], k, targets) for k in range(1, SECTIONS)]
    return grads, parts


def exchange(send):
    return swap(chain(swap(send, "branch")), "branch")


def shards(
    layer_input,
    cotangent,
    state_in,
    state_out,
    step_size,
    saved_states,
    decay_rate,
    skip_gain,
    lengths,
):
    grad_scale = 1.0 / math.sqrt(FAMILIES * ROWS * BRANCHES * HEADDIM)
    everyone = tuple(range(SECTIONS))
    packs = swap(pack_small(state_in, state_out, step_size, decay_rate, skip_gain), "section")
    packs, layer_input, saved_states = lax.optimization_barrier((packs, layer_input, saved_states))
    xs, states = sort_heads(layer_input, saved_states)
    xs = [send_on(xs[k - 1], k, everyone) for k in range(1, SECTIONS)]
    states = [states[0]] + [send_on(states[k], k, everyone) for k in range(1, SECTIONS)]
    send, upstream = first_phase(3, lengths, cotangent, packs)
    ends = exchange(send)
    early = later_phase(3, True, packs, upstream, ends, layer_input, xs, states)
    early_grads, early_parts = send_home(early, (2, 3))
    ends = exchange(early[9])
    late = later_phase(1, False, packs, early[10], ends, layer_input, xs, states)
    late_grads, late_parts = send_home(late, (0, 1))
    small = jnp.concatenate([early[8], late[8]], axis=0)[::-1, :, 0:2]
    small = jnp.transpose(small, (0, 2, 1)).reshape(1, 1, LANES)
    small = jnp.sum(swap(jnp.broadcast_to(small, (BRANCHES, 8, LANES)), "branch")[:, 0], axis=0)
    small = swap(small.reshape(SECTIONS, 2 * GROUP), "section").reshape(SECTIONS, 2, GROUP)
    small = small * grad_scale
    decay_sum = small[:, 0].reshape(1, SECTIONS * GROUP)
    skip_sum = small[:, 1].reshape(1, SECTIONS * GROUP)
    outs = home(early_grads, late_grads, early_parts, late_parts)
    return tuple(outs) + (decay_sum, skip_sum)


def solution(mesh):
    placed = (
        P("section", None, "branch", None),
        P(None, "branch", None),
        P("section", None, "branch", None),
        P("section", None, "branch", None),
        P("section", None, "branch", None),
        P("section", None, "branch", None, None, None),
        P("section", None),
        P("section", None),
        P(),
    )
    return jax.shard_map(
        shards,
        mesh=mesh,
        in_specs=placed,
        out_specs=(
            P("section", None, "branch", None),
            P("section", None, "branch", None),
            P("section", None, "branch", None),
            P("section", None, "branch", None),
            P("section", None),
            P("section", None),
        ),
        check_vma=False,
    )
```

time: 2200 us -> 259 us (0.12)
  the two profiles are of different devices: /device:TPU:0 before, /device:TPU:64 now
where the time goes in v1:
time: 259 us; the launch traced here: 258 us
  Pallas kernels  88.5 us (34%)
  starting transfers between devices  63.3 us (24%)
  waiting for transfers between devices  52.9 us (20%)
  blocking collectives  28 us (11%)
  local copies, waits for them, and re-layouts  24.3 us (9%)
    pallas_call x1, Pallas kernels, home(): pl.pallas_call(home_kernel, out_shape=[shape((1, FAMILIES, ROWS, SECTIONS...  49 us
    ppermute x18, starting transfers between devices, send_on(): return lax.ppermute(value, 'section', pairs)  35.9 us
    ppermute x18, waiting for transfers between devices, send_on(): return lax.ppermute(value, 'section', pairs)  32.8 us
    all_to_all x2, blocking collectives, swap(): return lax.all_to_all(value, axis, 0, 0, tiled=True)  28 us
    all_to_all x5, starting transfers between devices, swap(): return lax.all_to_all(value, axis, 0, 0, tiled=True)  27.4 us
    pallas_call x2, Pallas kernels, later_phase(): pl.pallas_call(functools.partial(later_kernel, high_at, goes_on), out_sha...  27.1 us
    unnamed x64, local copies, waits for them, and re-layouts  22.2 us
    all_to_all x5, waiting for transfers between devices, swap(): return lax.all_to_all(value, axis, 0, 0, tiled=True)  20.1 us
  transfers between devices with their start and end apart: 23, of which 7 were waited for; matrix products, arithmetic and copies ran while one was open for 1% of the time, Pallas kernels for 7%

profile of v1, /device:TPU:64, one launch (start us, length us, event | category | flops | bytes accessed | tf_op | source)
XLA Modules:
  0.0 258.1 jit_solution(16867561218258750262)
XLA Ops:
  0.6 0.9 copy.38.in_ref
  1.6 0.9 copy.39.out_ref
  2.5 0.9 copy.40.step_ref
  3.5 0.6 copy-done.17
  4.1 0.7 copy-done.18
  5.0 13.1 %all_to_all.39.pack_ref.refs_0_ = f32[4,320,128]{2,1,0:T(8,128)S(1)} all-to-all(f32[4,320,128]{2,1,0:T(8,128)S(1)} %pack_small.1), channel_id=1, replica_groups=mesh['section'=4,'branch'=32] {'section'}, dimensions={0} | all-to-all | bytes 1310720 | tf_op jit(solution)/shard_map/all_to_all | solution.py:520
  18.1 5.3 %first_phase.1 = (bf16[32,112,128]{2,1,0:T(8,128)(2,1)S(1)}, bf16[2,128,1024]{2,1,0:T(8,128)(2,1)S(1)}) custom-call(s32[2,16]{1,0:T(2,128)S(1)} %copy-done.16, bf16[2,128,4096]{2,1,0:T(8,128)(2,1)S(1)} %copy-done.4, f32[4,320,128]{2,1,0:T(8,128)S(1)} %all_to_all.39.pack_ref.refs_0_), custom_call_target="tpu_custom_call" | custom-call | tf_op jit(solution)/shard_map/first_phase/pallas_call | solution.py:444
  23.4 0.9 copy-done.5
  24.3 0.8 copy-done.10
  25.1 7.4 %all-to-all-start.1 = ((bf16[32,112,128]{2,1,0:T(8,128)(2,1)}), bf16[32,112,128]{2,1,0:T(8,128)(2,1)}, u32[]{:S(2)}, u32[]{:S(2)}) async-start(bf16[32,112,128]{2,1,0:T(8,128)(2,1)} %copy-done.5), calls=%async_computation.1 | async-start | bytes 1835008 | tf_op jit(solution)/shard_map/all_to_all | solution.py:520
  32.6 3.4 %sort_heads.1 = (bf16[2,128,1024]{2,1,0:T(8,128)(2,1)}, bf16[2,128,1024]{2,1,0:T(8,128)(2,1)}, bf16[2,128,1024]{2,1,0:T(8,128)(2,1)}, bf16[2,512,128]{2,1,0:T(8,...) custom-call(s32[1]{0:T(128)} %bitcast.at_ref, ...), custom_call_target="tpu_custom_call" | custom-call | tf_op jit(solution)/shard_map/sort_heads/pallas_call | solution.py:428
  36.0 0.7 copy-done.22
  36.7 1.8 collective-permute-start.3
  38.5 2.1 collective-permute-start
  40.6 2.0 collective-permute-start.2
  42.6 5.9 %all-to-all-done.1.got_ref = bf16[32,112,128]{2,1,0:T(8,128)(2,1)} async-done(((bf16[32,112,128]{2,1,0:T(8,128)(2,1)}), bf16[32,112,128]{2,1,0:T(8,128)(2,1)}, u32[]{:S(2)}, u32[]{:S(2)}) %all-to-all-start.1) | async-done | bytes 917536 | tf_op jit(solution)/shard_map/all_to_all | solution.py:520
  48.5 2.3 chain.2
  50.8 3.9 %all-to-all-start.2 = ((bf16[32,64,128]{2,1,0:T(8,128)(2,1)}), bf16[32,64,128]{2,1,0:T(8,128)(2,1)S(1)}, u32[]{:S(2)}, u32[]{:S(2)}) async-start(bf16[32,64,128]{2,1,0:T(8,128)(2,1)} %chain.2), calls=%async_computation.2 | async-start | bytes 1048576 | tf_op jit(solution)/shard_map/all_to_all | solution.py:520
  54.7 2.8 %collective-permute-start.4 = (bf16[2,512,128]{2,1,0:T(8,128)(2,1)}, bf16[2,512,128]{2,1,0:T(8,128)(2,1)S(1)}, u32[]{:S(2)}, u32[]{:S(2)}) collective-permute-start(bf16[2,512,128]{2,1,0:T(8,128)(2,1)} %copy-done.22), channel_id=1, source_target_pairs={{0,64},{32,96},{64,0},{96,32},{1,65},{33,97},{65,1},{97,33},{2,66}... | collective-permute-start | bytes 786440 | tf_op jit(solution)/shard_map/ppermute | solution.py:525
  58.1 16.6 %collective-permute-done.4.refs_9_ = bf16[2,512,128]{2,1,0:T(8,128)(2,1)S(1)} collective-permute-done((bf16[2,512,128]{2,1,0:T(8,128)(2,1)}, bf16[2,512,128]{2,1,0:T(8,128)(2,1)S(1)}, u32[]{:S(2)}, u32[]{:S(2)}) %collective-permute-start.4) | collective-permute-done | bytes 262176 | tf_op jit(solution)/shard_map/ppermute | solution.py:525
  74.7 2.2 collective-permute-done.5.refs_10_
  76.9 0.8 copy-done.2
  77.7 1.0 copy-done.11
  78.7 16.5 %later_phase.2 = (bf16[2,128,1024]{2,1,0:T(8,128)(2,1)S(1)}, bf16[2,128,1024]{2,1,0:T(8,128)(2,1)S(1)}, bf16[2,128,1024]{2,1,0:T(8,128)(2,1)S(1)}, bf16[2,128,10...) custom-call(f32[4,320,128]{2,1,0:T(8,128)} %copy-done.1, ...), custom_call_target="tpu_custom_call" | custom-call | tf_op jit(solution)/shard_map/later_phase/pallas_call | solution.py:467
  95.2 0.8 copy-done.6
  96.0 0.8 copy-done.12
  97.4 0.8 copy-done.19
  98.2 0.8 copy-done.20
  99.0 0.8 copy-done.21
  99.8 0.6 copy-done.26
  100.4 0.6 copy-done.27
  101.1 0.6 copy-done.28
  101.7 7.4 %all-to-all-start.3 = ((bf16[32,112,128]{2,1,0:T(8,128)(2,1)}), bf16[32,112,128]{2,1,0:T(8,128)(2,1)S(1)}, u32[]{:S(2)}, u32[]{:S(2)}) async-start(bf16[32,112,128]{2,1,0:T(8,128)(2,1)} %get-tuple-element.59), calls=%async_computation.3 | async-start | bytes 1835008 | tf_op jit(solution)/shard_map/all_to_all | solution.py:520
  109.1 3.9 %collective-permute-start.6 = (bf16[2,128,1024]{2,1,0:T(8,128)(2,1)}, bf16[2,128,1024]{2,1,0:T(8,128)(2,1)}, u32[]{:S(2)}, u32[]{:S(2)}) collective-permute-start(bf16[2,128,1024]{2,1,0:T(8,128)(2,1)} %copy-done.21), channel_id=1, source_target_pairs={{32,64},{64,96},{33,65},{65,97},{34,66},{66,98},{35,67},{67,99},{3... | collective-permute-start | bytes 1572872 | tf_op jit(solution)/shard_map/ppermute | solution.py:525
  113.0 12.0 %all-to-all-done.3.got_ref = bf16[32,112,128]{2,1,0:T(8,128)(2,1)S(1)} async-done(((bf16[32,112,128]{2,1,0:T(8,128)(2,1)}), bf16[32,112,128]{2,1,0:T(8,128)(2,1)S(1)}, u32[]{:S(2)}, u32[]{:S(2)}) %all-to-all-start.3) | async-done | bytes 917536 | tf_op jit(solution)/shard_map/all_to_all | solution.py:520
  125.0 1.2 chain.3
  126.2 3.9 %all-to-all-start.4 = ((bf16[32,64,128]{2,1,0:T(8,128)(2,1)}), bf16[32,64,128]{2,1,0:T(8,128)(2,1)S(1)}, u32[]{:S(2)}, u32[]{:S(2)}) async-start(bf16[32,64,128]{2,1,0:T(8,128)(2,1)} %chain.3), calls=%async_computation.4 | async-start | bytes 1048576 | tf_op jit(solution)/shard_map/all_to_all | solution.py:520
  130.1 1.3 collective-permute-start.7
  131.4 3.9 %collective-permute-start.12 = (bf16[288,128]{1,0:T(8,128)(2,1)}, bf16[288,128]{1,0:T(8,128)(2,1)S(1)}, u32[]{:S(2)}, u32[]{:S(2)}) collective-permute-start(bf16[288,128]{1,0:T(8,128)(2,1)} %copy-done.28), channel_id=1, source_target_pairs={{32,64},{64,96},{33,65},{65,97},{34,66},{66,98},{35,67},{67,99},{3... | collective-permute-start | bytes 221192 | tf_op jit(solution)/shard_map/ppermute | solution.py:525
  135.3 1.3 collective-permute-start.13
  136.6 1.3 collective-permute-start.14
  137.9 13.0 %collective-permute-done.12.refs_9_ = bf16[288,128]{1,0:T(8,128)(2,1)S(1)} collective-permute-done((bf16[288,128]{1,0:T(8,128)(2,1)}, bf16[288,128]{1,0:T(8,128)(2,1)S(1)}, u32[]{:S(2)}, u32[]{:S(2)}) %collective-permute-start.12) | collective-permute-done | bytes 73760 | tf_op jit(solution)/shard_map/ppermute | solution.py:525
  150.8 1.3 collective-permute-start.8
  152.1 1.0 copy-done.13
  153.2 10.6 %later_phase.3 = (bf16[2,128,1024]{2,1,0:T(8,128)(2,1)S(1)}, bf16[2,128,1024]{2,1,0:T(8,128)(2,1)}, bf16[2,128,1024]{2,1,0:T(8,128)(2,1)}, bf16[2,128,1024]{2,1,...) custom-call(f32[4,320,128]{2,1,0:T(8,128)} %copy-done.1, ...), custom_call_target="tpu_custom_call" | custom-call | tf_op jit(solution)/shard_map/later_phase/pallas_call | solution.py:467
  163.8 0.8 copy-done.8
  164.6 0.6 copy-done.24
  165.8 0.7 collective-permute-start.9
  166.5 5.1 %collective-permute-start.10 = (bf16[2,128,1024]{2,1,0:T(8,128)(2,1)}, bf16[2,128,1024]{2,1,0:T(8,128)(2,1)S(1)}, u32[]{:S(2)}, u32[]{:S(2)}) collective-permute-start(bf16[2,128,1024]{2,1,0:T(8,128)(2,1)} %get-tuple-element.62), channel_id=1, source_target_pairs={{64,0},{96,32},{65,1},{97,33},{66,2},{98,34},{67,3},{99,35},{68,4}... | collective-permute-start | bytes 1572872 | tf_op jit(solution)/shard_map/ppermute | solution.py:525
  171.7 1.3 collective-permute-start.11
  173.2 15.0 %all_to_all.40 = f32[32,8,128]{2,1,0:T(8,128)S(1)} all-to-all(f32[32,8,128]{2,1,0:T(8,128)S(1)} %broadcast_in_dim.12), channel_id=1, replica_groups=mesh['section'=4,'branch'=32] {'branch'}, dimensions={0} | all-to-all | bytes 262144 | tf_op jit(solution)/shard_map/all_to_all | solution.py:520
  188.2 0.7 all_to_all.30
  188.9 4.8 %all-to-all-start.6 = ((f32[4,1,32]{2,1,0:T(1,128)}), f32[4,1,32]{2,1,0:T(1,128)S(1)}, u32[]{:S(2)}, u32[]{:S(2)}) async-start(f32[4,1,32]{2,1,0:T(1,128)} %bitcast.3), calls=%async_computation.6 | async-start | bytes 4096 | tf_op jit(solution)/shard_map/all_to_all | solution.py:520
  193.7 0.7 collective-permute-start.15
  194.3 2.2 all-to-all-done.6
  196.6 4.3 %collective-permute-start.16 = (bf16[288,128]{1,0:T(8,128)(2,1)}, bf16[288,128]{1,0:T(8,128)(2,1)S(1)}, u32[]{:S(2)}, u32[]{:S(2)}) collective-permute-start(bf16[288,128]{1,0:T(8,128)(2,1)} %copy-done.24), channel_id=1, source_target_pairs={{64,0},{96,32},{65,1},{97,33},{66,2},{98,34},{67,3},{99,35},{68,4}... | collective-permute-start | bytes 221192 | tf_op jit(solution)/shard_map/ppermute | solution.py:525
  200.9 1.7 collective-permute-start.17
  203.8 1.1 collective-permute-done.17.refs_15_
  204.9 1.0 copy-done.7
  205.9 1.0 copy-done.9
  207.0 49.0 %home.1 = (bf16[1,2,128,4096]{3,2,1,0:T(8,128)(2,1)}, f32[1,2,128,64]{3,2,1,0:T(8,128)S(1)}, f32[1,2,128,64]{3,2,1,0:T(8,128)S(1)}, f32[1,2,128,64]{3,2,1,0:T(8,128)S(1)}) custom-call(bf16[2,128,1024]{2,1,0:T(8,128)(2,1)S(1)} %copy-done.7, bf16[2,128,1024]{2,1,0:T(8,128)(2,1)} %collective-permute-done.6.refs_1_, ...), custom_call_target="tpu_custom_call" | custom-call | tf_op jit(solution)/shard_map/home/pallas_call | solution.py:499
  256.0 0.7 copy.44
  256.7 0.7 copy.45
  257.4 0.7 copy.46
  (69 shorter events, 3.6 us)
Async XLA Ops:
  0.6 17.4 %copy-start.16 = (s32[2,16]{1,0:T(2,128)S(1)}, s32[2,16]{1,0:T(2,128)}, u32[]{:S(2)}) copy-start(s32[2,16]{1,0:T(2,128)} %lengths_ref.1) | copy-start | bytes 388
  3.5 0.7 copy-start.17
  4.1 0.7 copy-start.18
  4.8 13.3 %copy-start.4 = (bf16[2,128,4096]{2,1,0:T(8,128)(2,1)S(1)}, bf16[2,128,4096]{2,1,0:T(8,128)(2,1)}, u32[]{:S(2)}) copy-start(bf16[2,128,4096]{2,1,0:T(8,128)(2,1)} %cot_ref.1) | copy-start | bytes 6291460
  18.1 7.1 %copy-start.1 = (f32[4,320,128]{2,1,0:T(8,128)}, f32[4,320,128]{2,1,0:T(8,128)S(1)}, u32[]{:S(2)}) copy-start(f32[4,320,128]{2,1,0:T(8,128)S(1)} %all_to_all.39.pack_ref.refs_0_) | copy-start | bytes 1966084
  18.1 14.5 %copy-start = (bf16[1,2,128,4096]{3,2,1,0:T(8,128)(2,1)S(1)}, bf16[1,2,128,4096]{3,2,1,0:T(8,128)(2,1)}, u32[]{:S(2)}) copy-start(bf16[1,2,128,4096]{3,2,1,0:T(8,128)(2,1)} %refs_3_.1) | copy-start | bytes 6291460
  23.4 0.9 copy-start.5
  24.3 0.8 copy-start.10
  25.1 23.4 %all-to-all-start.1 = ((bf16[32,112,128]{2,1,0:T(8,128)(2,1)}), bf16[32,112,128]{2,1,0:T(8,128)(2,1)}, u32[]{:S(2)}, u32[]{:S(2)}) async-start(bf16[32,112,128]{2,1,0:T(8,128)(2,1)} %copy-done.5), calls=%async_computation.1 | async-start | bytes 1835008 | tf_op jit(solution)/shard_map/all_to_all | solution.py:520
  36.0 0.7 copy-start.22
  36.7 20.8 %collective-permute-start.3 = (bf16[2,512,128]{2,1,0:T(8,128)(2,1)}, bf16[2,512,128]{2,1,0:T(8,128)(2,1)S(1)}, u32[]{:S(2)}, u32[]{:S(2)}) collective-permute-start(bf16[2,512,128]{2,1,0:T(8,128)(2,1)} %get-tuple-element.51), channel_id=1, source_target_pairs={{0,32},{32,64},{64,96},{96,0},{1,33},{33,65},{65,97},{97,1},{2,34}... | collective-permute-start | bytes 786440 | tf_op jit(solution)/shard_map/ppermute | solution.py:525
  38.5 38.3 %collective-permute-start = (bf16[2,128,1024]{2,1,0:T(8,128)(2,1)}, bf16[2,128,1024]{2,1,0:T(8,128)(2,1)S(1)}, u32[]{:S(2)}, u32[]{:S(2)}) collective-permute-start(bf16[2,128,1024]{2,1,0:T(8,128)(2,1)} %get-tuple-element.47), channel_id=1, source_target_pairs={{0,32},{32,64},{64,96},{96,0},{1,33},{33,65},{65,97},{97,1},{2,34}... | collective-permute-start | bytes 1572872 | tf_op jit(solution)/shard_map/ppermute | solution.py:525
  40.6 36.3 %collective-permute-start.1 = (bf16[2,128,1024]{2,1,0:T(8,128)(2,1)}, bf16[2,128,1024]{2,1,0:T(8,128)(2,1)S(1)}, u32[]{:S(2)}, u32[]{:S(2)}) collective-permute-start(bf16[2,128,1024]{2,1,0:T(8,128)(2,1)} %get-tuple-element.48), channel_id=1, source_target_pairs={{0,64},{32,96},{64,0},{96,32},{1,65},{33,97},{65,1},{97,33},{2,66}... | collective-permute-start | bytes 1572872 | tf_op jit(solution)/shard_map/ppermute | solution.py:525
  40.6 36.3 %collective-permute-start.2 = (bf16[2,128,1024]{2,1,0:T(8,128)(2,1)}, bf16[2,128,1024]{2,1,0:T(8,128)(2,1)S(1)}, u32[]{:S(2)}, u32[]{:S(2)}) collective-permute-start(bf16[2,128,1024]{2,1,0:T(8,128)(2,1)} %get-tuple-element.49), channel_id=1, source_target_pairs={{0,96},{32,0},{64,32},{96,64},{1,97},{33,1},{65,33},{97,65},{2,98}... | collective-permute-start | bytes 1572872 | tf_op jit(solution)/shard_map/ppermute | solution.py:525
  50.8 26.0 %all-to-all-start.2 = ((bf16[32,64,128]{2,1,0:T(8,128)(2,1)}), bf16[32,64,128]{2,1,0:T(8,128)(2,1)S(1)}, u32[]{:S(2)}, u32[]{:S(2)}) async-start(bf16[32,64,128]{2,1,0:T(8,128)(2,1)} %chain.2), calls=%async_computation.2 | async-start | bytes 1048576 | tf_op jit(solution)/shard_map/all_to_all | solution.py:520
  54.7 19.9 %collective-permute-start.4 = (bf16[2,512,128]{2,1,0:T(8,128)(2,1)}, bf16[2,512,128]{2,1,0:T(8,128)(2,1)S(1)}, u32[]{:S(2)}, u32[]{:S(2)}) collective-permute-start(bf16[2,512,128]{2,1,0:T(8,128)(2,1)} %copy-done.22), channel_id=1, source_target_pairs={{0,64},{32,96},{64,0},{96,32},{1,65},{33,97},{65,1},{97,33},{2,66}... | collective-permute-start | bytes 786440 | tf_op jit(solution)/shard_map/ppermute | solution.py:525
  57.5 19.3 %collective-permute-start.5 = (bf16[2,512,128]{2,1,0:T(8,128)(2,1)S(1)}, bf16[2,512,128]{2,1,0:T(8,128)(2,1)S(1)}, u32[]{:S(2)}, u32[]{:S(2)}) collective-permute-start(bf16[2,512,128]{2,1,0:T(8,128)(2,1)S(1)} %get-tuple-element.53), channel_id=1, source_target_pairs={{0,96},{32,0},{64,32},{96,64},{1,97},{33,1},{65,33},{97,65},{2,98}... | collective-permute-start | bytes 786440 | tf_op jit(solution)/shard_map/ppermute | solution.py:525
  76.9 0.8 copy-start.2
  77.7 1.0 copy-start.11
  95.2 0.8 copy-start.6
  96.0 0.8 copy-start.12
  96.8 0.6 copy-start.14
  97.4 0.8 copy-start.19
  98.2 0.8 copy-start.20
  99.0 0.8 copy-start.21
  99.8 0.6 copy-start.26
  100.4 0.6 copy-start.27
  101.1 0.6 copy-start.28
  101.7 50.4 %copy-start.3 = (bf16[2,128,1024]{2,1,0:T(8,128)(2,1)S(1)}, bf16[2,128,1024]{2,1,0:T(8,128)(2,1)}, u32[]{:S(2)}) copy-start(bf16[2,128,1024]{2,1,0:T(8,128)(2,1)} %copy-done.2) | copy-start | bytes 1572868
  101.7 23.3 %all-to-all-start.3 = ((bf16[32,112,128]{2,1,0:T(8,128)(2,1)}), bf16[32,112,128]{2,1,0:T(8,128)(2,1)S(1)}, u32[]{:S(2)}, u32[]{:S(2)}) async-start(bf16[32,112,128]{2,1,0:T(8,128)(2,1)} %get-tuple-element.59), calls=%async_computation.3 | async-start | bytes 1835008 | tf_op jit(solution)/shard_map/all_to_all | solution.py:520
  109.1 62.6 %collective-permute-start.6 = (bf16[2,128,1024]{2,1,0:T(8,128)(2,1)}, bf16[2,128,1024]{2,1,0:T(8,128)(2,1)}, u32[]{:S(2)}, u32[]{:S(2)}) collective-permute-start(bf16[2,128,1024]{2,1,0:T(8,128)(2,1)} %copy-done.21), channel_id=1, source_target_pairs={{32,64},{64,96},{33,65},{65,97},{34,66},{66,98},{35,67},{67,99},{3... | collective-permute-start | bytes 1572872 | tf_op jit(solution)/shard_map/ppermute | solution.py:525
  126.2 26.0 %all-to-all-start.4 = ((bf16[32,64,128]{2,1,0:T(8,128)(2,1)}), bf16[32,64,128]{2,1,0:T(8,128)(2,1)S(1)}, u32[]{:S(2)}, u32[]{:S(2)}) async-start(bf16[32,64,128]{2,1,0:T(8,128)(2,1)} %chain.3), calls=%async_computation.4 | async-start | bytes 1048576 | tf_op jit(solution)/shard_map/all_to_all | solution.py:520
  130.1 63.6 %collective-permute-start.7 = (bf16[2,128,1024]{2,1,0:T(8,128)(2,1)}, bf16[2,128,1024]{2,1,0:T(8,128)(2,1)}, u32[]{:S(2)}, u32[]{:S(2)}) collective-permute-start(bf16[2,128,1024]{2,1,0:T(8,128)(2,1)} %copy-done.20), channel_id=1, source_target_pairs={{0,64},{32,96},{1,65},{33,97},{2,66},{34,98},{3,67},{35,99},{4,68}... | collective-permute-start | bytes 1572872 | tf_op jit(solution)/shard_map/ppermute | solution.py:525
  131.4 19.5 %collective-permute-start.12 = (bf16[288,128]{1,0:T(8,128)(2,1)}, bf16[288,128]{1,0:T(8,128)(2,1)S(1)}, u32[]{:S(2)}, u32[]{:S(2)}) collective-permute-start(bf16[288,128]{1,0:T(8,128)(2,1)} %copy-done.28), channel_id=1, source_target_pairs={{32,64},{64,96},{33,65},{65,97},{34,66},{66,98},{35,67},{67,99},{3... | collective-permute-start | bytes 221192 | tf_op jit(solution)/shard_map/ppermute | solution.py:525
  135.3 30.6 %collective-permute-start.13 = (bf16[288,128]{1,0:T(8,128)(2,1)}, bf16[288,128]{1,0:T(8,128)(2,1)S(1)}, u32[]{:S(2)}, u32[]{:S(2)}) collective-permute-start(bf16[288,128]{1,0:T(8,128)(2,1)} %copy-done.27), channel_id=1, source_target_pairs={{0,64},{32,96},{1,65},{33,97},{2,66},{34,98},{3,67},{35,99},{4,68}... | collective-permute-start | bytes 221192 | tf_op jit(solution)/shard_map/ppermute | solution.py:525
  136.6 30.0 %collective-permute-start.14 = (bf16[288,128]{1,0:T(8,128)(2,1)}, bf16[288,128]{1,0:T(8,128)(2,1)S(1)}, u32[]{:S(2)}, u32[]{:S(2)}) collective-permute-start(bf16[288,128]{1,0:T(8,128)(2,1)} %copy-done.26), channel_id=1, source_target_pairs={{0,96},{96,64},{1,97},{97,65},{2,98},{98,66},{3,99},{99,67},{4,100... | collective-permute-start | bytes 221192 | tf_op jit(solution)/shard_map/ppermute | solution.py:525
  150.8 45.8 %collective-permute-start.8 = (bf16[2,128,1024]{2,1,0:T(8,128)(2,1)}, bf16[2,128,1024]{2,1,0:T(8,128)(2,1)}, u32[]{:S(2)}, u32[]{:S(2)}) collective-permute-start(bf16[2,128,1024]{2,1,0:T(8,128)(2,1)} %copy-done.19), channel_id=1, source_target_pairs={{0,96},{96,64},{1,97},{97,65},{2,98},{98,66},{3,99},{99,67},{4,100... | collective-permute-start | bytes 1572872 | tf_op jit(solution)/shard_map/ppermute | solution.py:525
  152.1 1.0 copy-start.13
  153.2 51.7 %copy-start.15 = (bf16[288,128]{1,0:T(8,128)(2,1)S(1)}, bf16[288,128]{1,0:T(8,128)(2,1)}, u32[]{:S(2)}) copy-start(bf16[288,128]{1,0:T(8,128)(2,1)} %copy-done.14) | copy-start | bytes 221188
  163.8 0.8 copy-start.8
  164.6 0.6 copy-start.24
  165.2 0.6 copy-start.25
  165.8 7.2 %copy-start.23 = (bf16[288,128]{1,0:T(8,128)(2,1)}, bf16[288,128]{1,0:T(8,128)(2,1)S(1)}, u32[]{:S(2)}) copy-start(bf16[288,128]{1,0:T(8,128)(2,1)S(1)} %get-tuple-element.71) | copy-start | bytes 221188
  165.8 39.0 %collective-permute-start.9 = (bf16[2,128,1024]{2,1,0:T(8,128)(2,1)}, bf16[2,128,1024]{2,1,0:T(8,128)(2,1)S(1)}, u32[]{:S(2)}, u32[]{:S(2)}) collective-permute-start(bf16[2,128,1024]{2,1,0:T(8,128)(2,1)} %get-tuple-element.61), channel_id=1, source_target_pairs={{0,32},{96,0},{1,33},{97,1},{2,34},{98,2},{3,35},{99,3},{4,36},{10... | collective-permute-start | bytes 1572872 | tf_op jit(solution)/shard_map/ppermute | solution.py:525
  166.5 38.4 %collective-permute-start.10 = (bf16[2,128,1024]{2,1,0:T(8,128)(2,1)}, bf16[2,128,1024]{2,1,0:T(8,128)(2,1)S(1)}, u32[]{:S(2)}, u32[]{:S(2)}) collective-permute-start(bf16[2,128,1024]{2,1,0:T(8,128)(2,1)} %get-tuple-element.62), channel_id=1, source_target_pairs={{64,0},{96,32},{65,1},{97,33},{66,2},{98,34},{67,3},{99,35},{68,4}... | collective-permute-start | bytes 1572872 | tf_op jit(solution)/shard_map/ppermute | solution.py:525
  171.7 33.2 %collective-permute-start.11 = (bf16[2,128,1024]{2,1,0:T(8,128)(2,1)}, bf16[2,128,1024]{2,1,0:T(8,128)(2,1)S(1)}, u32[]{:S(2)}, u32[]{:S(2)}) collective-permute-start(bf16[2,128,1024]{2,1,0:T(8,128)(2,1)} %get-tuple-element.63), channel_id=1, source_target_pairs={{32,0},{64,32},{33,1},{65,33},{34,2},{66,34},{35,3},{67,35},{36,4}... | collective-permute-start | bytes 1572872 | tf_op jit(solution)/shard_map/ppermute | solution.py:525
  188.9 7.6 %all-to-all-start.6 = ((f32[4,1,32]{2,1,0:T(1,128)}), f32[4,1,32]{2,1,0:T(1,128)S(1)}, u32[]{:S(2)}, u32[]{:S(2)}) async-start(f32[4,1,32]{2,1,0:T(1,128)} %bitcast.3), calls=%async_computation.6 | async-start | bytes 4096 | tf_op jit(solution)/shard_map/all_to_all | solution.py:520
  193.7 7.2 %collective-permute-start.15 = (bf16[288,128]{1,0:T(8,128)(2,1)}, bf16[288,128]{1,0:T(8,128)(2,1)S(1)}, u32[]{:S(2)}, u32[]{:S(2)}) collective-permute-start(bf16[288,128]{1,0:T(8,128)(2,1)} %copy-done.25), channel_id=1, source_target_pairs={{0,32},{96,0},{1,33},{97,1},{2,34},{98,2},{3,35},{99,3},{4,36},{10... | collective-permute-start | bytes 221192 | tf_op jit(solution)/shard_map/ppermute | solution.py:525
  196.6 7.2 %collective-permute-start.16 = (bf16[288,128]{1,0:T(8,128)(2,1)}, bf16[288,128]{1,0:T(8,128)(2,1)S(1)}, u32[]{:S(2)}, u32[]{:S(2)}) collective-permute-start(bf16[288,128]{1,0:T(8,128)(2,1)} %copy-done.24), channel_id=1, source_target_pairs={{64,0},{96,32},{65,1},{97,33},{66,2},{98,34},{67,3},{99,35},{68,4}... | collective-permute-start | bytes 221192 | tf_op jit(solution)/shard_map/ppermute | solution.py:525
  200.9 4.0 %collective-permute-start.17 = (bf16[288,128]{1,0:T(8,128)(2,1)}, bf16[288,128]{1,0:T(8,128)(2,1)S(1)}, u32[]{:S(2)}, u32[]{:S(2)}) collective-permute-start(bf16[288,128]{1,0:T(8,128)(2,1)} %copy-done.23), channel_id=1, source_target_pairs={{32,0},{64,32},{33,1},{65,33},{34,2},{66,34},{35,3},{67,35},{36,4}... | collective-permute-start | bytes 221192 | tf_op jit(solution)/shard_map/ppermute | solution.py:525
  204.9 1.0 copy-start.7
  205.9 1.0 copy-start.9

commit v2 on v1

v2 whole, which is shorter than its diff:
```python
import functools
import math

import jax
import jax.numpy as jnp
from jax import lax
from jax.experimental import pallas as pl
from jax.experimental.pallas import tpu as pltpu
from jax.sharding import PartitionSpec as P

F32 = jnp.float32
BF16 = jnp.bfloat16

SECTIONS = 4
FAMILIES = 2
ROWS = 128
STATE = 64
HEADDIM = 64
GROUP = 16
COLS = GROUP * HEADDIM
LANES = 128
CHUNK = 256
BRANCHES = 32
SEND_ROWS = 112
PACK_ROWS = FAMILIES * ROWS + 4 * GROUP
GRAD_ROWS = FAMILIES * (ROWS + GROUP)
VMEM_LIMIT = 63 * 1024 * 1024

NN = (((1,), (0,)), ((), ()))
NT = (((1,), (1,)), ((), ()))
TN = (((0,), (0,)), ((), ()))


def dot(a, b, dims):
    return lax.dot_general(a, b, dims, preferred_element_type=F32)


def split(a):
    high = a.astype(BF16)
    return high, (a - high.astype(F32)).astype(BF16)


def dot3(a, b, dims):
    return dot(a[0], b[0], dims) + dot(a[1], b[0], dims) + dot(a[0], b[1], dims)


def dot2(a, b, dims):
    return dot(a[0], b, dims) + dot(a[1], b, dims)


def lane_ids(shape):
    return lax.broadcasted_iota(jnp.int32, shape, len(shape) - 1)


def half(rolled, plain, side):
    lanes = lane_ids(plain.shape)
    if side == 0:
        return jnp.where(lanes < STATE, plain, 0.0)
    return jnp.where(lanes >= STATE, rolled, 0.0)


def expander():
    row = lax.broadcasted_iota(jnp.int32, (2 * GROUP, COLS), 0) & (GROUP - 1)
    col = lax.broadcasted_iota(jnp.int32, (2 * GROUP, COLS), 1) >> 6
    return jnp.where(row == col, 1.0, 0.0).astype(BF16)


def stack_split(a):
    high = a.astype(BF16).astype(F32)
    return jnp.concatenate([high, a - high], axis=0).astype(BF16)


def fetch_packs(layers, pack_refs, pack_buf, sems):
    mine = lax.axis_index("section")
    for at in layers:
        away = lax.rem(mine - at + SECTIONS, SECTIONS)
        for k in range(SECTIONS):

            @pl.when(away == k)
            def _():
                pltpu.make_async_copy(pack_refs[k], pack_buf.at[at], sems.at[at]).start()


def wait_packs(layers, pack_refs, pack_buf, sems):
    for at in layers:
        pltpu.make_async_copy(pack_refs[0], pack_buf.at[at], sems.at[at]).wait()


class Layer:
    def __init__(self, pack_ref, layer, family):
        base = FAMILIES * ROWS
        both = pack_ref[layer, family * ROWS : (family + 1) * ROWS, :]
        turned = pltpu.roll(both, STATE, 1)
        self.b = (half(both, both, 0), half(turned, turned, 1))
        self.c = (half(turned, turned, 0), half(both, both, 1))
        self.step = pack_ref[layer, base + family * GROUP : base + (family + 1) * GROUP, :]
        self.decay = pack_ref[layer, base + 2 * GROUP : base + 3 * GROUP, :]
        gain = pack_ref[layer, base + 3 * GROUP : base + 4 * GROUP, :]
        row = lax.broadcasted_iota(jnp.int32, (ROWS, ROWS), 0)
        col = lax.broadcasted_iota(jnp.int32, (ROWS, ROWS), 1)
        self.row, self.col = row, col
        upper = jnp.where(row <= col, 1.0, 0.0).astype(BF16)
        drop = -self.decay * self.step
        first = drop.astype(BF16)
        rest = drop - first.astype(F32)
        second = rest.astype(BF16)
        third = (rest - second.astype(F32)).astype(BF16)
        logs = dot(first, upper, NN) + dot(second, upper, NN) + dot(third, upper, NN)
        carried = jnp.exp(logs)
        scale = self.step * jnp.exp(-logs)
        total = jnp.sum(jnp.where(lane_ids(carried.shape) == ROWS - 1, carried, 0.0), axis=1, keepdims=True)
        self.total = jnp.broadcast_to(total, (GROUP, LANES))
        self.carried2 = stack_split(carried)
        self.scale2 = stack_split(scale)
        self.gain2 = stack_split(gain)
        pulled = dot3(split(self.b[0]), split(self.c[0]), NT)
        self.pull = split(jnp.where(row <= col, pulled, 0.0))


def phase_a(family, upper_at, high, low, expand, send_ref):
    c_pair = split(jnp.transpose(jnp.concatenate([high.c[0], low.c[1]], axis=0)))
    c_both = split(jnp.transpose(low.c[0] + low.c[1]))
    b_both = high.b[0] + high.b[1]
    b_tile = jnp.concatenate([b_both] * (CHUNK // LANES), axis=1)
    lanes = lane_ids((STATE // 2, LANES))
    for chunk in range(COLS // CHUNK):
        cols = slice(chunk * CHUNK, (chunk + 1) * CHUNK)
        spread = expand[:, cols]
        carried = dot(high.carried2, spread, TN)
        scale = dot(high.scale2, spread, TN)
        gain = dot(high.gain2, spread, TN)
        low_carried = dot(low.carried2, spread, TN)
        upstream = upper_at(cols)
        hat = carried * upstream
        hat2 = split(hat)
        pulled = dot(high.pull[0], hat2[0], NN)
        low_hat = low_carried * (gain * upstream + scale * pulled)
        low_hat2 = split(low_hat)
        both = tuple(jnp.concatenate([a, b], axis=0) for a, b in zip(hat2, low_hat2))
        begin = jnp.transpose(dot3(c_pair, both, NN)).astype(BF16)
        response = split(low_carried * scale * b_tile)
        move = jnp.transpose(dot3(c_both, response, NN))
        for inner in range(CHUNK // HEADDIM):
            head = family * GROUP + chunk * (CHUNK // HEADDIM) + inner
            top = inner * HEADDIM
            send_ref[head, 0:HEADDIM, :] = begin[top : top + HEADDIM, :]
            first = move[top : top + 32, :]
            second = move[top + 32 : top + 64, :]
            send_ref[head, HEADDIM : HEADDIM + 32, :] = jnp.where(lanes < STATE, first, second).astype(BF16)
    totals = jnp.where(lane_ids((GROUP, LANES)) < STATE, high.total, low.total)
    total_high = totals.astype(BF16).astype(F32)
    total_low = totals - total_high
    place = lax.broadcasted_iota(jnp.int32, (16, LANES), 0)
    for inner in range(GROUP):
        one = jnp.broadcast_to(total_high[inner : inner + 1, :], (16, LANES))
        two = jnp.broadcast_to(total_low[inner : inner + 1, :], (16, LANES))
        block = jnp.where(place == 0, one, jnp.where(place == 1, two, 0.0))
        send_ref[family * GROUP + inner, 96:112, :] = block.astype(BF16)


def phase_b(family, side, layer, upper_at, end_ref, expand, put_grad):
    b2 = split(layer.b[side])
    per_chunk = CHUNK // HEADDIM
    for chunk in range(COLS // CHUNK):
        cols = slice(chunk * CHUNK, (chunk + 1) * CHUNK)
        spread = expand[:, cols]
        carried = dot(layer.carried2, spread, TN)
        scale = dot(layer.scale2, spread, TN)
        gain = dot(layer.gain2, spread, TN)
        upstream = upper_at(cols)
        first = family * GROUP + chunk * per_chunk
        ends = end_ref[first : first + per_chunk].reshape(CHUNK, LANES)
        pulled = dot(layer.pull[0], (carried * upstream).astype(BF16), NN) + dot2(b2, ends, NT)
        put_grad(cols, (gain * upstream + scale * pulled).astype(BF16))


def phase_c(family, side, layer, upper_at, x_ref, s_ref, end_ref, expand):
    b_one, c_one = layer.b[side].astype(BF16), layer.c[side].astype(BF16)
    pull = layer.pull[0]
    read = dot(c_one, b_one, NT)
    read = jnp.where(layer.row >= layer.col, read, 0.0).astype(BF16)
    pairs = jnp.zeros((ROWS, ROWS), F32)
    grad_out = jnp.zeros((ROWS, LANES), F32)
    grad_in = jnp.zeros((ROWS, LANES), F32)
    flow = jnp.zeros((GROUP, ROWS), F32)
    worth = jnp.zeros((GROUP, ROWS), F32)
    ending = jnp.zeros((GROUP, ROWS), F32)
    skips = jnp.zeros((GROUP, ROWS), F32)
    lanes = lane_ids((CHUNK, LANES))
    per_chunk = CHUNK // HEADDIM
    for chunk in range(COLS // CHUNK):
        cols = slice(chunk * CHUNK, (chunk + 1) * CHUNK)
        spread = expand[:, cols]
        one = spread[0:GROUP]
        carried = dot(layer.carried2, spread, TN)
        scale = dot(layer.scale2, spread, TN)
        upstream = upper_at(cols)
        x = x_ref[family, :, cols].astype(F32)
        hat = carried * upstream
        hat_one = hat.astype(BF16)
        x_hat = scale * x
        x_one = x_hat.astype(BF16)
        first = family * GROUP + chunk * per_chunk
        ends = end_ref[first : first + per_chunk].reshape(CHUNK, LANES)
        top = (chunk % 2) * CHUNK
        packed = s_ref[family, top : top + CHUNK, :].astype(F32)
        if (chunk < 2) != (side == 0):
            packed = pltpu.roll(packed, STATE, 1)
        saved = jnp.where((lanes < STATE) == (side == 0), packed, 0.0)
        saved_one = saved.astype(BF16)
        end_in = dot(b_one, ends, NT)
        pulled = dot(pull, hat_one, NN) + end_in
        forward = dot(read, x_one, NN) + dot(c_one, saved_one, NT)
        pairs = pairs + dot(hat_one, x_one, NT)
        grad_out = grad_out + dot(hat_one, saved_one, NN)
        grad_in = grad_in + dot(x_one, ends, NN)
        x_pulled = x_hat * pulled
        worth = worth + dot(one, x_pulled.astype(BF16), NT)
        flow = flow + dot(one, (hat * forward - x_pulled).astype(BF16), NT)
        ending = ending + dot(one, (x_hat * end_in).astype(BF16), NT)
        ending = ending + dot(one, (ends.astype(F32) * saved).astype(BF16), NN)
        skips = skips + dot(one, (x * upstream).astype(BF16), NT)
    pairs = jnp.where(layer.row >= layer.col, pairs, 0.0).astype(BF16)
    grad_out = grad_out + dot(pairs, b_one, NN)
    grad_in = grad_in + dot(pairs, c_one, TN)
    lanes = lane_ids((ROWS, LANES))
    if side == 0:
        grads = jnp.where(lanes < STATE, grad_in, pltpu.roll(grad_out, STATE, 1))
    else:
        grads = jnp.where(lanes < STATE, pltpu.roll(grad_in, STATE, 1), grad_out)
    later = jnp.where(layer.row >= layer.col, 1.0, 0.0).astype(BF16)
    rate = dot2(split(flow), later, NN) + jnp.sum(ending, axis=1, keepdims=True)
    grad_step = worth / layer.step - layer.decay * rate
    decay_part = jnp.sum(-layer.step * rate, axis=1, keepdims=True)
    skip_part = jnp.sum(skips, axis=1, keepdims=True)
    place = lane_ids((GROUP, LANES))
    small = jnp.where(place == 0, decay_part, jnp.where(place == 1, skip_part, 0.0))
    return grads, grad_step, small


def first_kernel(high_at, after, *refs):
    lengths_ref, cot_ref = refs[:2]
    pack_refs = refs[2:6]
    send_ref, up_ref, cot_buf, send_buf, pack_ref, sems, pack_sem = refs[6 + after :]
    layers = (high_at, high_at - 1)
    fetch_packs(layers, pack_refs, pack_ref, pack_sem)
    mine = lax.axis_index("section")
    branch = lax.axis_index("branch")
    at = pl.multiple_of(mine * COLS, COLS)
    copy = pltpu.make_async_copy(cot_ref.at[:, :, pl.ds(at, COLS)], cot_buf, sems.at[3])
    copy.start()
    expand = expander()
    wait_packs(layers, pack_refs, pack_ref, pack_sem)
    copy.wait()
    copies = []
    for family in range(FAMILIES):
        slot = jnp.clip(branch - BRANCHES // 2, 0, BRANCHES // 2 - 1)
        limit = jnp.where(branch >= BRANCHES // 2, lengths_ref[family, slot], ROWS)

        def upper_at(cols):
            rows = lax.broadcasted_iota(jnp.int32, (ROWS, CHUNK), 0)
            value = jnp.where(rows < limit, cot_buf[family, :, cols].astype(F32), 0.0)
            cot_buf[family, :, cols] = value.astype(BF16)
            return value

        high = Layer(pack_ref, high_at, family)
        low = Layer(pack_ref, high_at - 1, family)
        phase_a(family, upper_at, high, low, expand, send_buf)
        heads = pl.ds(family * GROUP, GROUP)
        copies.append(pltpu.make_async_copy(send_buf.at[heads], send_ref.at[heads], sems.at[family]))
        copies[-1].start()
    copies.append(pltpu.make_async_copy(cot_buf, up_ref, sems.at[2]))
    copies[-1].start()
    for copy in copies:
        copy.wait()


def later_kernel(high_at, goes_on, after, *refs):
    pack_refs = refs[:4]
    up_ref, end_ref = refs[4:6]
    refs = refs[6 + after :]
    grad_refs, keep_refs = refs[0:4], refs[4:6]
    rest = refs[6:]
    if goes_on:
        send_ref, grad_buf, up_buf, end_buf, pack_ref, grad_sem, keep_sem, in_sem, pack_sem, send_buf, send_sem = rest
    else:
        grad_buf, up_buf, end_buf, pack_ref, grad_sem, keep_sem, in_sem, pack_sem = rest
    layers = range(high_at, high_at - (4 if goes_on else 2), -1)
    fetch_packs(layers[:2], pack_refs, pack_ref, pack_sem)
    ins = [
        pltpu.make_async_copy(up_ref, up_buf, in_sem.at[0]),
        pltpu.make_async_copy(end_ref, end_buf, in_sem.at[1]),
    ]
    for copy in ins:
        copy.start()
    fetch_packs(layers[2:], pack_refs, pack_ref, pack_sem)
    mine = lax.axis_index("section")
    expand = expander()
    wait_packs(layers[:2], pack_refs, pack_ref, pack_sem)
    for copy in ins:
        copy.wait()
    for side in range(2):
        layer_at = high_at - side
        for family in range(FAMILIES):

            def upper_at(cols):
                if side == 0:
                    return up_buf[family, :, cols].astype(F32)
                return grad_buf[0, family, :, cols].astype(F32)

            def put_grad(cols, value):
                grad_buf[side, family, :, cols] = value

            layer = Layer(pack_ref, layer_at, family)
            phase_b(family, side, layer, upper_at, end_buf, expand, put_grad)
        ahead = lax.rem(layer_at - mine + SECTIONS, SECTIONS)
        for k in range(SECTIONS):

            @pl.when(ahead == k)
            def _():
                pltpu.make_async_copy(grad_buf.at[side], grad_refs[k], grad_sem.at[side]).start()

    copies = [pltpu.make_async_copy(grad_buf.at[side], keep_refs[side], keep_sem.at[side]) for side in range(2)]
    for copy in copies:
        copy.start()
    if goes_on:
        wait_packs(layers[2:], pack_refs, pack_ref, pack_sem)
        for family in range(FAMILIES):

            def upper_at(cols):
                return grad_buf[1, family, :, cols].astype(F32)

            high = Layer(pack_ref, high_at - 2, family)
            low = Layer(pack_ref, high_at - 3, family)
            phase_a(family, upper_at, high, low, expand, send_buf)
            heads = pl.ds(family * GROUP, GROUP)
            copies.append(pltpu.make_async_copy(send_buf.at[heads], send_ref.at[heads], send_sem.at[family]))
            copies[-1].start()
    for copy in copies:
        copy.wait()
    for side in range(2):
        pltpu.make_async_copy(grad_buf.at[side], grad_refs[0], grad_sem.at[side]).wait()


def other_kernel(high_at, sides, after, *refs):
    pack_refs, up_refs = refs[:4], refs[4:6]
    end_ref, own_x = refs[6:8]
    x_refs, s_refs = refs[8:11], refs[11:15]
    held_ref, small_refs = refs[15], refs[16:18]
    refs = refs[18 + after :]
    last = 1 in sides
    part_refs, rest = (refs[:4], refs[4:]) if last else (refs[:1], refs[1:])
    rate_ref, rest = rest[0], rest[1:]
    x_buf, s_buf, up_buf, end_buf, part_buf, pack_ref, x_sem, s_sem, up_sem, part_sem, end_sem, pack_sem = rest
    mine = lax.axis_index("section")
    at = pl.multiple_of(mine * COLS, COLS)
    sources = (own_x.at[0, :, :, pl.ds(at, COLS)],) + tuple(x_refs)
    layers = [high_at - side for side in sides]
    fetch_packs(layers, pack_refs, pack_ref, pack_sem)
    ends = pltpu.make_async_copy(end_ref, end_buf, end_sem.at[0])
    ends.start()
    for side in sides:
        away = lax.rem(mine - (high_at - side) + SECTIONS, SECTIONS)
        pltpu.make_async_copy(up_refs[side], up_buf.at[side], up_sem.at[side]).start()
        for k in range(SECTIONS):

            @pl.when(away == k)
            def _():
                pltpu.make_async_copy(sources[k], x_buf.at[side], x_sem.at[side]).start()
                pltpu.make_async_copy(s_refs[k], s_buf.at[side], s_sem.at[side]).start()

    if sides == (1,):
        held = pltpu.make_async_copy(held_ref, part_buf.at[0], part_sem.at[0])
        held.start()
    expand = expander()
    wait_packs(layers, pack_refs, pack_ref, pack_sem)
    ends.wait()
    smalls_of = []
    for side in sides:
        pltpu.make_async_copy(up_refs[side], up_buf.at[side], up_sem.at[side]).wait()
        pltpu.make_async_copy(x_refs[0], x_buf.at[side], x_sem.at[side]).wait()
        pltpu.make_async_copy(s_refs[0], s_buf.at[side], s_sem.at[side]).wait()
        smalls = jnp.zeros((GROUP, LANES), F32)
        for family in range(FAMILIES):

            def upper_at(cols):
                return up_buf[side, family, :, cols].astype(F32)

            layer = Layer(pack_ref, high_at - side, family)
            grads, grad_step, small = phase_c(
                family, side, layer, upper_at, x_buf.at[side], s_buf.at[side], end_buf, expand
            )
            part_buf[side, family * ROWS : (family + 1) * ROWS, :] = grads.astype(BF16)
            below = FAMILIES * ROWS + family * GROUP
            part_buf[side, below : below + GROUP, :] = grad_step.astype(BF16)
            smalls = smalls + small
        smalls_of.append(smalls)
    if len(sides) == 1:
        rate_ref[...] = smalls_of[0]
    else:
        blocks = smalls_of[::-1] + [small_refs[1][...], small_refs[0][...]]
        turned = jnp.transpose(jnp.concatenate(blocks + [jnp.zeros((STATE, LANES), F32)], axis=0))
        row = turned[0:1] + pltpu.roll(turned[1:2], STATE, 1)
        rate_ref[...] = jnp.broadcast_to(row[None], (BRANCHES, 1, LANES))
    if not last:
        copy = pltpu.make_async_copy(part_buf.at[0], part_refs[0], part_sem.at[0])
        copy.start()
        copy.wait()
        return
    if sides == (1,):
        held.wait()
    for side in range(2):
        ahead = lax.rem(high_at - side - mine + SECTIONS, SECTIONS)
        for k in range(SECTIONS):

            @pl.when(ahead == k)
            def _():
                pltpu.make_async_copy(part_buf.at[side], part_refs[k], part_sem.at[side]).start()

    for side in range(2):
        pltpu.make_async_copy(part_buf.at[side], part_refs[0], part_sem.at[side]).wait()


def chain_kernel(*refs):
    got_ref, end_ref = refs[0], refs[-1]
    lanes = lane_ids((STATE // 2, LANES))
    prompt = BRANCHES // 2
    fork = jnp.zeros((HEADDIM, LANES), F32)
    for at in range(prompt, BRANCHES):
        fork = fork + got_ref[at, 0:HEADDIM, :].astype(F32)
    plain, extra = fork, jnp.zeros((HEADDIM, LANES), F32)
    blank = jnp.zeros((STATE, LANES), F32)
    for at in range(prompt - 1, -1, -1):
        tail = got_ref[at, 96:112, :].astype(F32)
        total = tail[0:1, :] + tail[1:2, :]
        plain = total * plain
        extra = total * extra
        end_ref[at, :, :] = (plain + extra).astype(BF16)
        if at == 0:
            break
        packed = got_ref[at, HEADDIM : HEADDIM + 32, :].astype(F32)
        turned = pltpu.roll(packed, STATE, 1)
        move = jnp.concatenate(
            [jnp.where(lanes >= STATE, turned, 0.0), jnp.where(lanes >= STATE, packed, 0.0), blank], axis=0
        ).astype(BF16)
        extra = extra + dot2(split(plain), move, NN)
        plain = plain + got_ref[at, 0:HEADDIM, :].astype(F32)
    for at in range(prompt, BRANCHES):
        end_ref[at, :, :] = jnp.zeros((HEADDIM, LANES), BF16)


def pack_kernel(*refs):
    sources, decay_ref, gain_ref = refs[0:3], refs[3], refs[4]
    pack_refs = refs[5:9]
    in_ref, out_ref, step_ref, both_ref, rate_ref, sems, send_sems = refs[9:]
    copies = [
        pltpu.make_async_copy(source.at[0], to, sems.at[at])
        for at, (source, to) in enumerate(zip(sources, (in_ref, out_ref, step_ref)))
    ]
    for copy in copies:
        copy.start()
    mine = lax.axis_index("section")
    base = FAMILIES * ROWS
    rate_ref[0] = jnp.transpose(jnp.broadcast_to(decay_ref[...], (LANES, SECTIONS * GROUP)))
    rate_ref[1] = jnp.transpose(jnp.broadcast_to(gain_ref[...], (LANES, SECTIONS * GROUP)))
    for copy in copies:
        copy.wait()
    for k in range(SECTIONS):
        heads = pl.ds(pl.multiple_of(lax.rem(mine + k, SECTIONS) * GROUP, GROUP), GROUP)
        for family in range(FAMILIES):
            both_ref[k, base + family * GROUP : base + (family + 1) * GROUP, :] = step_ref[family, heads, :]
        both_ref[k, base + 2 * GROUP : base + 3 * GROUP, :] = rate_ref[0, heads, :]
        both_ref[k, base + 3 * GROUP : base + 4 * GROUP, :] = rate_ref[1, heads, :]
    for family in range(FAMILIES):
        turned = jnp.transpose(jnp.concatenate([in_ref[family], out_ref[family]], axis=0))
        for k in range(SECTIONS):
            both_ref[k, family * ROWS : (family + 1) * ROWS, :] = turned
    copies = []
    for k in range(SECTIONS):
        copies.append(pltpu.make_async_copy(both_ref.at[k], pack_refs[k], send_sems.at[k]))
        copies[-1].start()
    for copy in copies:
        copy.wait()


def sort_kernel(at_ref, x1, x2, x3, s0, s1, s2, s3, o1, o2, o3, p0, p1, p2, p3):
    for x_ref, o_ref in ((x1, o1), (x2, o2), (x3, o3)):
        o_ref[0] = x_ref[0, 0]
    for s_ref, p_ref in ((s0, p0), (s1, p1), (s2, p2), (s3, p3)):
        whole = s_ref[0, 0, 0].reshape(COLS, STATE)
        p_ref[0] = jnp.concatenate([whole[: COLS // 2], whole[COLS // 2 :]], axis=1).astype(BF16)


def fetch_home(early, late, to, sems):
    mine = lax.axis_index("section")
    for is_early, pieces in ((True, early), (False, late)):

        @pl.when((mine >= 2) == is_early)
        def _():
            for k in range(SECTIONS):
                source = lax.rem(mine - k + SECTIONS, SECTIONS)
                pltpu.make_async_copy(pieces[k], to(source), sems.at[k]).start()

    for k in range(SECTIONS):
        pltpu.make_async_copy(early[k], to(k), sems.at[k]).wait()


def home_small_kernel(*refs):
    early, late = refs[0:4], refs[4:8]
    in_ref, out_ref, step_ref, part_buf, part_sem = refs[8:]
    fetch_home(early, late, lambda source: part_buf.at[source], part_sem)
    for family in range(FAMILIES):
        rows = slice(family * ROWS, (family + 1) * ROWS)
        total = part_buf[0, rows, :].astype(F32)
        for k in range(1, SECTIONS):
            total = total + part_buf[k, rows, :].astype(F32)
        turned = jnp.transpose(total)
        in_ref[0, family] = turned[0:STATE]
        out_ref[0, family] = turned[STATE:]
        below = FAMILIES * ROWS + family * GROUP
        for k in range(SECTIONS):
            step_ref[0, family, k * GROUP : (k + 1) * GROUP, :] = part_buf[k, below : below + GROUP, :].astype(F32)


def home_grad_kernel(*refs):
    early, late = refs[0:4], refs[4:8]
    grad_ref, grad_buf, grad_sem = refs[8:]
    fetch_home(early, late, lambda source: grad_buf.at[:, :, pl.ds(source * COLS, COLS)], grad_sem)
    out = pltpu.make_async_copy(grad_buf, grad_ref.at[0], grad_sem.at[0])
    out.start()
    out.wait()


def rate_sum_kernel(scale, *refs):
    got_ref, sum_ref = refs[0], refs[-1]
    total = got_ref[0]
    for at in range(1, BRANCHES):
        total = total + got_ref[at]
    sum_ref[...] = jnp.broadcast_to((total * scale)[None], (SECTIONS, 1, LANES))


def rate_home_kernel(got_ref, decay_ref, skip_ref):
    mine = lax.axis_index("section")
    section = (lane_ids((8, LANES)) & (STATE - 1)) >> 4
    total = jnp.zeros((8, LANES), F32)
    for at in range(SECTIONS):
        row = jnp.broadcast_to(got_ref[at], (8, LANES))
        shift = lax.rem(at - mine + SECTIONS, SECTIONS) * GROUP
        ahead, behind = pltpu.roll(row, shift, 1), pltpu.roll(row, shift + STATE, 1)
        low = (lane_ids((8, LANES)) & (STATE - 1)) >= shift
        total = jnp.where(section == at, jnp.where(low, ahead, behind), total)
    decay_ref[...] = total[0:1, 0:STATE]
    skip_ref[...] = total[0:1, STATE:]


VM = pl.BlockSpec(memory_space=pltpu.VMEM)
SM = pl.BlockSpec(memory_space=pltpu.SMEM)
ANY = pl.BlockSpec(memory_space=pl.ANY)
HBM = pl.BlockSpec(memory_space=pltpu.HBM)
PARAMS = pltpu.CompilerParams(vmem_limit_bytes=VMEM_LIMIT)
SMALL_PARAMS = pltpu.CompilerParams(vmem_limit_bytes=32 * 1024 * 1024)


PACKS = pltpu.VMEM((SECTIONS, PACK_ROWS, LANES), F32)


def shape(dims, dtype):
    return jax.ShapeDtypeStruct(dims, dtype)


def cost(flops):
    return pl.CostEstimate(flops=flops, bytes_accessed=4_000_000, transcendentals=0)


def sems(count):
    return pltpu.SemaphoreType.DMA((count,))


def pack_small(state_in, state_out, step_size, decay_rate, skip_gain):
    turned = [jnp.transpose(value, (0, 1, 3, 2)) for value in (state_in, state_out, step_size)]
    return pl.pallas_call(
        pack_kernel,
        out_shape=[shape((PACK_ROWS, LANES), F32)] * SECTIONS,
        in_specs=[ANY] * 3 + [VM] * 2,
        out_specs=[HBM] * SECTIONS,
        scratch_shapes=[
            pltpu.VMEM((FAMILIES, STATE, ROWS), F32),
            pltpu.VMEM((FAMILIES, STATE, ROWS), F32),
            pltpu.VMEM((FAMILIES, SECTIONS * GROUP, ROWS), F32),
            pltpu.VMEM((SECTIONS, PACK_ROWS, LANES), F32),
            pltpu.VMEM((2, SECTIONS * GROUP, LANES), F32),
            sems(3),
            sems(4),
        ],
        compiler_params=PARAMS,
        name="pack_small",
    )(*turned, decay_rate, skip_gain)


def sort_heads(layer_input, saved_states):
    mine = jnp.full((1,), lax.axis_index("section"), jnp.int32)

    def x_spec(k):
        return pl.BlockSpec(
            (1, 1, ROWS, COLS), lambda f, at: (0, f, 0, lax.rem(at[0] + k, SECTIONS))
        )

    def s_spec(k):
        return pl.BlockSpec(
            (1, 1, 1, GROUP, HEADDIM, STATE), lambda f, at: (0, f, 0, lax.rem(at[0] + k, SECTIONS), 0, 0)
        )

    x_out = pl.BlockSpec((1, ROWS, COLS), lambda f, at: (f, 0, 0))
    s_out = pl.BlockSpec((1, COLS // 2, LANES), lambda f, at: (f, 0, 0))
    outs = pl.pallas_call(
        sort_kernel,
        grid_spec=pltpu.PrefetchScalarGridSpec(
            num_scalar_prefetch=1,
            grid=(FAMILIES,),
            in_specs=[x_spec(1), x_spec(2), x_spec(3)] + [s_spec(k) for k in range(SECTIONS)],
            out_specs=[x_out] * 3 + [s_out] * 4,
        ),
        out_shape=[shape((FAMILIES, ROWS, COLS), BF16)] * 3 + [shape((FAMILIES, COLS // 2, LANES), BF16)] * 4,
        compiler_params=PARAMS,
        cost_estimate=cost(4_000_000_000),
        name="sort_heads",
    )(mine, layer_input, layer_input, layer_input, *([saved_states] * 4))
    return outs[:3], outs[3:]


def first_phase(high_at, lengths, cotangent, packs, after):
    return pl.pallas_call(
        functools.partial(first_kernel, high_at, len(after)),
        out_shape=[
            shape((BRANCHES, SEND_ROWS, LANES), BF16),
            shape((FAMILIES, ROWS, COLS), BF16),
        ],
        in_specs=[SM] + [ANY] * (5 + len(after)),
        out_specs=[HBM, HBM],
        scratch_shapes=[
            pltpu.VMEM((FAMILIES, ROWS, COLS), BF16),
            pltpu.VMEM((BRANCHES, SEND_ROWS, LANES), BF16),
            PACKS,
            sems(4),
            sems(4),
        ],
        compiler_params=PARAMS,
        name="first_phase",
    )(lengths, cotangent, *packs, *after)


def later_phase(high_at, goes_on, packs, upstream, ends, after):
    outs = [shape((FAMILIES, ROWS, COLS), BF16)] * 4
    outs += [shape((FAMILIES, ROWS, COLS), BF16)] * 2
    scratch = [
        pltpu.VMEM((2, FAMILIES, ROWS, COLS), BF16),
        pltpu.VMEM((FAMILIES, ROWS, COLS), BF16),
        pltpu.VMEM((BRANCHES, HEADDIM, LANES), BF16),
        PACKS,
        sems(2),
        sems(2),
        sems(2),
        sems(4),
    ]
    if goes_on:
        outs += [shape((BRANCHES, SEND_ROWS, LANES), BF16)]
        scratch += [pltpu.VMEM((BRANCHES, SEND_ROWS, LANES), BF16), sems(2)]
    return pl.pallas_call(
        functools.partial(later_kernel, high_at, goes_on, len(after)),
        out_shape=outs,
        in_specs=[ANY] * (6 + len(after)),
        out_specs=[HBM] * len(outs),
        scratch_shapes=scratch,
        compiler_params=PARAMS,
        name="later_phase",
    )(*packs, upstream, ends, *after)


def other_phase(high_at, sides, packs, ups, ends, layer_input, xs, states, held, smalls, after):
    count = 4 if 1 in sides else 1
    return pl.pallas_call(
        functools.partial(other_kernel, high_at, sides, len(after)),
        out_shape=[shape((GRAD_ROWS, LANES), BF16)] * count
        + [shape((GROUP, LANES), F32) if len(sides) == 1 else shape((BRANCHES, 1, LANES), F32)],
        in_specs=[ANY] * 16 + [VM] * 2 + [ANY] * len(after),
        out_specs=[HBM] * count + [VM],
        scratch_shapes=[
            pltpu.VMEM((2, FAMILIES, ROWS, COLS), BF16),
            pltpu.VMEM((2, FAMILIES, COLS // 2, LANES), BF16),
            pltpu.VMEM((2, FAMILIES, ROWS, COLS), BF16),
            pltpu.VMEM((BRANCHES, HEADDIM, LANES), BF16),
            pltpu.VMEM((2, GRAD_ROWS, LANES), BF16),
            PACKS,
            sems(2),
            sems(2),
            sems(2),
            sems(2),
            sems(1),
            sems(4),
        ],
        compiler_params=PARAMS,
        cost_estimate=cost(6_000_000_000 * len(sides)),
        name="other_phase",
    )(*packs, *ups, ends, layer_input, *xs, *states, held, *smalls, *after)


def chain(got, after):
    return pl.pallas_call(
        chain_kernel,
        out_shape=shape((BRANCHES, HEADDIM, LANES), BF16),
        in_specs=[VM] + [ANY] * len(after),
        out_specs=VM,
        compiler_params=SMALL_PARAMS,
        name="chain",
    )(got, *after)


def home_small(early, late):
    return pl.pallas_call(
        home_small_kernel,
        out_shape=[
            shape((1, FAMILIES, STATE, ROWS), F32),
            shape((1, FAMILIES, STATE, ROWS), F32),
            shape((1, FAMILIES, SECTIONS * GROUP, ROWS), F32),
        ],
        in_specs=[ANY] * 8,
        out_specs=[VM] * 3,
        scratch_shapes=[pltpu.VMEM((SECTIONS, GRAD_ROWS, LANES), BF16), sems(SECTIONS)],
        compiler_params=PARAMS,
        name="home_small",
    )(*early, *late)


def home_grad(early, late):
    return pl.pallas_call(
        home_grad_kernel,
        out_shape=shape((1, FAMILIES, ROWS, SECTIONS * COLS), BF16),
        in_specs=[ANY] * 8,
        out_specs=HBM,
        scratch_shapes=[pltpu.VMEM((FAMILIES, ROWS, SECTIONS * COLS), BF16), sems(SECTIONS)],
        compiler_params=PARAMS,
        cost_estimate=cost(3_000_000_000),
        name="home_grad",
    )(*early, *late)


def rate_sum(got, scale, after):
    return pl.pallas_call(
        functools.partial(rate_sum_kernel, scale),
        out_shape=shape((SECTIONS, 1, LANES), F32),
        in_specs=[VM] + [ANY] * len(after),
        out_specs=VM,
        compiler_params=SMALL_PARAMS,
        name="rate_sum",
    )(got, *after)


def rate_home(got):
    return pl.pallas_call(
        rate_home_kernel,
        out_shape=[shape((1, SECTIONS * GROUP), F32)] * 2,
        in_specs=[VM],
        out_specs=[VM] * 2,
        compiler_params=SMALL_PARAMS,
        name="rate_home",
    )(got)


def swap(value, axis):
    return lax.all_to_all(value, axis, 0, 0, tiled=True)


def send_on(value, k, targets):
    pairs = [(i, (i + k) % SECTIONS) for i in range(SECTIONS) if (i + k) % SECTIONS in targets]
    return lax.ppermute(value, "section", pairs)


def send_home(pieces, targets):
    return [pieces[0]] + [send_on(pieces[k], k, targets) for k in range(1, SECTIONS)]


def exchange(send, after):
    return swap(chain(swap(send, "branch"), after), "branch")


def shards(
    layer_input,
    cotangent,
    state_in,
    state_out,
    step_size,
    saved_states,
    decay_rate,
    skip_gain,
    lengths,
):
    grad_scale = 1.0 / math.sqrt(FAMILIES * ROWS * BRANCHES * HEADDIM)
    everyone = tuple(range(SECTIONS))
    packs = pack_small(state_in, state_out, step_size, decay_rate, skip_gain)
    packs = [packs[0]] + [send_on(packs[k], k, everyone) for k in range(1, SECTIONS)]
    sorted_xs, sorted_states = sort_heads(layer_input, saved_states)
    xs = [send_on(sorted_xs[k - 1], k, everyone) for k in range(1, SECTIONS)]
    states = [sorted_states[0]] + [send_on(sorted_states[k], k, everyone) for k in range(1, SECTIONS)]
    top, upstream = first_phase(3, lengths, cotangent, packs, [sorted_states[0]])
    ends = exchange(top, [])
    early = later_phase(3, True, packs, upstream, ends, xs + states[1:])
    early_grads = send_home(early[:4], (2, 3))
    ups = (upstream, early[4])
    blank = jnp.zeros((GROUP, LANES), F32)
    held, small_a = other_phase(3, (0,), packs, ups, ends, layer_input, xs, states, packs[0], [blank, blank], [])
    got = swap(early[6], "branch")
    next_ends = swap(chain(got, [held]), "branch")
    *early_parts, small_b = other_phase(
        3, (1,), packs, ups, ends, layer_input, xs, states, held, [small_a, small_a], []
    )
    early_parts = send_home(early_parts, (2, 3))
    late = later_phase(1, False, packs, early[5], next_ends, early_grads[1:])
    late_grads = send_home(late[:4], (0, 1))
    ups = (early[5], late[4])
    *late_parts, rates = other_phase(
        1, (0, 1), packs, ups, next_ends, layer_input, xs, states, packs[0], [small_a, small_b], early_parts[1:]
    )
    late_parts = send_home(late_parts, (0, 1))
    others = home_small(early_parts, late_parts)
    rates = rate_sum(swap(rates, "branch"), grad_scale, late_parts[1:])
    rates = rate_home(swap(rates, "section"))
    others = tuple(jnp.transpose(value, (0, 1, 3, 2)) for value in others)
    return (home_grad(early_grads, late_grads),) + others + tuple(rates)


def solution(mesh):
    placed = (
        P("section", None, "branch", None),
        P(None, "branch", None),
        P("section", None, "branch", None),
        P("section", None, "branch", None),
        P("section", None, "branch", None),
        P("section", None, "branch", None, None, None),
        P("section", None),
        P("section", None),
        P(),
    )
    return jax.shard_map(
        shards,
        mesh=mesh,
        in_specs=placed,
        out_specs=(
            P("section", None, "branch", None),
            P("section", None, "branch", None),
            P("section", None, "branch", None),
            P("section", None, "branch", None),
            P("section", None),
            P("section", None),
        ),
        check_vma=False,
    )
```

time: 259 us -> 199 us (0.77)
  the two profiles are of different devices: /device:TPU:64 before, /device:TPU:0 now
where the time goes in v2:
time: 199 us; the launch traced here: 198 us
  starting transfers between devices  74.9 us (38%)
  Pallas kernels  61.7 us (31%)
  waiting for transfers between devices  38.9 us (20%)
  blocking collectives  14.5 us (7%)
  local copies, waits for them, and re-layouts  6.82 us (3%)
    ppermute x21, starting transfers between devices, send_on(): return lax.ppermute(value, 'section', pairs)  44.8 us
    all_to_all x5, starting transfers between devices, swap(): return lax.all_to_all(value, axis, 0, 0, tiled=True)  30 us
    ppermute x21, waiting for transfers between devices, send_on(): return lax.ppermute(value, 'section', pairs)  26 us
    pallas_call x3, Pallas kernels, other_phase(): pl.pallas_call(functools.partial(other_kernel, high_at, sides, len(after)...  25.9 us
    all_to_all x1, blocking collectives, swap(): return lax.all_to_all(value, axis, 0, 0, tiled=True)  14.5 us
    pallas_call x2, Pallas kernels, later_phase(): pl.pallas_call(functools.partial(later_kernel, high_at, goes_on, len(afte...  14.2 us
    all_to_all x5, waiting for transfers between devices, swap(): return lax.all_to_all(value, axis, 0, 0, tiled=True)  12.9 us
    pallas_call x1, Pallas kernels, first_phase(): pl.pallas_call(functools.partial(first_kernel, high_at, len(after)), out_...  6.88 us
  transfers between devices with their start and end apart: 26, of which 6 were waited for; matrix products, arithmetic and copies ran while one was open for 0% of the time, Pallas kernels for 20%

profile of v2, /device:TPU:0, one launch (start us, length us, event | category | flops | bytes accessed | tf_op | source)
XLA Modules:
  0.0 198.1 jit_solution(5586072427702107582)
XLA Ops:
  0.6 2.6 %pack_small.1 = (f32[320,128]{1,0:T(8,128)}, f32[320,128]{1,0:T(8,128)}, f32[320,128]{1,0:T(8,128)}, f32[320,128]{1,0:T(8,128)}) custom-call(f32[1,2,64,128]{3,2,1,0:T(8,128)} %bitcast.7, f32[1,2,64,128]{3,2,1,0:T(8,128)} %bitcast.8, f32[1,2,64,128]{3,2,1,0:T(8,128)} %bitcast.9, f32[1,64]{1,0:T(1,128)} %refs_3_.1, f32[1,64]{1,0:T(1,128)} %refs_4_.1), custom_call_target="tpu_custom_call" | custom-call | tf_op jit(solution)/shard_map/pack_small/pallas_call | solution.py:581
  3.2 2.1 %collective-permute-start = (f32[320,128]{1,0:T(8,128)}, f32[320,128]{1,0:T(8,128)S(1)}, u32[]{:S(2)}, u32[]{:S(2)}) collective-permute-start(f32[320,128]{1,0:T(8,128)} %get-tuple-element.49), channel_id=1, source_target_pairs={{0,32},{32,64},{64,96},{96,0},{1,33},{33,65},{65,97},{97,1},{2,34}... | collective-permute-start | bytes 491528 | tf_op jit(solution)/shard_map/ppermute | solution.py:775
  5.3 3.6 %collective-permute-start.1 = (f32[320,128]{1,0:T(8,128)}, f32[320,128]{1,0:T(8,128)S(1)}, u32[]{:S(2)}, u32[]{:S(2)}) collective-permute-start(f32[320,128]{1,0:T(8,128)} %get-tuple-element.50), channel_id=1, source_target_pairs={{0,64},{32,96},{64,0},{96,32},{1,65},{33,97},{65,1},{97,33},{2,66}... | collective-permute-start | bytes 491528 | tf_op jit(solution)/shard_map/ppermute | solution.py:775
  8.9 1.0 collective-permute-start.2
  9.9 4.0 %sort_heads.1 = (bf16[2,128,1024]{2,1,0:T(8,128)(2,1)}, bf16[2,128,1024]{2,1,0:T(8,128)(2,1)}, bf16[2,128,1024]{2,1,0:T(8,128)(2,1)}, bf16[2,512,128]{2,1,0:T(8,...) custom-call(s32[1]{0:T(128)} %bitcast.3.at_ref, ...), custom_call_target="tpu_custom_call" | custom-call | flops 4000000000 | bytes 4000000 | tf_op jit(solution)/shard_map/sort_heads/pallas_call | solution.py:615
  13.9 2.6 %collective-permute-done.1.refs_4_.refs_2_ = f32[320,128]{1,0:T(8,128)S(1)} collective-permute-done((f32[320,128]{1,0:T(8,128)}, f32[320,128]{1,0:T(8,128)S(1)}, u32[]{:S(2)}, u32[]{:S(2)}) %collective-permute-start.1) | collective-permute-done | bytes 163872 | tf_op jit(solution)/shard_map/ppermute | solution.py:775
  16.5 0.0 collective-permute-done.2.refs_5_.refs_3_
  16.5 0.7 copy-done.7
  17.2 0.1 copy-done.8
  17.2 6.9 %first_phase.1 = (bf16[32,112,128]{2,1,0:T(8,128)(2,1)}, bf16[2,128,1024]{2,1,0:T(8,128)(2,1)}) custom-call(s32[2,16]{1,0:T(2,128)} %refs_0_.1, bf16[2,128,4096]{2,1,0:T(8,128)(2,1)} %refs_1_.1, f32[320,128]{1,0:T(8,128)} %get-tuple-element.48.refs_2_.refs_0_.refs_15_, f32[320,128]{1,0:T(8,128)} %copy-done.6, f32[320,128]{1,0:T(8,128)} %copy-done.7, ...), custom_call_target="tpu_custom_call" | custom-call | tf_op jit(solution)/shard_map/first_phase/pallas_call | solution.py:632
  24.1 7.3 %all-to-all-start = ((bf16[32,112,128]{2,1,0:T(8,128)(2,1)}), bf16[32,112,128]{2,1,0:T(8,128)(2,1)S(1)}, u32[]{:S(2)}, u32[]{:S(2)}) async-start(bf16[32,112,128]{2,1,0:T(8,128)(2,1)} %get-tuple-element.54), calls=%async_computation | async-start | bytes 1835008 | tf_op jit(solution)/shard_map/all_to_all | solution.py:770
  31.5 1.2 collective-permute-start.6
  32.7 1.0 collective-permute-start.3
  33.6 2.6 %collective-permute-start.4 = (bf16[2,128,1024]{2,1,0:T(8,128)(2,1)}, bf16[2,128,1024]{2,1,0:T(8,128)(2,1)S(1)}, u32[]{:S(2)}, u32[]{:S(2)}) collective-permute-start(bf16[2,128,1024]{2,1,0:T(8,128)(2,1)} %get-tuple-element.56), channel_id=1, source_target_pairs={{0,64},{32,96},{64,0},{96,32},{1,65},{33,97},{65,1},{97,33},{2,66}... | collective-permute-start | bytes 1572872 | tf_op jit(solution)/shard_map/ppermute | solution.py:775
  36.2 1.5 collective-permute-start.5
  37.7 9.7 %all-to-all-done.refs_0_ = bf16[32,112,128]{2,1,0:T(8,128)(2,1)S(1)} async-done(((bf16[32,112,128]{2,1,0:T(8,128)(2,1)}), bf16[32,112,128]{2,1,0:T(8,128)(2,1)S(1)}, u32[]{:S(2)}, u32[]{:S(2)}) %all-to-all-start) | async-done | bytes 917536 | tf_op jit(solution)/shard_map/all_to_all | solution.py:770
  47.4 1.2 chain.2
  48.5 3.9 %all-to-all-start.1 = ((bf16[32,64,128]{2,1,0:T(8,128)(2,1)}), bf16[32,64,128]{2,1,0:T(8,128)(2,1)S(1)}, u32[]{:S(2)}, u32[]{:S(2)}) async-start(bf16[32,64,128]{2,1,0:T(8,128)(2,1)} %chain.2), calls=%async_computation.1 | async-start | bytes 1048576 | tf_op jit(solution)/shard_map/all_to_all | solution.py:770
  52.4 2.2 %collective-permute-start.7 = (bf16[2,512,128]{2,1,0:T(8,128)(2,1)}, bf16[2,512,128]{2,1,0:T(8,128)(2,1)S(1)}, u32[]{:S(2)}, u32[]{:S(2)}) collective-permute-start(bf16[2,512,128]{2,1,0:T(8,128)(2,1)} %get-tuple-element.59), channel_id=1, source_target_pairs={{0,64},{32,96},{64,0},{96,32},{1,65},{33,97},{65,1},{97,33},{2,66}... | collective-permute-start | bytes 786440 | tf_op jit(solution)/shard_map/ppermute | solution.py:775
  54.7 0.0 collective-permute-done.6.refs_9_.refs_12_
  54.7 1.7 collective-permute-start.8
  56.4 13.5 %collective-permute-done.7.refs_10_.refs_13_ = bf16[2,512,128]{2,1,0:T(8,128)(2,1)S(1)} collective-permute-done((bf16[2,512,128]{2,1,0:T(8,128)(2,1)}, bf16[2,512,128]{2,1,0:T(8,128)(2,1)S(1)}, u32[]{:S(2)}, u32[]{:S(2)}) %collective-permute-start.7) | collective-permute-done | bytes 262176 | tf_op jit(solution)/shard_map/ppermute | solution.py:775
  69.8 1.2 collective-permute-done.8.refs_11_.refs_14_
  71.1 0.0 collective-permute-done.3.refs_6_.refs_8_
  71.1 0.7 copy-done.14
  71.8 0.2 copy-done.9
  72.0 0.6 copy-done.10
  72.6 0.2 copy-done.11
  72.7 0.8 copy-done.5
  73.5 8.9 %later_phase.2 = (bf16[2,128,1024]{2,1,0:T(8,128)(2,1)}, bf16[2,128,1024]{2,1,0:T(8,128)(2,1)}, bf16[2,128,1024]{2,1,0:T(8,128)(2,1)}, bf16[2,128,1024]{2,1,0:T(...) custom-call(f32[320,128]{1,0:T(8,128)} %get-tuple-element.48.refs_2_.refs_0, ...), custom_call_target="tpu_custom_call" | custom-call | tf_op jit(solution)/shard_map/later_phase/pallas_call | solution.py:668
  82.4 7.3 %all-to-all-start.2 = ((bf16[32,112,128]{2,1,0:T(8,128)(2,1)}), bf16[32,112,128]{2,1,0:T(8,128)(2,1)S(1)}, u32[]{:S(2)}, u32[]{:S(2)}) async-start(bf16[32,112,128]{2,1,0:T(8,128)(2,1)} %get-tuple-element.66), calls=%async_computation.2 | async-start | bytes 1835008 | tf_op jit(solution)/shard_map/all_to_all | solution.py:770
  89.7 1.5 collective-permute-start.9
  91.1 7.2 %collective-permute-start.10 = (bf16[2,128,1024]{2,1,0:T(8,128)(2,1)}, bf16[2,128,1024]{2,1,0:T(8,128)(2,1)}, u32[]{:S(2)}, u32[]{:S(2)}) collective-permute-start(bf16[2,128,1024]{2,1,0:T(8,128)(2,1)} %get-tuple-element.63), channel_id=1, source_target_pairs={{0,64},{32,96},{1,65},{33,97},{2,66},{34,98},{3,67},{35,99},{4,68}... | collective-permute-start | bytes 1572872 | tf_op jit(solution)/shard_map/ppermute | solution.py:775
  98.3 2.1 %collective-permute-start.11 = (bf16[2,128,1024]{2,1,0:T(8,128)(2,1)}, bf16[2,128,1024]{2,1,0:T(8,128)(2,1)}, u32[]{:S(2)}, u32[]{:S(2)}) collective-permute-start(bf16[2,128,1024]{2,1,0:T(8,128)(2,1)} %get-tuple-element.64), channel_id=1, source_target_pairs={{0,96},{96,64},{1,97},{97,65},{2,98},{98,66},{3,99},{99,67},{4,100... | collective-permute-start | bytes 1572872 | tf_op jit(solution)/shard_map/ppermute | solution.py:775
  100.4 0.6 broadcast_in_dim.7.refs_16_.refs_17_
  101.0 7.3 %other_phase.3 = (bf16[288,128]{1,0:T(8,128)(2,1)}, f32[16,128]{1,0:T(8,128)}) custom-call(f32[320,128]{1,0:T(8,128)} %get-tuple-element.48.refs_2_.refs_0_.refs_15_, f32[320,128]{1,0:T(8,128)} %copy-done.6, f32[320,128]{1,0:T(8,128)} %copy-done.7, f32[320,128]{1,0:T(8,128)} %copy-done.8, bf16[2,128,1024]{2,1,0:T(8,128)(2,1)} %get-tuple-element.53.refs_4_, ...), custom_call_target="tpu_custom_call" | custom-call | flops 6000000000 | bytes 4000000 | tf_op jit(solution)/shard_map/other_phase/pallas_call | solution.py:681
  108.3 0.9 copy-done.3
  109.2 1.2 chain.3
  110.4 7.6 %all-to-all-start.3 = ((bf16[32,64,128]{2,1,0:T(8,128)(2,1)}), bf16[32,64,128]{2,1,0:T(8,128)(2,1)S(1)}, u32[]{:S(2)}, u32[]{:S(2)}) async-start(bf16[32,64,128]{2,1,0:T(8,128)(2,1)} %chain.3), calls=%async_computation.3 | async-start | bytes 1048576 | tf_op jit(solution)/shard_map/all_to_all | solution.py:770
  118.0 7.3 %other_phase.4 = (bf16[288,128]{1,0:T(8,128)(2,1)}, bf16[288,128]{1,0:T(8,128)(2,1)}, bf16[288,128]{1,0:T(8,128)(2,1)}, bf16[288,128]{1,0:T(8,128)(2,1)}, f32[16,128]{1,0:T(8,128)}) custom-call(f32[320,128]{1,0:T(8,128)} %get-tuple-element.48.refs_2_.refs_0_.refs_15_, f32[320,128]{1,0:T(8,128)} %copy-done.6, f32[320,128]{1,0:T(8,128)} %copy-done.7, ...), custom_call_target="tpu_custom_call" | custom-call | flops 6000000000 | bytes 4000000 | tf_op jit(solution)/shard_map/other_phase/pallas_call | solution.py:681
  125.3 0.7 collective-permute-start.15
  126.0 3.6 %collective-permute-start.16 = (bf16[288,128]{1,0:T(8,128)(2,1)}, bf16[288,128]{1,0:T(8,128)(2,1)S(1)}, u32[]{:S(2)}, u32[]{:S(2)}) collective-permute-start(bf16[288,128]{1,0:T(8,128)(2,1)} %get-tuple-element.76), channel_id=1, source_target_pairs={{0,64},{32,96},{1,65},{33,97},{2,66},{34,98},{3,67},{35,99},{4,68}... | collective-permute-start | bytes 221192 | tf_op jit(solution)/shard_map/ppermute | solution.py:775
  129.6 1.3 collective-permute-start.17
  130.9 0.0 copy-start.4
  130.9 0.8 copy-done.4
  131.7 5.3 %later_phase.3 = (bf16[2,128,1024]{2,1,0:T(8,128)(2,1)}, bf16[2,128,1024]{2,1,0:T(8,128)(2,1)}, bf16[2,128,1024]{2,1,0:T(8,128)(2,1)}, bf16[2,128,1024]{2,1,0:T(...) custom-call(f32[320,128]{1,0:T(8,128)} %get-tuple-element.48.refs_2_.refs_0_.refs_15_, ...), custom_call_target="tpu_custom_call" | custom-call | tf_op jit(solution)/shard_map/later_phase/pallas_call | solution.py:668
  137.0 1.9 collective-permute-start.12
  139.0 1.3 collective-permute-start.13
  140.3 1.3 collective-permute-start.14
  141.7 0.6 copy-done.16
  142.2 0.0 copy-done.17
  142.3 11.3 %other_phase.5 = (bf16[288,128]{1,0:T(8,128)(2,1)}, bf16[288,128]{1,0:T(8,128)(2,1)}, bf16[288,128]{1,0:T(8,128)(2,1)}, bf16[288,128]{1,0:T(8,128)(2,1)}, f32[32,1,128]{2,1,0:T(1,128)}) custom-call(f32[320,128]{1,0:T(8,128)} %get-tuple-element.48.refs_2_.refs_0_.refs_15_, f32[320,128]{1,0:T(8,128)} %copy-done.6, f32[320,128]{1,0:T(8,128)} %copy-done.7, ...), custom_call_target="tpu_custom_call" | custom-call | flops 12000000000 | bytes 4000000 | tf_op jit(solution)/shard_map/other_phase/pallas_call | solution.py:681
  153.6 4.6 %collective-permute-start.18 = (bf16[288,128]{1,0:T(8,128)(2,1)}, bf16[288,128]{1,0:T(8,128)(2,1)S(1)}, u32[]{:S(2)}, u32[]{:S(2)}) collective-permute-start(bf16[288,128]{1,0:T(8,128)(2,1)} %get-tuple-element.81), channel_id=1, source_target_pairs={{0,32},{96,0},{1,33},{97,1},{2,34},{98,2},{3,35},{99,3},{4,36},{10... | collective-permute-start | bytes 221192 | tf_op jit(solution)/shard_map/ppermute | solution.py:775
  158.2 1.3 collective-permute-start.19
  159.5 8.6 %collective-permute-done.18.refs_5_.refs_1_ = bf16[288,128]{1,0:T(8,128)(2,1)S(1)} collective-permute-done((bf16[288,128]{1,0:T(8,128)(2,1)}, bf16[288,128]{1,0:T(8,128)(2,1)S(1)}, u32[]{:S(2)}, u32[]{:S(2)}) %collective-permute-start.18) | collective-permute-done | bytes 73760 | tf_op jit(solution)/shard_map/ppermute | solution.py:775
  168.1 1.3 collective-permute-start.20
  169.4 14.5 %all_to_all.30.refs_0_ = f32[32,1,128]{2,1,0:T(1,128)S(1)} all-to-all(f32[32,1,128]{2,1,0:T(1,128)} %get-tuple-element.87), channel_id=1, replica_groups=mesh['section'=4,'branch'=32] {'branch'}, dimensions={0} | all-to-all | bytes 32768 | tf_op jit(solution)/shard_map/all_to_all | solution.py:770
  183.9 0.6 rate_sum.1
  184.6 3.9 %all-to-all-start.5 = ((f32[4,1,128]{2,1,0:T(1,128)}), f32[4,1,128]{2,1,0:T(1,128)S(1)}, u32[]{:S(2)}, u32[]{:S(2)}) async-start(f32[4,1,128]{2,1,0:T(1,128)} %rate_sum.1), calls=%async_computation.5 | async-start | bytes 4096 | tf_op jit(solution)/shard_map/all_to_all | solution.py:770
  188.5 1.8 home_small.1
  190.3 3.3 %all-to-all-done.5.got_ref = f32[4,1,128]{2,1,0:T(1,128)S(1)} async-done(((f32[4,1,128]{2,1,0:T(1,128)}), f32[4,1,128]{2,1,0:T(1,128)S(1)}, u32[]{:S(2)}, u32[]{:S(2)}) %all-to-all-start.5) | async-done | bytes 2080 | tf_op jit(solution)/shard_map/all_to_all | solution.py:770
  193.6 0.7 rate_home.1
  194.3 0.8 copy-done.18
  195.0 2.9 %home_grad.1 = bf16[1,2,128,4096]{3,2,1,0:T(8,128)(2,1)} custom-call(bf16[2,128,1024]{2,1,0:T(8,128)(2,1)} %get-tuple-element.61.refs_0_, bf16[2,128,1024]{2,1,0:T(8,128)(2,1)} %collective-permute-done.9.refs_6_.refs_1_, bf16[2,128,1024]{2,1,0:T(8,128)(2,1)} %collective-permute-done.10.refs_7_.refs_2_, ...), custom_call_target="tpu_custom_call" | custom-call | flops 3000000000 | bytes 4000000 | tf_op jit(solution)/shard_map/home_grad/pallas_call | solution.py:735
  (42 shorter events, 0.1 us)
Async XLA Ops:
  3.2 10.6 %collective-permute-start = (f32[320,128]{1,0:T(8,128)}, f32[320,128]{1,0:T(8,128)S(1)}, u32[]{:S(2)}, u32[]{:S(2)}) collective-permute-start(f32[320,128]{1,0:T(8,128)} %get-tuple-element.49), channel_id=1, source_target_pairs={{0,32},{32,64},{64,96},{96,0},{1,33},{33,65},{65,97},{97,1},{2,34}... | collective-permute-start | bytes 491528 | tf_op jit(solution)/shard_map/ppermute | solution.py:775
  5.3 11.2 %collective-permute-start.1 = (f32[320,128]{1,0:T(8,128)}, f32[320,128]{1,0:T(8,128)S(1)}, u32[]{:S(2)}, u32[]{:S(2)}) collective-permute-start(f32[320,128]{1,0:T(8,128)} %get-tuple-element.50), channel_id=1, source_target_pairs={{0,64},{32,96},{64,0},{96,32},{1,65},{33,97},{65,1},{97,33},{2,66}... | collective-permute-start | bytes 491528 | tf_op jit(solution)/shard_map/ppermute | solution.py:775
  8.9 7.6 %collective-permute-start.2 = (f32[320,128]{1,0:T(8,128)}, f32[320,128]{1,0:T(8,128)S(1)}, u32[]{:S(2)}, u32[]{:S(2)}) collective-permute-start(f32[320,128]{1,0:T(8,128)} %get-tuple-element.51), channel_id=1, source_target_pairs={{0,96},{32,0},{64,32},{96,64},{1,97},{33,1},{65,33},{97,65},{2,98}... | collective-permute-start | bytes 491528 | tf_op jit(solution)/shard_map/ppermute | solution.py:775
  13.9 2.7 %copy-start.6 = (f32[320,128]{1,0:T(8,128)}, f32[320,128]{1,0:T(8,128)S(1)}, u32[]{:S(2)}) copy-start(f32[320,128]{1,0:T(8,128)S(1)} %collective-permute-done.refs_3_.refs_1_) | copy-start | bytes 491524
  16.5 0.7 copy-start.7
  16.5 0.7 copy-start.8
  24.1 23.3 %all-to-all-start = ((bf16[32,112,128]{2,1,0:T(8,128)(2,1)}), bf16[32,112,128]{2,1,0:T(8,128)(2,1)S(1)}, u32[]{:S(2)}, u32[]{:S(2)}) async-start(bf16[32,112,128]{2,1,0:T(8,128)(2,1)} %get-tuple-element.54), calls=%async_computation | async-start | bytes 1835008 | tf_op jit(solution)/shard_map/all_to_all | solution.py:770
  31.5 23.2 %collective-permute-start.6 = (bf16[2,512,128]{2,1,0:T(8,128)(2,1)}, bf16[2,512,128]{2,1,0:T(8,128)(2,1)S(1)}, u32[]{:S(2)}, u32[]{:S(2)}) collective-permute-start(bf16[2,512,128]{2,1,0:T(8,128)(2,1)} %get-tuple-element.58), channel_id=1, source_target_pairs={{0,32},{32,64},{64,96},{96,0},{1,33},{33,65},{65,97},{97,1},{2,34}... | collective-permute-start | bytes 786440 | tf_op jit(solution)/shard_map/ppermute | solution.py:775
  32.7 38.4 %collective-permute-start.3 = (bf16[2,128,1024]{2,1,0:T(8,128)(2,1)}, bf16[2,128,1024]{2,1,0:T(8,128)(2,1)S(1)}, u32[]{:S(2)}, u32[]{:S(2)}) collective-permute-start(bf16[2,128,1024]{2,1,0:T(8,128)(2,1)} %get-tuple-element.55), channel_id=1, source_target_pairs={{0,32},{32,64},{64,96},{96,0},{1,33},{33,65},{65,97},{97,1},{2,34}... | collective-permute-start | bytes 1572872 | tf_op jit(solution)/shard_map/ppermute | solution.py:775
  33.6 37.4 %collective-permute-start.4 = (bf16[2,128,1024]{2,1,0:T(8,128)(2,1)}, bf16[2,128,1024]{2,1,0:T(8,128)(2,1)S(1)}, u32[]{:S(2)}, u32[]{:S(2)}) collective-permute-start(bf16[2,128,1024]{2,1,0:T(8,128)(2,1)} %get-tuple-element.56), channel_id=1, source_target_pairs={{0,64},{32,96},{64,0},{96,32},{1,65},{33,97},{65,1},{97,33},{2,66}... | collective-permute-start | bytes 1572872 | tf_op jit(solution)/shard_map/ppermute | solution.py:775
  36.2 35.6 %collective-permute-start.5 = (bf16[2,128,1024]{2,1,0:T(8,128)(2,1)}, bf16[2,128,1024]{2,1,0:T(8,128)(2,1)S(1)}, u32[]{:S(2)}, u32[]{:S(2)}) collective-permute-start(bf16[2,128,1024]{2,1,0:T(8,128)(2,1)} %get-tuple-element.57), channel_id=1, source_target_pairs={{0,96},{32,0},{64,32},{96,64},{1,97},{33,1},{65,33},{97,65},{2,98}... | collective-permute-start | bytes 1572872 | tf_op jit(solution)/shard_map/ppermute | solution.py:775
  48.5 23.3 %all-to-all-start.1 = ((bf16[32,64,128]{2,1,0:T(8,128)(2,1)}), bf16[32,64,128]{2,1,0:T(8,128)(2,1)S(1)}, u32[]{:S(2)}, u32[]{:S(2)}) async-start(bf16[32,64,128]{2,1,0:T(8,128)(2,1)} %chain.2), calls=%async_computation.1 | async-start | bytes 1048576 | tf_op jit(solution)/shard_map/all_to_all | solution.py:770
  52.4 17.4 %collective-permute-start.7 = (bf16[2,512,128]{2,1,0:T(8,128)(2,1)}, bf16[2,512,128]{2,1,0:T(8,128)(2,1)S(1)}, u32[]{:S(2)}, u32[]{:S(2)}) collective-permute-start(bf16[2,512,128]{2,1,0:T(8,128)(2,1)} %get-tuple-element.59), channel_id=1, source_target_pairs={{0,64},{32,96},{64,0},{96,32},{1,65},{33,97},{65,1},{97,33},{2,66}... | collective-permute-start | bytes 786440 | tf_op jit(solution)/shard_map/ppermute | solution.py:775
  54.7 18.1 %copy-start.12 = (bf16[2,512,128]{2,1,0:T(8,128)(2,1)}, bf16[2,512,128]{2,1,0:T(8,128)(2,1)S(1)}, u32[]{:S(2)}) copy-start(bf16[2,512,128]{2,1,0:T(8,128)(2,1)S(1)} %collective-permute-done.6.refs_9_.refs_12_) | copy-start | bytes 786436
  54.7 16.4 %collective-permute-start.8 = (bf16[2,512,128]{2,1,0:T(8,128)(2,1)}, bf16[2,512,128]{2,1,0:T(8,128)(2,1)S(1)}, u32[]{:S(2)}, u32[]{:S(2)}) collective-permute-start(bf16[2,512,128]{2,1,0:T(8,128)(2,1)} %get-tuple-element.60), channel_id=1, source_target_pairs={{0,96},{32,0},{64,32},{96,64},{1,97},{33,1},{65,33},{97,65},{2,98}... | collective-permute-start | bytes 786440 | tf_op jit(solution)/shard_map/ppermute | solution.py:775
  69.8 1.2 copy-start.13
  71.1 0.7 copy-start.14
  71.1 0.9 copy-start.9
  71.8 0.8 copy-start.10
  71.8 1.0 copy-start.11
  72.7 0.8 copy-start.5
  82.4 25.9 %all-to-all-start.2 = ((bf16[32,112,128]{2,1,0:T(8,128)(2,1)}), bf16[32,112,128]{2,1,0:T(8,128)(2,1)S(1)}, u32[]{:S(2)}, u32[]{:S(2)}) async-start(bf16[32,112,128]{2,1,0:T(8,128)(2,1)} %get-tuple-element.66), calls=%async_computation.2 | async-start | bytes 1835008 | tf_op jit(solution)/shard_map/all_to_all | solution.py:770
  89.7 39.9 %collective-permute-start.9 = (bf16[2,128,1024]{2,1,0:T(8,128)(2,1)}, bf16[2,128,1024]{2,1,0:T(8,128)(2,1)}, u32[]{:S(2)}, u32[]{:S(2)}) collective-permute-start(bf16[2,128,1024]{2,1,0:T(8,128)(2,1)} %get-tuple-element.62), channel_id=1, source_target_pairs={{32,64},{64,96},{33,65},{65,97},{34,66},{66,98},{35,67},{67,99},{3... | collective-permute-start | bytes 1572872 | tf_op jit(solution)/shard_map/ppermute | solution.py:775
  91.1 39.8 %collective-permute-start.10 = (bf16[2,128,1024]{2,1,0:T(8,128)(2,1)}, bf16[2,128,1024]{2,1,0:T(8,128)(2,1)}, u32[]{:S(2)}, u32[]{:S(2)}) collective-permute-start(bf16[2,128,1024]{2,1,0:T(8,128)(2,1)} %get-tuple-element.63), channel_id=1, source_target_pairs={{0,64},{32,96},{1,65},{33,97},{2,66},{34,98},{3,67},{35,99},{4,68}... | collective-permute-start | bytes 1572872 | tf_op jit(solution)/shard_map/ppermute | solution.py:775
  98.3 32.6 %collective-permute-start.11 = (bf16[2,128,1024]{2,1,0:T(8,128)(2,1)}, bf16[2,128,1024]{2,1,0:T(8,128)(2,1)}, u32[]{:S(2)}, u32[]{:S(2)}) collective-permute-start(bf16[2,128,1024]{2,1,0:T(8,128)(2,1)} %get-tuple-element.64), channel_id=1, source_target_pairs={{0,96},{96,64},{1,97},{97,65},{2,98},{98,66},{3,99},{99,67},{4,100... | collective-permute-start | bytes 1572872 | tf_op jit(solution)/shard_map/ppermute | solution.py:775
  108.3 0.9 copy-start.3
  110.4 20.6 %all-to-all-start.3 = ((bf16[32,64,128]{2,1,0:T(8,128)(2,1)}), bf16[32,64,128]{2,1,0:T(8,128)(2,1)S(1)}, u32[]{:S(2)}, u32[]{:S(2)}) async-start(bf16[32,64,128]{2,1,0:T(8,128)(2,1)} %chain.3), calls=%async_computation.3 | async-start | bytes 1048576 | tf_op jit(solution)/shard_map/all_to_all | solution.py:770
  125.3 15.0 %collective-permute-start.15 = (bf16[288,128]{1,0:T(8,128)(2,1)}, bf16[288,128]{1,0:T(8,128)(2,1)S(1)}, u32[]{:S(2)}, u32[]{:S(2)}) collective-permute-start(bf16[288,128]{1,0:T(8,128)(2,1)} %get-tuple-element.75), channel_id=1, source_target_pairs={{32,64},{64,96},{33,65},{65,97},{34,66},{66,98},{35,67},{67,99},{3... | collective-permute-start | bytes 221192 | tf_op jit(solution)/shard_map/ppermute | solution.py:775
  126.0 15.6 %collective-permute-start.16 = (bf16[288,128]{1,0:T(8,128)(2,1)}, bf16[288,128]{1,0:T(8,128)(2,1)S(1)}, u32[]{:S(2)}, u32[]{:S(2)}) collective-permute-start(bf16[288,128]{1,0:T(8,128)(2,1)} %get-tuple-element.76), channel_id=1, source_target_pairs={{0,64},{32,96},{1,65},{33,97},{2,66},{34,98},{3,67},{35,99},{4,68}... | collective-permute-start | bytes 221192 | tf_op jit(solution)/shard_map/ppermute | solution.py:775
  129.6 12.0 %collective-permute-start.17 = (bf16[288,128]{1,0:T(8,128)(2,1)}, bf16[288,128]{1,0:T(8,128)(2,1)S(1)}, u32[]{:S(2)}, u32[]{:S(2)}) collective-permute-start(bf16[288,128]{1,0:T(8,128)(2,1)} %get-tuple-element.77), channel_id=1, source_target_pairs={{0,96},{96,64},{1,97},{97,65},{2,98},{98,66},{3,99},{99,67},{4,100... | collective-permute-start | bytes 221192 | tf_op jit(solution)/shard_map/ppermute | solution.py:775
  130.9 0.8 copy-start.4
  137.0 57.2 %collective-permute-start.12 = (bf16[2,128,1024]{2,1,0:T(8,128)(2,1)}, bf16[2,128,1024]{2,1,0:T(8,128)(2,1)}, u32[]{:S(2)}, u32[]{:S(2)}) collective-permute-start(bf16[2,128,1024]{2,1,0:T(8,128)(2,1)} %get-tuple-element.70), channel_id=1, source_target_pairs={{0,32},{96,0},{1,33},{97,1},{2,34},{98,2},{3,35},{99,3},{4,36},{10... | collective-permute-start | bytes 1572872 | tf_op jit(solution)/shard_map/ppermute | solution.py:775
  139.0 55.3 %collective-permute-start.13 = (bf16[2,128,1024]{2,1,0:T(8,128)(2,1)}, bf16[2,128,1024]{2,1,0:T(8,128)(2,1)}, u32[]{:S(2)}, u32[]{:S(2)}) collective-permute-start(bf16[2,128,1024]{2,1,0:T(8,128)(2,1)} %get-tuple-element.71), channel_id=1, source_target_pairs={{64,0},{96,32},{65,1},{97,33},{66,2},{98,34},{67,3},{99,35},{68,4}... | collective-permute-start | bytes 1572872 | tf_op jit(solution)/shard_map/ppermute | solution.py:775
  140.3 1.4 copy-start.15
  140.3 53.9 %collective-permute-start.14 = (bf16[2,128,1024]{2,1,0:T(8,128)(2,1)}, bf16[2,128,1024]{2,1,0:T(8,128)(2,1)S(1)}, u32[]{:S(2)}, u32[]{:S(2)}) collective-permute-start(bf16[2,128,1024]{2,1,0:T(8,128)(2,1)} %get-tuple-element.72), channel_id=1, source_target_pairs={{32,0},{64,32},{33,1},{65,33},{34,2},{66,34},{35,3},{67,35},{36,4}... | collective-permute-start | bytes 1572872 | tf_op jit(solution)/shard_map/ppermute | solution.py:775
  141.6 0.6 copy-start.16
  141.6 0.6 copy-start.17
  153.6 14.5 %collective-permute-start.18 = (bf16[288,128]{1,0:T(8,128)(2,1)}, bf16[288,128]{1,0:T(8,128)(2,1)S(1)}, u32[]{:S(2)}, u32[]{:S(2)}) collective-permute-start(bf16[288,128]{1,0:T(8,128)(2,1)} %get-tuple-element.81), channel_id=1, source_target_pairs={{0,32},{96,0},{1,33},{97,1},{2,34},{98,2},{3,35},{99,3},{4,36},{10... | collective-permute-start | bytes 221192 | tf_op jit(solution)/shard_map/ppermute | solution.py:775
  158.2 25.7 %collective-permute-start.19 = (bf16[288,128]{1,0:T(8,128)(2,1)}, bf16[288,128]{1,0:T(8,128)(2,1)S(1)}, u32[]{:S(2)}, u32[]{:S(2)}) collective-permute-start(bf16[288,128]{1,0:T(8,128)(2,1)} %get-tuple-element.82), channel_id=1, source_target_pairs={{64,0},{96,32},{65,1},{97,33},{66,2},{98,34},{67,3},{99,35},{68,4}... | collective-permute-start | bytes 221192 | tf_op jit(solution)/shard_map/ppermute | solution.py:775
  168.1 20.4 %copy-start = (bf16[288,128]{1,0:T(8,128)(2,1)}, bf16[288,128]{1,0:T(8,128)(2,1)S(1)}, u32[]{:S(2)}) copy-start(bf16[288,128]{1,0:T(8,128)(2,1)S(1)} %collective-permute-done.18.refs_5_.refs_1_) | copy-start | bytes 221188
  168.1 15.8 %collective-permute-start.20 = (bf16[288,128]{1,0:T(8,128)(2,1)}, bf16[288,128]{1,0:T(8,128)(2,1)S(1)}, u32[]{:S(2)}, u32[]{:S(2)}) collective-permute-start(bf16[288,128]{1,0:T(8,128)(2,1)} %get-tuple-element.83), channel_id=1, source_target_pairs={{32,0},{64,32},{33,1},{65,33},{34,2},{66,34},{35,3},{67,35},{36,4}... | collective-permute-start | bytes 221192 | tf_op jit(solution)/shard_map/ppermute | solution.py:775
  183.9 4.5 %copy-start.1 = (bf16[288,128]{1,0:T(8,128)(2,1)}, bf16[288,128]{1,0:T(8,128)(2,1)S(1)}, u32[]{:S(2)}) copy-start(bf16[288,128]{1,0:T(8,128)(2,1)S(1)} %collective-permute-done.19.refs_6_.refs_2_) | copy-start | bytes 221188
  183.9 4.5 %copy-start.2 = (bf16[288,128]{1,0:T(8,128)(2,1)}, bf16[288,128]{1,0:T(8,128)(2,1)S(1)}, u32[]{:S(2)}) copy-start(bf16[288,128]{1,0:T(8,128)(2,1)S(1)} %collective-permute-done.20.refs_7_.refs_3_) | copy-start | bytes 221188
  184.6 9.0 %all-to-all-start.5 = ((f32[4,1,128]{2,1,0:T(1,128)}), f32[4,1,128]{2,1,0:T(1,128)S(1)}, u32[]{:S(2)}, u32[]{:S(2)}) async-start(f32[4,1,128]{2,1,0:T(1,128)} %rate_sum.1), calls=%async_computation.5 | async-start | bytes 4096 | tf_op jit(solution)/shard_map/all_to_all | solution.py:770
  194.2 0.8 copy-start.18

commit v3 on v2

v3 whole, which is shorter than its diff:
```python
import functools
import math

import jax
import jax.numpy as jnp
from jax import lax
from jax.experimental import pallas as pl
from jax.experimental.pallas import tpu as pltpu
from jax.sharding import PartitionSpec as P

F32 = jnp.float32
BF16 = jnp.bfloat16

SECTIONS = 4
FAMILIES = 2
ROWS = 128
STATE = 64
HEADDIM = 64
GROUP = 16
COLS = GROUP * HEADDIM
LANES = 128
CHUNK = 256
PER_CHUNK = CHUNK // HEADDIM
BRANCHES = 32
SEND_ROWS = 112
PACK_ROWS = FAMILIES * ROWS + 4 * GROUP
GRAD_ROWS = FAMILIES * (ROWS + GROUP)
HOME_ROWS = GRAD_ROWS + 16
SAVED_ROWS = COLS + COLS // 2
VMEM_LIMIT = 63 * 1024 * 1024

NN = (((1,), (0,)), ((), ()))
NT = (((1,), (1,)), ((), ()))
TN = (((0,), (0,)), ((), ()))


def dot(a, b, dims):
    return lax.dot_general(a, b, dims, preferred_element_type=F32)


def split(a):
    high = a.astype(BF16)
    return high, (a - high.astype(F32)).astype(BF16)


def dot3(a, b, dims):
    return dot(a[0], b[0], dims) + dot(a[1], b[0], dims) + dot(a[0], b[1], dims)


def dot2(a, b, dims):
    return dot(a[0], b, dims) + dot(a[1], b, dims)


def lane_ids(shape):
    return lax.broadcasted_iota(jnp.int32, shape, len(shape) - 1)


def half(rolled, plain, side):
    lanes = lane_ids(plain.shape)
    if side == 0:
        return jnp.where(lanes < STATE, plain, 0.0)
    return jnp.where(lanes >= STATE, rolled, 0.0)


def by_head(value, chunk):
    first = chunk * PER_CHUNK
    return jnp.concatenate(
        [jnp.broadcast_to(value[first + at : first + at + 1, :], (HEADDIM, LANES)) for at in range(PER_CHUNK)], axis=0
    )


def head_sums(value):
    return jnp.sum(value.reshape(PER_CHUNK, HEADDIM, LANES), axis=1)


def fetch_packs(layers, pack_refs, pack_buf, sems):
    mine = lax.axis_index("section")
    for at in layers:
        away = lax.rem(mine - at + SECTIONS, SECTIONS)
        for k in range(SECTIONS):

            @pl.when(away == k)
            def _():
                pltpu.make_async_copy(pack_refs[k], pack_buf.at[at], sems.at[at]).start()


def wait_packs(layers, pack_refs, pack_buf, sems):
    for at in layers:
        pltpu.make_async_copy(pack_refs[0], pack_buf.at[at], sems.at[at]).wait()


class Layer:
    def __init__(self, pack_ref, layer, family):
        base = FAMILIES * ROWS
        both = pack_ref[layer, family * ROWS : (family + 1) * ROWS, :]
        turned = pltpu.roll(both, STATE, 1)
        self.b = (half(both, both, 0), half(turned, turned, 1))
        self.c = (half(turned, turned, 0), half(both, both, 1))
        self.step = pack_ref[layer, base + family * GROUP : base + (family + 1) * GROUP, :]
        self.decay = pack_ref[layer, base + 2 * GROUP : base + 3 * GROUP, :]
        gain = pack_ref[layer, base + 3 * GROUP : base + 4 * GROUP, :]
        row = lax.broadcasted_iota(jnp.int32, (ROWS, ROWS), 0)
        col = lax.broadcasted_iota(jnp.int32, (ROWS, ROWS), 1)
        self.row, self.col = row, col
        upper = jnp.where(row <= col, 1.0, 0.0).astype(BF16)
        drop = -self.decay * self.step
        first = drop.astype(BF16)
        rest = drop - first.astype(F32)
        second = rest.astype(BF16)
        third = (rest - second.astype(F32)).astype(BF16)
        logs = dot(first, upper, NN) + dot(second, upper, NN) + dot(third, upper, NN)
        carried = jnp.exp(logs)
        scale = self.step * jnp.exp(-logs)
        total = jnp.sum(jnp.where(lane_ids(carried.shape) == ROWS - 1, carried, 0.0), axis=1, keepdims=True)
        self.total = jnp.broadcast_to(total, (GROUP, LANES))
        self.carried, self.scale, self.gain = carried, scale, gain
        read = dot3(split(self.c[0]), split(self.b[0]), NT)
        self.read = jnp.where(row >= col, read, 0.0)


def phase_a(family, upper_at, high, low, send_ref):
    c_pair = split(jnp.concatenate([high.c[0], low.c[1]], axis=0))
    c_both = split(low.c[0] + low.c[1])
    b_turned = jnp.transpose(high.b[0])[0:STATE]
    b_tile = jnp.concatenate([b_turned] * PER_CHUNK, axis=0)
    read = high.read.astype(BF16)
    mixed = low.carried * high.scale
    lanes = lane_ids((STATE // 2, LANES))
    for chunk in range(COLS // CHUNK):
        rows = slice(chunk * CHUNK, (chunk + 1) * CHUNK)
        upstream = upper_at(rows)
        hat2 = split(by_head(high.carried, chunk) * upstream)
        pulled = dot(hat2[0], read, NN)
        low_up = by_head(high.gain, chunk) * upstream + by_head(high.scale, chunk) * pulled
        low_hat2 = split(by_head(low.carried, chunk) * low_up)
        both = tuple(jnp.concatenate([a, b], axis=1) for a, b in zip(hat2, low_hat2))
        begin = dot3(both, c_pair, NN).astype(BF16)
        move = dot3(split(by_head(mixed, chunk) * b_tile), c_both, NN)
        for inner in range(PER_CHUNK):
            head = family * GROUP + chunk * PER_CHUNK + inner
            top = inner * HEADDIM
            send_ref[head, 0:HEADDIM, :] = begin[top : top + HEADDIM, :]
            first = move[top : top + 32, :]
            second = move[top + 32 : top + 64, :]
            send_ref[head, HEADDIM : HEADDIM + 32, :] = jnp.where(lanes < STATE, first, second).astype(BF16)
    totals = jnp.where(lane_ids((GROUP, LANES)) < STATE, high.total, low.total)
    total_high = totals.astype(BF16).astype(F32)
    total_low = totals - total_high
    place = lax.broadcasted_iota(jnp.int32, (16, LANES), 0)
    for inner in range(GROUP):
        one = jnp.broadcast_to(total_high[inner : inner + 1, :], (16, LANES))
        two = jnp.broadcast_to(total_low[inner : inner + 1, :], (16, LANES))
        block = jnp.where(place == 0, one, jnp.where(place == 1, two, 0.0))
        send_ref[family * GROUP + inner, 96:112, :] = block.astype(BF16)


def phase_b(family, side, layer, upper_at, end_ref, put_grad):
    b2 = split(jnp.transpose(layer.b[side]))
    weights = jnp.concatenate([layer.read.astype(BF16), b2[0]], axis=0)
    for chunk in range(COLS // CHUNK):
        rows = slice(chunk * CHUNK, (chunk + 1) * CHUNK)
        upstream = upper_at(rows)
        first = family * GROUP + chunk * PER_CHUNK
        ends = end_ref[first : first + PER_CHUNK].reshape(CHUNK, LANES)
        hat = (by_head(layer.carried, chunk) * upstream).astype(BF16)
        pulled = dot(jnp.concatenate([hat, ends], axis=1), weights, NN) + dot(ends, b2[1], NN)
        grad = by_head(layer.gain, chunk) * upstream + by_head(layer.scale, chunk) * pulled
        put_grad(rows, grad.astype(BF16))


def phase_c(family, side, layer, upper_at, saved_ref, end_ref):
    b_one, c_one = layer.b[side].astype(BF16), layer.c[side].astype(BF16)
    b_turned = jnp.transpose(layer.b[side]).astype(BF16)
    read = layer.read.astype(BF16)
    weights = jnp.concatenate([jnp.transpose(layer.read), jnp.transpose(layer.c[side])], axis=0).astype(BF16)
    left = jnp.zeros((ROWS, ROWS + LANES), F32)
    grad_in = jnp.zeros((ROWS, LANES), F32)
    flow, worth, ending, skips = [], [], [], []
    lanes = lane_ids((CHUNK, LANES))
    for chunk in range(COLS // CHUNK):
        rows = slice(chunk * CHUNK, (chunk + 1) * CHUNK)
        upstream = upper_at(rows)
        x = saved_ref[family, rows, :].astype(F32)
        hat = by_head(layer.carried, chunk) * upstream
        hat_one = hat.astype(BF16)
        x_hat = by_head(layer.scale, chunk) * x
        x_one = x_hat.astype(BF16)
        first = family * GROUP + chunk * PER_CHUNK
        ends = end_ref[first : first + PER_CHUNK].reshape(CHUNK, LANES)
        top = COLS + (chunk % 2) * CHUNK
        packed = saved_ref[family, top : top + CHUNK, :].astype(F32)
        if (chunk < 2) != (side == 0):
            packed = pltpu.roll(packed, STATE, 1)
        saved = jnp.where((lanes < STATE) == (side == 0), packed, 0.0)
        x_saved = jnp.concatenate([x_one, saved.astype(BF16)], axis=1)
        end_in = dot(ends, b_turned, NN)
        pulled = dot(hat_one, read, NN) + end_in
        forward = dot(x_saved, weights, NN)
        left = left + dot(hat_one, x_saved, TN)
        grad_in = grad_in + dot(x_one, ends, TN)
        x_pulled = x_hat * pulled
        worth.append(head_sums(x_pulled))
        flow.append(head_sums(hat * forward - x_pulled))
        ending.append(head_sums(x_hat * end_in + ends.astype(F32) * saved))
        skips.append(head_sums(x * upstream))
    flow, worth, ending, skips = (jnp.concatenate(part, axis=0) for part in (flow, worth, ending, skips))
    pairs, grad_out = left[:, 0:ROWS], left[:, ROWS:]
    pairs = jnp.where(layer.row >= layer.col, pairs, 0.0).astype(BF16)
    grad_out = grad_out + dot(pairs, b_one, NN)
    grad_in = grad_in + dot(pairs, c_one, TN)
    lanes = lane_ids((ROWS, LANES))
    if side == 0:
        grads = jnp.where(lanes < STATE, grad_in, pltpu.roll(grad_out, STATE, 1))
    else:
        grads = jnp.where(lanes < STATE, pltpu.roll(grad_in, STATE, 1), grad_out)
    later = jnp.where(layer.row >= layer.col, 1.0, 0.0).astype(BF16)
    rate = dot2(split(flow), later, NN) + jnp.sum(ending, axis=1, keepdims=True)
    grad_step = worth / layer.step - layer.decay * rate
    decay_part = jnp.sum(-layer.step * rate, axis=1, keepdims=True)
    skip_part = jnp.sum(skips, axis=1, keepdims=True)
    place = lane_ids((GROUP, LANES))
    small = jnp.where(place == 0, decay_part, jnp.where(place == 1, skip_part, 0.0))
    return grads, grad_step, small


def first_kernel(high_at, after, *refs):
    lengths_ref, cot_ref = refs[:2]
    pack_refs = refs[2:6]
    send_ref, up_ref, cot_buf, up_buf, send_buf, pack_ref, sems, pack_sem = refs[6 + after :]
    layers = (high_at, high_at - 1)
    fetch_packs(layers, pack_refs, pack_ref, pack_sem)
    mine = lax.axis_index("section")
    branch = lax.axis_index("branch")
    at = pl.multiple_of(mine * COLS, COLS)
    copy = pltpu.make_async_copy(cot_ref.at[:, :, pl.ds(at, COLS)], cot_buf, sems.at[3])
    copy.start()
    wait_packs(layers, pack_refs, pack_ref, pack_sem)
    copy.wait()
    copies = []
    for family in range(FAMILIES):
        slot = jnp.clip(branch - BRANCHES // 2, 0, BRANCHES // 2 - 1)
        limit = jnp.where(branch >= BRANCHES // 2, lengths_ref[family, slot], ROWS)

        def upper_at(rows):
            at = lane_ids((CHUNK, ROWS))
            value = jnp.where(at < limit, jnp.transpose(cot_buf[family, :, rows].astype(F32)), 0.0)
            up_buf[family, rows, :] = value.astype(BF16)
            return value

        high = Layer(pack_ref, high_at, family)
        low = Layer(pack_ref, high_at - 1, family)
        phase_a(family, upper_at, high, low, send_buf)
        heads = pl.ds(family * GROUP, GROUP)
        copies.append(pltpu.make_async_copy(send_buf.at[heads], send_ref.at[heads], sems.at[family]))
        copies[-1].start()
    copies.append(pltpu.make_async_copy(up_buf, up_ref, sems.at[2]))
    copies[-1].start()
    for copy in copies:
        copy.wait()


def later_kernel(high_at, goes_on, after, *refs):
    pack_refs = refs[:4]
    up_ref, end_ref = refs[4:6]
    refs = refs[6 + after :]
    grad_refs, keep_refs = refs[0:4], refs[4:6]
    rest = refs[6:]
    if goes_on:
        send_ref, grad_buf, up_buf, end_buf, pack_ref, grad_sem, keep_sem, in_sem, pack_sem, send_buf, send_sem = rest
    else:
        grad_buf, up_buf, end_buf, pack_ref, grad_sem, keep_sem, in_sem, pack_sem = rest
    layers = range(high_at, high_at - (4 if goes_on else 2), -1)
    fetch_packs(layers[:2], pack_refs, pack_ref, pack_sem)
    ins = [
        pltpu.make_async_copy(up_ref, up_buf, in_sem.at[0]),
        pltpu.make_async_copy(end_ref, end_buf, in_sem.at[1]),
    ]
    for copy in ins:
        copy.start()
    fetch_packs(layers[2:], pack_refs, pack_ref, pack_sem)
    mine = lax.axis_index("section")
    wait_packs(layers[:2], pack_refs, pack_ref, pack_sem)
    for copy in ins:
        copy.wait()
    for side in range(2):
        layer_at = high_at - side
        for family in range(FAMILIES):

            def upper_at(rows):
                if side == 0:
                    return up_buf[family, rows, :].astype(F32)
                return grad_buf[0, family, rows, :].astype(F32)

            def put_grad(rows, value):
                grad_buf[side, family, rows, :] = value

            layer = Layer(pack_ref, layer_at, family)
            phase_b(family, side, layer, upper_at, end_buf, put_grad)
        ahead = lax.rem(layer_at - mine + SECTIONS, SECTIONS)
        for k in range(SECTIONS):

            @pl.when(ahead == k)
            def _():
                pltpu.make_async_copy(grad_buf.at[side], grad_refs[k], grad_sem.at[side]).start()

    copies = [pltpu.make_async_copy(grad_buf.at[side], keep_refs[side], keep_sem.at[side]) for side in range(2)]
    for copy in copies:
        copy.start()
    if goes_on:
        wait_packs(layers[2:], pack_refs, pack_ref, pack_sem)
        for family in range(FAMILIES):

            def upper_at(rows):
                return grad_buf[1, family, rows, :].astype(F32)

            high = Layer(pack_ref, high_at - 2, family)
            low = Layer(pack_ref, high_at - 3, family)
            phase_a(family, upper_at, high, low, send_buf)
            heads = pl.ds(family * GROUP, GROUP)
            copies.append(pltpu.make_async_copy(send_buf.at[heads], send_ref.at[heads], send_sem.at[family]))
            copies[-1].start()
    for copy in copies:
        copy.wait()
    for side in range(2):
        pltpu.make_async_copy(grad_buf.at[side], grad_refs[0], grad_sem.at[side]).wait()


def other_kernel(high_at, sides, after, *refs):
    pack_refs, up_refs, end_ref, saved_refs = refs[:4], refs[4:6], refs[6], refs[7:11]
    refs = refs[11:]
    final = len(sides) == 2
    if final:
        held_refs, small_refs, refs = refs[0:2], refs[2:4], refs[4:]
    refs = refs[after:]
    part_refs, refs = (refs[:4], refs[4:]) if final else (refs[:1], refs[1:])
    rate_ref, saved_buf, up_buf, end_buf, part_buf, pack_ref = refs[:6]
    saved_sem, up_sem, part_sem, end_sem, pack_sem = refs[6:]
    mine = lax.axis_index("section")
    layers = [high_at - side for side in sides]
    fetch_packs(layers, pack_refs, pack_ref, pack_sem)
    ends = pltpu.make_async_copy(end_ref, end_buf, end_sem.at[0])
    ends.start()
    for side in sides:
        away = lax.rem(mine - (high_at - side) + SECTIONS, SECTIONS)
        pltpu.make_async_copy(up_refs[side], up_buf.at[side], up_sem.at[side]).start()
        for k in range(SECTIONS):

            @pl.when(away == k)
            def _():
                pltpu.make_async_copy(saved_refs[k], saved_buf.at[side], saved_sem.at[side]).start()

    def hand_on(source, layer_at):
        to = [part.at[pl.ds(0, GRAD_ROWS)] for part in part_refs] if final else part_refs
        copies = [pltpu.make_async_copy(source, part, part_sem.at[layer_at]) for part in to]
        if final:
            ahead = lax.rem(layer_at - mine + SECTIONS, SECTIONS)
            for k in range(SECTIONS):

                @pl.when(ahead == k)
                def _():
                    copies[k].start()
        else:
            copies[0].start()
        moved.append(copies[0])

    moved = []
    if final:
        for side in range(2):
            hand_on(held_refs[side], high_at + 2 - side)
    wait_packs(layers, pack_refs, pack_ref, pack_sem)
    ends.wait()
    smalls_of = []
    for side in sides:
        pltpu.make_async_copy(up_refs[side], up_buf.at[side], up_sem.at[side]).wait()
        pltpu.make_async_copy(saved_refs[0], saved_buf.at[side], saved_sem.at[side]).wait()
        smalls = jnp.zeros((GROUP, LANES), F32)
        for family in range(FAMILIES):

            def upper_at(rows):
                return up_buf[side, family, rows, :].astype(F32)

            layer = Layer(pack_ref, high_at - side, family)
            grads, grad_step, small = phase_c(family, side, layer, upper_at, saved_buf.at[side], end_buf)
            part_buf[side, family * ROWS : (family + 1) * ROWS, :] = grads.astype(BF16)
            below = FAMILIES * ROWS + family * GROUP
            part_buf[side, below : below + GROUP, :] = grad_step.astype(BF16)
            smalls = smalls + small
        hand_on(part_buf.at[side], high_at - side)
        smalls_of.append(smalls)
    if final:
        blocks = smalls_of[::-1] + [small_refs[1][...], small_refs[0][...]]
        turned = jnp.transpose(jnp.concatenate(blocks + [jnp.zeros((STATE, LANES), F32)], axis=0))
        row = turned[0:1] + pltpu.roll(turned[1:2], STATE, 1)
        rate_ref[...] = jnp.broadcast_to(row[None], (BRANCHES, 1, LANES))
    else:
        rate_ref[...] = smalls_of[0]
    for copy in moved:
        copy.wait()


def chain_kernel(*refs):
    got_ref, end_ref = refs[0], refs[-1]
    lanes = lane_ids((STATE // 2, LANES))
    prompt = BRANCHES // 2
    fork = jnp.zeros((HEADDIM, LANES), F32)
    for at in range(prompt, BRANCHES):
        fork = fork + got_ref[at, 0:HEADDIM, :].astype(F32)
    plain, extra = fork, jnp.zeros((HEADDIM, LANES), F32)
    blank = jnp.zeros((STATE, LANES), F32)
    for at in range(prompt - 1, -1, -1):
        tail = got_ref[at, 96:112, :].astype(F32)
        total = tail[0:1, :] + tail[1:2, :]
        plain = total * plain
        extra = total * extra
        end_ref[at, :, :] = (plain + extra).astype(BF16)
        if at == 0:
            break
        packed = got_ref[at, HEADDIM : HEADDIM + 32, :].astype(F32)
        turned = pltpu.roll(packed, STATE, 1)
        move = jnp.concatenate(
            [jnp.where(lanes >= STATE, turned, 0.0), jnp.where(lanes >= STATE, packed, 0.0), blank], axis=0
        ).astype(BF16)
        extra = extra + dot2(split(plain), move, NN)
        plain = plain + got_ref[at, 0:HEADDIM, :].astype(F32)
    for at in range(prompt, BRANCHES):
        end_ref[at, :, :] = jnp.zeros((HEADDIM, LANES), BF16)


def pack_kernel(*refs):
    sources, decay_ref, gain_ref = refs[0:3], refs[3], refs[4]
    pack_refs = refs[5:9]
    in_ref, out_ref, step_ref, both_ref, rate_ref, sems, send_sems = refs[9:]
    copies = [
        pltpu.make_async_copy(source.at[0], to, sems.at[at])
        for at, (source, to) in enumerate(zip(sources, (in_ref, out_ref, step_ref)))
    ]
    for copy in copies:
        copy.start()
    mine = lax.axis_index("section")
    base = FAMILIES * ROWS
    rate_ref[0] = jnp.transpose(jnp.broadcast_to(decay_ref[...], (LANES, SECTIONS * GROUP)))
    rate_ref[1] = jnp.transpose(jnp.broadcast_to(gain_ref[...], (LANES, SECTIONS * GROUP)))
    for copy in copies:
        copy.wait()
    for k in range(SECTIONS):
        heads = pl.ds(pl.multiple_of(lax.rem(mine + k, SECTIONS) * GROUP, GROUP), GROUP)
        for family in range(FAMILIES):
            both_ref[k, base + family * GROUP : base + (family + 1) * GROUP, :] = step_ref[family, heads, :]
        both_ref[k, base + 2 * GROUP : base + 3 * GROUP, :] = rate_ref[0, heads, :]
        both_ref[k, base + 3 * GROUP : base + 4 * GROUP, :] = rate_ref[1, heads, :]
    for family in range(FAMILIES):
        turned = jnp.transpose(jnp.concatenate([in_ref[family], out_ref[family]], axis=0))
        for k in range(SECTIONS):
            both_ref[k, family * ROWS : (family + 1) * ROWS, :] = turned
    copies = []
    for k in range(SECTIONS):
        copies.append(pltpu.make_async_copy(both_ref.at[k], pack_refs[k], send_sems.at[k]))
        copies[-1].start()
    for copy in copies:
        copy.wait()


def sort_kernel(at_ref, *refs):
    for x_ref, s_ref, o_ref in zip(refs[0:4], refs[4:8], refs[8:12]):
        o_ref[0, 0:COLS] = jnp.transpose(x_ref[0, 0])
        whole = s_ref[0, 0, 0].reshape(COLS, STATE)
        o_ref[0, COLS:SAVED_ROWS] = jnp.concatenate([whole[: COLS // 2], whole[COLS // 2 :]], axis=1).astype(BF16)


def fetch_home(early, late, to, sems):
    mine = lax.axis_index("section")
    for is_early, pieces in ((True, early), (False, late)):

        @pl.when((mine >= 2) == is_early)
        def _():
            for k in range(SECTIONS):
                source = lax.rem(mine - k + SECTIONS, SECTIONS)
                pltpu.make_async_copy(pieces[k], to(source), sems.at[k]).start()

    for k in range(SECTIONS):
        pltpu.make_async_copy(early[k], to(k), sems.at[k]).wait()


def home_small_kernel(*refs):
    piece_refs = refs[:4]
    in_ref, out_ref, step_ref, decay_ref, skip_ref, part_ref, part_sem = refs[4:]
    mine = lax.axis_index("section")
    for k in range(SECTIONS):
        source = lax.rem(mine - k + SECTIONS, SECTIONS)
        pltpu.make_async_copy(piece_refs[k], part_ref.at[source], part_sem.at[k]).start()
    for k in range(SECTIONS):
        pltpu.make_async_copy(piece_refs[k], part_ref.at[k], part_sem.at[k]).wait()
    for family in range(FAMILIES):
        rows = slice(family * ROWS, (family + 1) * ROWS)
        total = part_ref[0, rows, :].astype(F32)
        for k in range(1, SECTIONS):
            total = total + part_ref[k, rows, :].astype(F32)
        turned = jnp.transpose(total)
        in_ref[0, family] = turned[0:STATE]
        out_ref[0, family] = turned[STATE:]
        below = FAMILIES * ROWS + family * GROUP
        for k in range(SECTIONS):
            step_ref[0, family, k * GROUP : (k + 1) * GROUP, :] = part_ref[k, below : below + GROUP, :].astype(F32)
    section = (lane_ids((8, LANES)) & (STATE - 1)) >> 4
    total = jnp.zeros((8, LANES), F32)
    for at in range(SECTIONS):
        tail = part_ref[at, GRAD_ROWS:HOME_ROWS, :].astype(F32)
        row = jnp.broadcast_to(tail[0:1] + tail[1:2], (8, LANES))
        shift = lax.rem(at - mine + SECTIONS, SECTIONS) * GROUP
        ahead, behind = pltpu.roll(row, shift, 1), pltpu.roll(row, shift + STATE, 1)
        low = (lane_ids((8, LANES)) & (STATE - 1)) >= shift
        total = jnp.where(section == at, jnp.where(low, ahead, behind), total)
    decay_ref[...] = total[0:1, 0:STATE]
    skip_ref[...] = total[0:1, STATE:]


def home_grad_kernel(*refs):
    early, late = refs[0:4], refs[4:8]
    grad_ref, turned_buf, grad_buf, grad_sem, out_sem = refs[8:]
    fetch_home(early, late, lambda source: turned_buf.at[source], grad_sem)
    outs = []
    for source in range(SECTIONS):
        cols = slice(source * COLS, (source + 1) * COLS)
        for family in range(FAMILIES):
            grad_buf[family, :, cols] = jnp.transpose(turned_buf[source, family])
        outs.append(
            pltpu.make_async_copy(
                grad_buf.at[:, :, pl.ds(source * COLS, COLS)],
                grad_ref.at[0, :, :, pl.ds(source * COLS, COLS)],
                out_sem.at[source],
            )
        )
        outs[-1].start()
    for out in outs:
        out.wait()


def rate_sum_kernel(scale, *refs):
    got_ref, part_refs, buf, sems = refs[0], refs[5:9], refs[9], refs[10]
    total = got_ref[0]
    for at in range(1, BRANCHES):
        total = total + got_ref[at]
    total = jnp.broadcast_to(total * scale, (16, LANES))
    high = total.astype(BF16).astype(F32)
    place = lax.broadcasted_iota(jnp.int32, (16, LANES), 0)
    buf[...] = jnp.where(place == 0, high, jnp.where(place == 1, total - high, 0.0)).astype(BF16)
    copies = [
        pltpu.make_async_copy(buf, part_refs[to].at[pl.ds(GRAD_ROWS, 16)], sems.at[to]) for to in range(SECTIONS)
    ]
    for copy in copies:
        copy.start()
    for copy in copies:
        copy.wait()


VM = pl.BlockSpec(memory_space=pltpu.VMEM)
SM = pl.BlockSpec(memory_space=pltpu.SMEM)
ANY = pl.BlockSpec(memory_space=pl.ANY)
HBM = pl.BlockSpec(memory_space=pltpu.HBM)
PARAMS = pltpu.CompilerParams(vmem_limit_bytes=VMEM_LIMIT)
SMALL_PARAMS = pltpu.CompilerParams(vmem_limit_bytes=32 * 1024 * 1024)


PACKS = pltpu.VMEM((SECTIONS, PACK_ROWS, LANES), F32)


def shape(dims, dtype):
    return jax.ShapeDtypeStruct(dims, dtype)


def cost(flops):
    return pl.CostEstimate(flops=flops, bytes_accessed=4_000_000, transcendentals=0)


def sems(count):
    return pltpu.SemaphoreType.DMA((count,))


def pack_small(state_in, state_out, step_size, decay_rate, skip_gain):
    turned = [jnp.transpose(value, (0, 1, 3, 2)) for value in (state_in, state_out, step_size)]
    return pl.pallas_call(
        pack_kernel,
        out_shape=[shape((PACK_ROWS, LANES), F32)] * SECTIONS,
        in_specs=[ANY] * 3 + [VM] * 2,
        out_specs=[HBM] * SECTIONS,
        scratch_shapes=[
            pltpu.VMEM((FAMILIES, STATE, ROWS), F32),
            pltpu.VMEM((FAMILIES, STATE, ROWS), F32),
            pltpu.VMEM((FAMILIES, SECTIONS * GROUP, ROWS), F32),
            pltpu.VMEM((SECTIONS, PACK_ROWS, LANES), F32),
            pltpu.VMEM((2, SECTIONS * GROUP, LANES), F32),
            sems(3),
            sems(4),
        ],
        compiler_params=PARAMS,
        name="pack_small",
    )(*turned, decay_rate, skip_gain)


def sort_heads(layer_input, saved_states):
    mine = jnp.full((1,), lax.axis_index("section"), jnp.int32)

    def x_spec(k):
        return pl.BlockSpec(
            (1, 1, ROWS, COLS), lambda f, at: (0, f, 0, lax.rem(at[0] + k, SECTIONS))
        )

    def s_spec(k):
        return pl.BlockSpec(
            (1, 1, 1, GROUP, HEADDIM, STATE), lambda f, at: (0, f, 0, lax.rem(at[0] + k, SECTIONS), 0, 0)
        )

    return pl.pallas_call(
        sort_kernel,
        grid_spec=pltpu.PrefetchScalarGridSpec(
            num_scalar_prefetch=1,
            grid=(FAMILIES,),
            in_specs=[x_spec(k) for k in range(SECTIONS)] + [s_spec(k) for k in range(SECTIONS)],
            out_specs=[pl.BlockSpec((1, SAVED_ROWS, LANES), lambda f, at: (f, 0, 0))] * SECTIONS,
        ),
        out_shape=[shape((FAMILIES, SAVED_ROWS, LANES), BF16)] * SECTIONS,
        compiler_params=PARAMS,
        cost_estimate=cost(4_000_000_000),
        name="sort_heads",
    )(mine, *([layer_input] * SECTIONS), *([saved_states] * SECTIONS))


def first_phase(high_at, lengths, cotangent, packs, after):
    return pl.pallas_call(
        functools.partial(first_kernel, high_at, len(after)),
        out_shape=[
            shape((BRANCHES, SEND_ROWS, LANES), BF16),
            shape((FAMILIES, COLS, ROWS), BF16),
        ],
        in_specs=[SM] + [ANY] * (5 + len(after)),
        out_specs=[HBM, HBM],
        scratch_shapes=[
            pltpu.VMEM((FAMILIES, ROWS, COLS), BF16),
            pltpu.VMEM((FAMILIES, COLS, ROWS), BF16),
            pltpu.VMEM((BRANCHES, SEND_ROWS, LANES), BF16),
            PACKS,
            sems(4),
            sems(4),
        ],
        compiler_params=PARAMS,
        name="first_phase",
    )(lengths, cotangent, *packs, *after)


def later_phase(high_at, goes_on, packs, upstream, ends, after):
    outs = [shape((FAMILIES, COLS, ROWS), BF16)] * 4
    outs += [shape((FAMILIES, COLS, ROWS), BF16)] * 2
    scratch = [
        pltpu.VMEM((2, FAMILIES, COLS, ROWS), BF16),
        pltpu.VMEM((FAMILIES, COLS, ROWS), BF16),
        pltpu.VMEM((BRANCHES, HEADDIM, LANES), BF16),
        PACKS,
        sems(2),
        sems(2),
        sems(2),
        sems(4),
    ]
    if goes_on:
        outs += [shape((BRANCHES, SEND_ROWS, LANES), BF16)]
        scratch += [pltpu.VMEM((BRANCHES, SEND_ROWS, LANES), BF16), sems(2)]
    return pl.pallas_call(
        functools.partial(later_kernel, high_at, goes_on, len(after)),
        out_shape=outs,
        in_specs=[ANY] * (6 + len(after)),
        out_specs=[HBM] * len(outs),
        scratch_shapes=scratch,
        compiler_params=PARAMS,
        name="later_phase",
    )(*packs, upstream, ends, *after)


def other_phase(high_at, sides, packs, ups, ends, saved, held, after):
    final = len(sides) == 2
    if final:
        outs = [shape((HOME_ROWS, LANES), BF16)] * SECTIONS + [shape((BRANCHES, 1, LANES), F32)]
    else:
        outs = [shape((GRAD_ROWS, LANES), BF16), shape((GROUP, LANES), F32)]
    return pl.pallas_call(
        functools.partial(other_kernel, high_at, sides, len(after)),
        out_shape=outs,
        in_specs=[ANY] * 11 + ([ANY, ANY, VM, VM] if final else []) + [ANY] * len(after),
        out_specs=[HBM] * (len(outs) - 1) + [VM],
        scratch_shapes=[
            pltpu.VMEM((2, FAMILIES, SAVED_ROWS, LANES), BF16),
            pltpu.VMEM((2, FAMILIES, COLS, ROWS), BF16),
            pltpu.VMEM((BRANCHES, HEADDIM, LANES), BF16),
            pltpu.VMEM((2, GRAD_ROWS, LANES), BF16),
            PACKS,
            sems(2),
            sems(2),
            sems(4),
            sems(1),
            sems(4),
        ],
        compiler_params=PARAMS,
        cost_estimate=cost(6_000_000_000 * len(sides)),
        name="other_phase",
    )(*packs, *ups, ends, *saved, *held, *after)


def chain(got, after):
    return pl.pallas_call(
        chain_kernel,
        out_shape=shape((BRANCHES, HEADDIM, LANES), BF16),
        in_specs=[VM] + [ANY] * len(after),
        out_specs=VM,
        compiler_params=SMALL_PARAMS,
        name="chain",
    )(got, *after)


def home_small(parts):
    return pl.pallas_call(
        home_small_kernel,
        out_shape=[
            shape((1, FAMILIES, STATE, ROWS), F32),
            shape((1, FAMILIES, STATE, ROWS), F32),
            shape((1, FAMILIES, SECTIONS * GROUP, ROWS), F32),
            shape((1, SECTIONS * GROUP), F32),
            shape((1, SECTIONS * GROUP), F32),
        ],
        in_specs=[ANY] * 4,
        out_specs=[VM] * 5,
        scratch_shapes=[pltpu.VMEM((SECTIONS, HOME_ROWS, LANES), BF16), sems(SECTIONS)],
        compiler_params=PARAMS,
        name="home_small",
    )(*parts)


def home_grad(early, late):
    return pl.pallas_call(
        home_grad_kernel,
        out_shape=shape((1, FAMILIES, ROWS, SECTIONS * COLS), BF16),
        in_specs=[ANY] * 8,
        out_specs=HBM,
        scratch_shapes=[
            pltpu.VMEM((SECTIONS, FAMILIES, COLS, ROWS), BF16),
            pltpu.VMEM((FAMILIES, ROWS, SECTIONS * COLS), BF16),
            sems(SECTIONS),
            sems(SECTIONS),
        ],
        compiler_params=PARAMS,
        cost_estimate=cost(3_000_000_000),
        name="home_grad",
    )(*early, *late)


def rate_sum(got, parts, scale):
    return pl.pallas_call(
        functools.partial(rate_sum_kernel, scale),
        out_shape=[shape((HOME_ROWS, LANES), BF16)] * SECTIONS,
        in_specs=[VM] + [HBM] * SECTIONS,
        out_specs=[HBM] * SECTIONS,
        scratch_shapes=[pltpu.VMEM((16, LANES), BF16), sems(SECTIONS)],
        input_output_aliases={1 + k: k for k in range(SECTIONS)},
        compiler_params=PARAMS,
        name="rate_sum",
    )(got, *parts)


def swap(value, axis):
    return lax.all_to_all(value, axis, 0, 0, tiled=True)


def send_on(value, k, targets):
    pairs = [(i, (i + k) % SECTIONS) for i in range(SECTIONS) if (i + k) % SECTIONS in targets]
    return lax.ppermute(value, "section", pairs)


def send_home(pieces, targets):
    return [pieces[0]] + [send_on(pieces[k], k, targets) for k in range(1, SECTIONS)]


def exchange(send, after):
    return swap(chain(swap(send, "branch"), after), "branch")


def shards(
    layer_input,
    cotangent,
    state_in,
    state_out,
    step_size,
    saved_states,
    decay_rate,
    skip_gain,
    lengths,
):
    grad_scale = 1.0 / math.sqrt(FAMILIES * ROWS * BRANCHES * HEADDIM)
    everyone = tuple(range(SECTIONS))
    packs = pack_small(state_in, state_out, step_size, decay_rate, skip_gain)
    packs = [packs[0]] + [send_on(packs[k], k, everyone) for k in range(1, SECTIONS)]
    saved = sort_heads(layer_input, saved_states)
    top, upstream = first_phase(3, lengths, cotangent, packs, [saved[0]])
    saved = [saved[0]] + [send_on(saved[k], k, everyone) for k in range(1, SECTIONS)]
    ends = exchange(top, [])
    early = later_phase(3, True, packs, upstream, ends, [saved[1], saved[3]])
    early_grads = send_home(early[:4], (2, 3))
    ups = (upstream, early[4])
    part_a, small_a = other_phase(3, (0,), packs, ups, ends, saved, [], [])
    next_ends = exchange(early[6], [part_a])
    part_b, small_b = other_phase(3, (1,), packs, ups, ends, saved, [], [])
    late = later_phase(1, False, packs, early[5], next_ends, early_grads[1:] + [part_b])
    late_grads = send_home(late[:4], (0, 1))
    ups = (early[5], late[4])
    *parts, rates = other_phase(1, (0, 1), packs, ups, next_ends, saved, [part_a, part_b, small_a, small_b], [])
    parts = send_home(rate_sum(swap(rates, "branch"), parts, grad_scale), everyone)
    *others, decay_sum, skip_sum = home_small(parts)
    others = tuple(jnp.transpose(value, (0, 1, 3, 2)) for value in others)
    return (home_grad(early_grads, late_grads),) + others + (decay_sum, skip_sum)


def solution(mesh):
    placed = (
        P("section", None, "branch", None),
        P(None, "branch", None),
        P("section", None, "branch", None),
        P("section", None, "branch", None),
        P("section", None, "branch", None),
        P("section", None, "branch", None, None, None),
        P("section", None),
        P("section", None),
        P(),
    )
    return jax.shard_map(
        shards,
        mesh=mesh,
        in_specs=placed,
        out_specs=(
            P("section", None, "branch", None),
            P("section", None, "branch", None),
            P("section", None, "branch", None),
            P("section", None, "branch", None),
            P("section", None),
            P("section", None),
        ),
        check_vma=False,
    )
```

time: 199 us -> 163 us (0.82)
  starting transfers between devices: 74.9 us -> 57.4 us
  Pallas kernels: 61.7 us -> 50.7 us
  waiting for transfers between devices: 38.9 us -> 35.5 us
  blocking collectives: 14.5 us -> 11.6 us
  local copies, waits for them, and re-layouts: 6.82 us -> 4.62 us
    ppermute x21 -> x15, waiting for transfers between devices: 26 us -> 5.69 us  [send_on(): return lax.ppermute(value, 'section', pairs)]
    all_to_all x5 -> x4, waiting for transfers between devices: 12.9 us -> 29.8 us  [swap(): return lax.all_to_all(value, axis, 0, 0, tiled=True)]
    ppermute x21 -> x15, starting transfers between devices: 44.8 us -> 35.6 us  [send_on(): return lax.ppermute(value, 'section', pairs)]
    pallas_call x3, Pallas kernels: 25.9 us -> 17.3 us  [other_phase(): pl.pallas_call(functools.partial(other_kernel, high_at, sides, len(after)...]
    all_to_all x5 -> x4, starting transfers between devices: 30 us -> 21.8 us  [swap(): return lax.all_to_all(value, axis, 0, 0, tiled=True)]
    all_to_all x1, blocking collectives: 14.5 us -> 11.6 us  [swap(): return lax.all_to_all(value, axis, 0, 0, tiled=True)]
    pallas_call x2, Pallas kernels: 14.2 us -> 11.8 us  [later_phase(): pl.pallas_call(functools.partial(later_kernel, high_at, goes_on, len(afte...]
    unnamed x38 -> x24, local copies, waits for them, and re-layouts: 6.22 us -> 4.62 us
  transfers between devices with their start and end apart: 26 -> 19, of which waited for: 6 -> 8; matrix products, arithmetic and copies ran while one was open for 0% -> 0% of each run, Pallas kernels for 20% -> 21%
where the time goes in v3:
time: 163 us; the launch traced here: 161 us
  starting transfers between devices  57.4 us (35%)
  Pallas kernels  50.7 us (31%)
  waiting for transfers between devices  35.5 us (22%)
  blocking collectives  11.6 us (7%)
  local copies, waits for them, and re-layouts  4.62 us (3%)
    ppermute x15, starting transfers between devices, send_on(): return lax.ppermute(value, 'section', pairs)  35.6 us
    all_to_all x4, waiting for transfers between devices, swap(): return lax.all_to_all(value, axis, 0, 0, tiled=True)  29.8 us
    all_to_all x4, starting transfers between devices, swap(): return lax.all_to_all(value, axis, 0, 0, tiled=True)  21.8 us
    pallas_call x3, Pallas kernels, other_phase(): pl.pallas_call(functools.partial(other_kernel, high_at, sides, len(after)...  17.3 us
    pallas_call x2, Pallas kernels, later_phase(): pl.pallas_call(functools.partial(later_kernel, high_at, goes_on, len(afte...  11.8 us
    all_to_all x1, blocking collectives, swap(): return lax.all_to_all(value, axis, 0, 0, tiled=True)  11.6 us
    pallas_call x1, Pallas kernels, first_phase(): pl.pallas_call(functools.partial(first_kernel, high_at, len(after)), out_...  5.91 us
    ppermute x15, waiting for transfers between devices, send_on(): return lax.ppermute(value, 'section', pairs)  5.69 us
  transfers between devices with their start and end apart: 19, of which 8 were waited for; matrix products, arithmetic and copies ran while one was open for 0% of the time, Pallas kernels for 21%

profile of v3, /device:TPU:0, one launch (start us, length us, event | category | flops | bytes accessed | tf_op | source)
XLA Modules:
  0.0 160.8 jit_solution(8484450116746029443)
XLA Ops:
  0.6 2.6 %pack_small.1 = (f32[320,128]{1,0:T(8,128)}, f32[320,128]{1,0:T(8,128)}, f32[320,128]{1,0:T(8,128)}, f32[320,128]{1,0:T(8,128)}) custom-call(f32[1,2,64,128]{3,2,1,0:T(8,128)} %bitcast.7, f32[1,2,64,128]{3,2,1,0:T(8,128)} %bitcast.8, f32[1,2,64,128]{3,2,1,0:T(8,128)} %bitcast.9, f32[1,64]{1,0:T(1,128)} %refs_3_.2, f32[1,64]{1,0:T(1,128)} %refs_4_.2), custom_call_target="tpu_custom_call" | custom-call | tf_op jit(solution)/shard_map/pack_small/pallas_call | solution.py:581
  3.2 2.1 %collective-permute-start = (f32[320,128]{1,0:T(8,128)}, f32[320,128]{1,0:T(8,128)S(1)}, u32[]{:S(2)}, u32[]{:S(2)}) collective-permute-start(f32[320,128]{1,0:T(8,128)} %get-tuple-element.47), channel_id=1, source_target_pairs={{0,32},{32,64},{64,96},{96,0},{1,33},{33,65},{65,97},{97,1},{2,34}... | collective-permute-start | bytes 491528 | tf_op jit(solution)/shard_map/ppermute | solution.py:772
  5.3 3.6 %collective-permute-start.1 = (f32[320,128]{1,0:T(8,128)}, f32[320,128]{1,0:T(8,128)S(1)}, u32[]{:S(2)}, u32[]{:S(2)}) collective-permute-start(f32[320,128]{1,0:T(8,128)} %get-tuple-element.48), channel_id=1, source_target_pairs={{0,64},{32,96},{64,0},{96,32},{1,65},{33,97},{65,1},{97,33},{2,66}... | collective-permute-start | bytes 491528 | tf_op jit(solution)/shard_map/ppermute | solution.py:772
  8.9 1.0 collective-permute-start.2
  9.9 4.4 %sort_heads.1 = (bf16[2,1536,128]{2,1,0:T(8,128)(2,1)}, bf16[2,1536,128]{2,1,0:T(8,128)(2,1)}, bf16[2,1536,128]{2,1,0:T(8,128)(2,1)}, bf16[2,1536,128]{2,1,0:T(8,128)(2,1)}) custom-call(s32[1]{0:T(128)} %bitcast.3.at_ref, bf16[1,2,128,4096]{3,2,1,0:T(8,128)(2,1)} %refs_3_.3, bf16[1,2,128,4096]{3,2,1,0:T(8,128)(2,1)} %refs_3_.3, ...), custom_call_target="tpu_custom_call" | custom-call | flops 4000000000 | bytes 4000000 | tf_op jit(solution)/shard_map/sort_heads/pallas_call | solution.py:613
  14.3 0.0 collective-permute-done.refs_3_.refs_1_
  14.3 0.0 copy-start.3
  14.3 2.2 %collective-permute-done.1.refs_4_.refs_2_ = f32[320,128]{1,0:T(8,128)S(1)} collective-permute-done((f32[320,128]{1,0:T(8,128)}, f32[320,128]{1,0:T(8,128)S(1)}, u32[]{:S(2)}, u32[]{:S(2)}) %collective-permute-start.1) | collective-permute-done | bytes 163872 | tf_op jit(solution)/shard_map/ppermute | solution.py:772
  16.5 0.0 collective-permute-done.2.refs_5_.refs_3_
  16.5 0.0 copy-done.3
  16.5 0.7 copy-done.4
  17.2 0.1 copy-done.5
  17.2 5.9 %first_phase.1 = (bf16[32,112,128]{2,1,0:T(8,128)(2,1)}, bf16[2,1024,128]{2,1,0:T(8,128)(2,1)}) custom-call(s32[2,16]{1,0:T(2,128)} %refs_0_.3, bf16[2,128,4096]{2,1,0:T(8,128)(2,1)} %refs_1_.3, f32[320,128]{1,0:T(8,128)} %get-tuple-element.46.refs_2_.refs_0_, f32[320,128]{1,0:T(8,128)} %copy-done.3, f32[320,128]{1,0:T(8,128)} %copy-done.4, ...), custom_call_target="tpu_custom_call" | custom-call | tf_op jit(solution)/shard_map/first_phase/pallas_call | solution.py:629
  23.1 7.3 %all-to-all-start = ((bf16[32,112,128]{2,1,0:T(8,128)(2,1)}), bf16[32,112,128]{2,1,0:T(8,128)(2,1)S(1)}, u32[]{:S(2)}, u32[]{:S(2)}) async-start(bf16[32,112,128]{2,1,0:T(8,128)(2,1)} %get-tuple-element.52), calls=%async_computation | async-start | bytes 1835008 | tf_op jit(solution)/shard_map/all_to_all | solution.py:767
  30.5 1.2 collective-permute-start.3
  31.7 2.1 %collective-permute-start.4 = (bf16[2,1536,128]{2,1,0:T(8,128)(2,1)}, bf16[2,1536,128]{2,1,0:T(8,128)(2,1)S(1)}, u32[]{:S(2)}, u32[]{:S(2)}) collective-permute-start(bf16[2,1536,128]{2,1,0:T(8,128)(2,1)} %get-tuple-element.54), channel_id=1, source_target_pairs={{0,96},{32,0},{64,32},{96,64},{1,97},{33,1},{65,33},{97,65},{2,98}... | collective-permute-start | bytes 2359304 | tf_op jit(solution)/shard_map/ppermute | solution.py:772
  33.8 12.6 %all-to-all-done.refs_0_ = bf16[32,112,128]{2,1,0:T(8,128)(2,1)S(1)} async-done(((bf16[32,112,128]{2,1,0:T(8,128)(2,1)}), bf16[32,112,128]{2,1,0:T(8,128)(2,1)S(1)}, u32[]{:S(2)}, u32[]{:S(2)}) %all-to-all-start) | async-done | bytes 917536 | tf_op jit(solution)/shard_map/all_to_all | solution.py:767
  46.4 1.2 chain.2
  47.6 3.9 %all-to-all-start.1 = ((bf16[32,64,128]{2,1,0:T(8,128)(2,1)}), bf16[32,64,128]{2,1,0:T(8,128)(2,1)S(1)}, u32[]{:S(2)}, u32[]{:S(2)}) async-start(bf16[32,64,128]{2,1,0:T(8,128)(2,1)} %chain.2), calls=%async_computation.1 | async-start | bytes 1048576 | tf_op jit(solution)/shard_map/all_to_all | solution.py:767
  51.5 2.2 %collective-permute-start.8 = (bf16[2,1536,128]{2,1,0:T(8,128)(2,1)}, bf16[2,1536,128]{2,1,0:T(8,128)(2,1)}, u32[]{:S(2)}, u32[]{:S(2)}) collective-permute-start(bf16[2,1536,128]{2,1,0:T(8,128)(2,1)} %get-tuple-element.62), channel_id=1, source_target_pairs={{0,64},{32,96},{64,0},{96,32},{1,65},{33,97},{65,1},{97,33},{2,66}... | collective-permute-start | bytes 2359304 | tf_op jit(solution)/shard_map/ppermute | solution.py:772
  53.7 0.0 collective-permute-done.3.refs_6_.refs_8_
  53.7 0.0 collective-permute-done.4.refs_7_.refs_10_
  53.7 0.0 copy-start.7
  53.7 9.5 %all-to-all-done.1.refs_5_.refs_6_ = bf16[32,64,128]{2,1,0:T(8,128)(2,1)S(1)} async-done(((bf16[32,64,128]{2,1,0:T(8,128)(2,1)}), bf16[32,64,128]{2,1,0:T(8,128)(2,1)S(1)}, u32[]{:S(2)}, u32[]{:S(2)}) %all-to-all-start.1) | async-done | bytes 524320 | tf_op jit(solution)/shard_map/all_to_all | solution.py:767
  63.2 0.0 copy-done.6
  63.2 0.0 copy-done.7
  63.2 0.8 copy-done.1
  64.0 7.2 %later_phase.2 = (bf16[2,1024,128]{2,1,0:T(8,128)(2,1)}, bf16[2,1024,128]{2,1,0:T(8,128)(2,1)}, bf16[2,1024,128]{2,1,0:T(8,128)(2,1)}, bf16[2,1024,128]{2,1,0:T(...) custom-call(f32[320,128]{1,0:T(8,128)} %get-tuple-element.46.refs_2_.refs_0, ...), custom_call_target="tpu_custom_call" | custom-call | tf_op jit(solution)/shard_map/later_phase/pallas_call | solution.py:666
  71.2 3.9 %all-to-all-start.2 = ((bf16[32,112,128]{2,1,0:T(8,128)(2,1)}), bf16[32,112,128]{2,1,0:T(8,128)(2,1)S(1)}, u32[]{:S(2)}, u32[]{:S(2)}) async-start(bf16[32,112,128]{2,1,0:T(8,128)(2,1)} %get-tuple-element.60), calls=%async_computation.2 | async-start | bytes 1835008 | tf_op jit(solution)/shard_map/all_to_all | solution.py:767
  75.2 1.5 collective-permute-start.5
  76.6 6.7 %collective-permute-start.6 = (bf16[2,1024,128]{2,1,0:T(8,128)(2,1)}, bf16[2,1024,128]{2,1,0:T(8,128)(2,1)}, u32[]{:S(2)}, u32[]{:S(2)}) collective-permute-start(bf16[2,1024,128]{2,1,0:T(8,128)(2,1)} %get-tuple-element.57), channel_id=1, source_target_pairs={{0,64},{32,96},{1,65},{33,97},{2,66},{34,98},{3,67},{35,99},{4,68}... | collective-permute-start | bytes 1572872 | tf_op jit(solution)/shard_map/ppermute | solution.py:772
  83.4 2.1 %collective-permute-start.7 = (bf16[2,1024,128]{2,1,0:T(8,128)(2,1)}, bf16[2,1024,128]{2,1,0:T(8,128)(2,1)}, u32[]{:S(2)}, u32[]{:S(2)}) collective-permute-start(bf16[2,1024,128]{2,1,0:T(8,128)(2,1)} %get-tuple-element.58), channel_id=1, source_target_pairs={{0,96},{96,64},{1,97},{97,65},{2,98},{98,66},{3,99},{99,67},{4,100... | collective-permute-start | bytes 1572872 | tf_op jit(solution)/shard_map/ppermute | solution.py:772
  85.5 0.0 collective-permute-done.8.refs_9_
  85.5 4.8 %other_phase.3 = (bf16[288,128]{1,0:T(8,128)(2,1)}, f32[16,128]{1,0:T(8,128)}) custom-call(f32[320,128]{1,0:T(8,128)} %get-tuple-element.46.refs_2_.refs_0_, f32[320,128]{1,0:T(8,128)} %copy-done.3, f32[320,128]{1,0:T(8,128)} %copy-done.4, f32[320,128]{1,0:T(8,128)} %copy-done.5, bf16[2,1024,128]{2,1,0:T(8,128)(2,1)} %get-tuple-element.51.refs_4_, ...), custom_call_target="tpu_custom_call" | custom-call | flops 6000000000 | bytes 4000000 | tf_op jit(solution)/shard_map/other_phase/pallas_call | solution.py:683
  90.3 0.8 all-to-all-done.2.refs_0_
  91.1 0.9 copy-done
  92.0 1.2 chain.3
  93.1 6.6 %all-to-all-start.3 = ((bf16[32,64,128]{2,1,0:T(8,128)(2,1)}), bf16[32,64,128]{2,1,0:T(8,128)(2,1)S(1)}, u32[]{:S(2)}, u32[]{:S(2)}) async-start(bf16[32,64,128]{2,1,0:T(8,128)(2,1)} %chain.3), calls=%async_computation.3 | async-start | bytes 1048576 | tf_op jit(solution)/shard_map/all_to_all | solution.py:767
  99.7 4.8 %other_phase.4 = (bf16[288,128]{1,0:T(8,128)(2,1)}, f32[16,128]{1,0:T(8,128)}) custom-call(f32[320,128]{1,0:T(8,128)} %get-tuple-element.46.refs_2_.refs_0_, f32[320,128]{1,0:T(8,128)} %copy-done.3, f32[320,128]{1,0:T(8,128)} %copy-done.4, f32[320,128]{1,0:T(8,128)} %copy-done.5, bf16[2,1024,128]{2,1,0:T(8,128)(2,1)} %get-tuple-element.51.refs_4_, ...), custom_call_target="tpu_custom_call" | custom-call | flops 6000000000 | bytes 4000000 | tf_op jit(solution)/shard_map/other_phase/pallas_call | solution.py:683
  104.6 0.0 collective-permute-done.5.refs_6_.refs_1_
  104.6 0.0 collective-permute-done.6.refs_7_.refs_2_
  104.6 0.0 collective-permute-done.7.refs_8_.refs_3_
  104.6 6.9 %all-to-all-done.3.refs_5_.refs_6_ = bf16[32,64,128]{2,1,0:T(8,128)(2,1)S(1)} async-done(((bf16[32,64,128]{2,1,0:T(8,128)(2,1)}), bf16[32,64,128]{2,1,0:T(8,128)(2,1)S(1)}, u32[]{:S(2)}, u32[]{:S(2)}) %all-to-all-start.3) | async-done | bytes 524320 | tf_op jit(solution)/shard_map/all_to_all | solution.py:767
  111.5 0.8 copy-done.2
  112.3 4.7 %later_phase.3 = (bf16[2,1024,128]{2,1,0:T(8,128)(2,1)}, bf16[2,1024,128]{2,1,0:T(8,128)(2,1)}, bf16[2,1024,128]{2,1,0:T(8,128)(2,1)}, bf16[2,1024,128]{2,1,0:T(...) custom-call(f32[320,128]{1,0:T(8,128)} %get-tuple-element.46.refs_2_.refs_0_, ...), custom_call_target="tpu_custom_call" | custom-call | tf_op jit(solution)/shard_map/later_phase/pallas_call | solution.py:666
  116.9 1.9 %collective-permute-start.9 = (bf16[2,1024,128]{2,1,0:T(8,128)(2,1)}, bf16[2,1024,128]{2,1,0:T(8,128)(2,1)S(1)}, u32[]{:S(2)}, u32[]{:S(2)}) collective-permute-start(bf16[2,1024,128]{2,1,0:T(8,128)(2,1)} %get-tuple-element.66), channel_id=1, source_target_pairs={{0,32},{96,0},{1,33},{97,1},{2,34},{98,2},{3,35},{99,3},{4,36},{10... | collective-permute-start | bytes 1572872 | tf_op jit(solution)/shard_map/ppermute | solution.py:772
  118.9 1.3 collective-permute-start.10
  120.2 1.3 collective-permute-start.11
  121.5 7.7 %other_phase.5 = (bf16[304,128]{1,0:T(8,128)(2,1)}, bf16[304,128]{1,0:T(8,128)(2,1)}, bf16[304,128]{1,0:T(8,128)(2,1)}, bf16[304,128]{1,0:T(8,128)(2,1)}, f32[32,1,128]{2,1,0:T(1,128)}) custom-call(f32[320,128]{1,0:T(8,128)} %get-tuple-element.46.refs_2_.refs_0_, f32[320,128]{1,0:T(8,128)} %copy-done.3, f32[320,128]{1,0:T(8,128)} %copy-done.4, ...), custom_call_target="tpu_custom_call" | custom-call | flops 12000000000 | bytes 4000000 | tf_op jit(solution)/shard_map/other_phase/pallas_call | solution.py:683
  129.2 11.6 %all_to_all.25.refs_0_ = f32[32,1,128]{2,1,0:T(1,128)} all-to-all(f32[32,1,128]{2,1,0:T(1,128)} %get-tuple-element.72), channel_id=1, replica_groups=mesh['section'=4,'branch'=32] {'branch'}, dimensions={0} | all-to-all | bytes 32768 | tf_op jit(solution)/shard_map/all_to_all | solution.py:767
  140.8 1.4 rate_sum.1
  142.2 2.7 %collective-permute-start.12 = (bf16[304,128]{1,0:T(8,128)(2,1)}, bf16[304,128]{1,0:T(8,128)(2,1)S(1)}, u32[]{:S(2)}, u32[]{:S(2)}) collective-permute-start(bf16[304,128]{1,0:T(8,128)(2,1)} %get-tuple-element.78), channel_id=1, source_target_pairs={{0,32},{32,64},{64,96},{96,0},{1,33},{33,65},{65,97},{97,1},{2,34}... | collective-permute-start | bytes 233480 | tf_op jit(solution)/shard_map/ppermute | solution.py:772
  144.9 3.2 %collective-permute-start.13 = (bf16[304,128]{1,0:T(8,128)(2,1)}, bf16[304,128]{1,0:T(8,128)(2,1)S(1)}, u32[]{:S(2)}, u32[]{:S(2)}) collective-permute-start(bf16[304,128]{1,0:T(8,128)(2,1)} %get-tuple-element.79), channel_id=1, source_target_pairs={{0,64},{32,96},{64,0},{96,32},{1,65},{33,97},{65,1},{97,33},{2,66}... | collective-permute-start | bytes 233480 | tf_op jit(solution)/shard_map/ppermute | solution.py:772
  148.1 1.2 collective-permute-done.12.refs_1_
  149.3 2.7 %collective-permute-start.14 = (bf16[304,128]{1,0:T(8,128)(2,1)}, bf16[304,128]{1,0:T(8,128)(2,1)S(1)}, u32[]{:S(2)}, u32[]{:S(2)}) collective-permute-start(bf16[304,128]{1,0:T(8,128)(2,1)} %get-tuple-element.80), channel_id=1, source_target_pairs={{0,96},{32,0},{64,32},{96,64},{1,97},{33,1},{65,33},{97,65},{2,98}... | collective-permute-start | bytes 233480 | tf_op jit(solution)/shard_map/ppermute | solution.py:772
  152.0 0.5 collective-permute-done.13.refs_2_
  152.5 1.8 %collective-permute-done.14.refs_3_ = bf16[304,128]{1,0:T(8,128)(2,1)S(1)} collective-permute-done((bf16[304,128]{1,0:T(8,128)(2,1)}, bf16[304,128]{1,0:T(8,128)(2,1)S(1)}, u32[]{:S(2)}, u32[]{:S(2)}) %collective-permute-start.14) | collective-permute-done | bytes 77856 | tf_op jit(solution)/shard_map/ppermute | solution.py:772
  154.3 0.6 copy-done.10
  155.0 1.8 %home_small.1 = (f32[1,2,64,128]{3,2,1,0:T(8,128)}, f32[1,2,64,128]{3,2,1,0:T(8,128)}, f32[1,2,64,128]{3,2,1,0:T(8,128)}, f32[1,64]{1,0:T(1,128)}, f32[1,64]{1,0:T(1,128)}) custom-call(bf16[304,128]{1,0:T(8,128)(2,1)} %get-tuple-element.77.refs_0_, bf16[304,128]{1,0:T(8,128)(2,1)} %copy-done.8, bf16[304,128]{1,0:T(8,128)(2,1)} %copy-done.9, ...), custom_call_target="tpu_custom_call" | custom-call | tf_op jit(solution)/shard_map/home_small/pallas_call | solution.py:718
  156.8 0.0 collective-permute-done.9.refs_5_
  156.8 0.0 collective-permute-done.10.refs_6_
  156.8 0.0 collective-permute-done.11.refs_7_
  156.8 0.8 copy-done.11
  157.6 3.1 %home_grad.1 = bf16[1,2,128,4096]{3,2,1,0:T(8,128)(2,1)} custom-call(bf16[2,1024,128]{2,1,0:T(8,128)(2,1)} %get-tuple-element.55.refs_0_, bf16[2,1024,128]{2,1,0:T(8,128)(2,1)} %collective-permute-done.5.refs_6_.refs_1_, bf16[2,1024,128]{2,1,0:T(8,128)(2,1)} %collective-permute-done.6.refs_7_.refs_2_, ...), custom_call_target="tpu_custom_call" | custom-call | flops 3000000000 | bytes 4000000 | tf_op jit(solution)/shard_map/home_grad/pallas_call | solution.py:736
  (12 shorter events, 0.0 us)
Async XLA Ops:
  3.2 11.1 %collective-permute-start = (f32[320,128]{1,0:T(8,128)}, f32[320,128]{1,0:T(8,128)S(1)}, u32[]{:S(2)}, u32[]{:S(2)}) collective-permute-start(f32[320,128]{1,0:T(8,128)} %get-tuple-element.47), channel_id=1, source_target_pairs={{0,32},{32,64},{64,96},{96,0},{1,33},{33,65},{65,97},{97,1},{2,34}... | collective-permute-start | bytes 491528 | tf_op jit(solution)/shard_map/ppermute | solution.py:772
  5.3 11.2 %collective-permute-start.1 = (f32[320,128]{1,0:T(8,128)}, f32[320,128]{1,0:T(8,128)S(1)}, u32[]{:S(2)}, u32[]{:S(2)}) collective-permute-start(f32[320,128]{1,0:T(8,128)} %get-tuple-element.48), channel_id=1, source_target_pairs={{0,64},{32,96},{64,0},{96,32},{1,65},{33,97},{65,1},{97,33},{2,66}... | collective-permute-start | bytes 491528 | tf_op jit(solution)/shard_map/ppermute | solution.py:772
  8.9 7.6 %collective-permute-start.2 = (f32[320,128]{1,0:T(8,128)}, f32[320,128]{1,0:T(8,128)S(1)}, u32[]{:S(2)}, u32[]{:S(2)}) collective-permute-start(f32[320,128]{1,0:T(8,128)} %get-tuple-element.49), channel_id=1, source_target_pairs={{0,96},{32,0},{64,32},{96,64},{1,97},{33,1},{65,33},{97,65},{2,98}... | collective-permute-start | bytes 491528 | tf_op jit(solution)/shard_map/ppermute | solution.py:772
  14.3 2.2 %copy-start.3 = (f32[320,128]{1,0:T(8,128)}, f32[320,128]{1,0:T(8,128)S(1)}, u32[]{:S(2)}) copy-start(f32[320,128]{1,0:T(8,128)S(1)} %collective-permute-done.refs_3_.refs_1_) | copy-start | bytes 491524
  16.5 0.7 copy-start.4
  16.5 0.7 copy-start.5
  23.1 23.3 %all-to-all-start = ((bf16[32,112,128]{2,1,0:T(8,128)(2,1)}), bf16[32,112,128]{2,1,0:T(8,128)(2,1)S(1)}, u32[]{:S(2)}, u32[]{:S(2)}) async-start(bf16[32,112,128]{2,1,0:T(8,128)(2,1)} %get-tuple-element.52), calls=%async_computation | async-start | bytes 1835008 | tf_op jit(solution)/shard_map/all_to_all | solution.py:767
  30.5 23.2 %collective-permute-start.3 = (bf16[2,1536,128]{2,1,0:T(8,128)(2,1)}, bf16[2,1536,128]{2,1,0:T(8,128)(2,1)S(1)}, u32[]{:S(2)}, u32[]{:S(2)}) collective-permute-start(bf16[2,1536,128]{2,1,0:T(8,128)(2,1)} %get-tuple-element.53), channel_id=1, source_target_pairs={{0,32},{32,64},{64,96},{96,0},{1,33},{33,65},{65,97},{97,1},{2,34}... | collective-permute-start | bytes 2359304 | tf_op jit(solution)/shard_map/ppermute | solution.py:772
  31.7 22.0 %collective-permute-start.4 = (bf16[2,1536,128]{2,1,0:T(8,128)(2,1)}, bf16[2,1536,128]{2,1,0:T(8,128)(2,1)S(1)}, u32[]{:S(2)}, u32[]{:S(2)}) collective-permute-start(bf16[2,1536,128]{2,1,0:T(8,128)(2,1)} %get-tuple-element.54), channel_id=1, source_target_pairs={{0,96},{32,0},{64,32},{96,64},{1,97},{33,1},{65,33},{97,65},{2,98}... | collective-permute-start | bytes 2359304 | tf_op jit(solution)/shard_map/ppermute | solution.py:772
  47.6 15.7 %all-to-all-start.1 = ((bf16[32,64,128]{2,1,0:T(8,128)(2,1)}), bf16[32,64,128]{2,1,0:T(8,128)(2,1)S(1)}, u32[]{:S(2)}, u32[]{:S(2)}) async-start(bf16[32,64,128]{2,1,0:T(8,128)(2,1)} %chain.2), calls=%async_computation.1 | async-start | bytes 1048576 | tf_op jit(solution)/shard_map/all_to_all | solution.py:767
  51.5 34.0 %collective-permute-start.8 = (bf16[2,1536,128]{2,1,0:T(8,128)(2,1)}, bf16[2,1536,128]{2,1,0:T(8,128)(2,1)}, u32[]{:S(2)}, u32[]{:S(2)}) collective-permute-start(bf16[2,1536,128]{2,1,0:T(8,128)(2,1)} %get-tuple-element.62), channel_id=1, source_target_pairs={{0,64},{32,96},{64,0},{96,32},{1,65},{33,97},{65,1},{97,33},{2,66}... | collective-permute-start | bytes 2359304 | tf_op jit(solution)/shard_map/ppermute | solution.py:772
  53.7 9.5 %copy-start.6 = (bf16[2,1536,128]{2,1,0:T(8,128)(2,1)}, bf16[2,1536,128]{2,1,0:T(8,128)(2,1)S(1)}, u32[]{:S(2)}) copy-start(bf16[2,1536,128]{2,1,0:T(8,128)(2,1)S(1)} %collective-permute-done.3.refs_6_.refs_8_) | copy-start | bytes 2359300
  53.7 9.5 %copy-start.7 = (bf16[2,1536,128]{2,1,0:T(8,128)(2,1)}, bf16[2,1536,128]{2,1,0:T(8,128)(2,1)S(1)}, u32[]{:S(2)}) copy-start(bf16[2,1536,128]{2,1,0:T(8,128)(2,1)S(1)} %collective-permute-done.4.refs_7_.refs_10_) | copy-start | bytes 2359300
  63.2 0.8 copy-start.1
  71.2 19.9 %all-to-all-start.2 = ((bf16[32,112,128]{2,1,0:T(8,128)(2,1)}), bf16[32,112,128]{2,1,0:T(8,128)(2,1)S(1)}, u32[]{:S(2)}, u32[]{:S(2)}) async-start(bf16[32,112,128]{2,1,0:T(8,128)(2,1)} %get-tuple-element.60), calls=%async_computation.2 | async-start | bytes 1835008 | tf_op jit(solution)/shard_map/all_to_all | solution.py:767
  75.2 29.4 %collective-permute-start.5 = (bf16[2,1024,128]{2,1,0:T(8,128)(2,1)}, bf16[2,1024,128]{2,1,0:T(8,128)(2,1)}, u32[]{:S(2)}, u32[]{:S(2)}) collective-permute-start(bf16[2,1024,128]{2,1,0:T(8,128)(2,1)} %get-tuple-element.56), channel_id=1, source_target_pairs={{32,64},{64,96},{33,65},{65,97},{34,66},{66,98},{35,67},{67,99},{3... | collective-permute-start | bytes 1572872 | tf_op jit(solution)/shard_map/ppermute | solution.py:772
  76.6 27.9 %collective-permute-start.6 = (bf16[2,1024,128]{2,1,0:T(8,128)(2,1)}, bf16[2,1024,128]{2,1,0:T(8,128)(2,1)}, u32[]{:S(2)}, u32[]{:S(2)}) collective-permute-start(bf16[2,1024,128]{2,1,0:T(8,128)(2,1)} %get-tuple-element.57), channel_id=1, source_target_pairs={{0,64},{32,96},{1,65},{33,97},{2,66},{34,98},{3,67},{35,99},{4,68}... | collective-permute-start | bytes 1572872 | tf_op jit(solution)/shard_map/ppermute | solution.py:772
  83.4 21.2 %collective-permute-start.7 = (bf16[2,1024,128]{2,1,0:T(8,128)(2,1)}, bf16[2,1024,128]{2,1,0:T(8,128)(2,1)}, u32[]{:S(2)}, u32[]{:S(2)}) collective-permute-start(bf16[2,1024,128]{2,1,0:T(8,128)(2,1)} %get-tuple-element.58), channel_id=1, source_target_pairs={{0,96},{96,64},{1,97},{97,65},{2,98},{98,66},{3,99},{99,67},{4,100... | collective-permute-start | bytes 1572872 | tf_op jit(solution)/shard_map/ppermute | solution.py:772
  91.1 0.9 copy-start
  93.1 18.4 %all-to-all-start.3 = ((bf16[32,64,128]{2,1,0:T(8,128)(2,1)}), bf16[32,64,128]{2,1,0:T(8,128)(2,1)S(1)}, u32[]{:S(2)}, u32[]{:S(2)}) async-start(bf16[32,64,128]{2,1,0:T(8,128)(2,1)} %chain.3), calls=%async_computation.3 | async-start | bytes 1048576 | tf_op jit(solution)/shard_map/all_to_all | solution.py:767
  111.5 0.8 copy-start.2
  116.9 39.8 %collective-permute-start.9 = (bf16[2,1024,128]{2,1,0:T(8,128)(2,1)}, bf16[2,1024,128]{2,1,0:T(8,128)(2,1)S(1)}, u32[]{:S(2)}, u32[]{:S(2)}) collective-permute-start(bf16[2,1024,128]{2,1,0:T(8,128)(2,1)} %get-tuple-element.66), channel_id=1, source_target_pairs={{0,32},{96,0},{1,33},{97,1},{2,34},{98,2},{3,35},{99,3},{4,36},{10... | collective-permute-start | bytes 1572872 | tf_op jit(solution)/shard_map/ppermute | solution.py:772
  118.9 37.9 %collective-permute-start.10 = (bf16[2,1024,128]{2,1,0:T(8,128)(2,1)}, bf16[2,1024,128]{2,1,0:T(8,128)(2,1)}, u32[]{:S(2)}, u32[]{:S(2)}) collective-permute-start(bf16[2,1024,128]{2,1,0:T(8,128)(2,1)} %get-tuple-element.67), channel_id=1, source_target_pairs={{64,0},{96,32},{65,1},{97,33},{66,2},{98,34},{67,3},{99,35},{68,4}... | collective-permute-start | bytes 1572872 | tf_op jit(solution)/shard_map/ppermute | solution.py:772
  120.2 36.6 %collective-permute-start.11 = (bf16[2,1024,128]{2,1,0:T(8,128)(2,1)}, bf16[2,1024,128]{2,1,0:T(8,128)(2,1)}, u32[]{:S(2)}, u32[]{:S(2)}) collective-permute-start(bf16[2,1024,128]{2,1,0:T(8,128)(2,1)} %get-tuple-element.68), channel_id=1, source_target_pairs={{32,0},{64,32},{33,1},{65,33},{34,2},{66,34},{35,3},{67,35},{36,4}... | collective-permute-start | bytes 1572872 | tf_op jit(solution)/shard_map/ppermute | solution.py:772
  142.2 7.1 %collective-permute-start.12 = (bf16[304,128]{1,0:T(8,128)(2,1)}, bf16[304,128]{1,0:T(8,128)(2,1)S(1)}, u32[]{:S(2)}, u32[]{:S(2)}) collective-permute-start(bf16[304,128]{1,0:T(8,128)(2,1)} %get-tuple-element.78), channel_id=1, source_target_pairs={{0,32},{32,64},{64,96},{96,0},{1,33},{33,65},{65,97},{97,1},{2,34}... | collective-permute-start | bytes 233480 | tf_op jit(solution)/shard_map/ppermute | solution.py:772
  144.9 7.5 %collective-permute-start.13 = (bf16[304,128]{1,0:T(8,128)(2,1)}, bf16[304,128]{1,0:T(8,128)(2,1)S(1)}, u32[]{:S(2)}, u32[]{:S(2)}) collective-permute-start(bf16[304,128]{1,0:T(8,128)(2,1)} %get-tuple-element.79), channel_id=1, source_target_pairs={{0,64},{32,96},{64,0},{96,32},{1,65},{33,97},{65,1},{97,33},{2,66}... | collective-permute-start | bytes 233480 | tf_op jit(solution)/shard_map/ppermute | solution.py:772
  149.3 5.0 %copy-start.8 = (bf16[304,128]{1,0:T(8,128)(2,1)}, bf16[304,128]{1,0:T(8,128)(2,1)S(1)}, u32[]{:S(2)}) copy-start(bf16[304,128]{1,0:T(8,128)(2,1)S(1)} %collective-permute-done.12.refs_1_) | copy-start | bytes 233476
  149.3 5.0 %collective-permute-start.14 = (bf16[304,128]{1,0:T(8,128)(2,1)}, bf16[304,128]{1,0:T(8,128)(2,1)S(1)}, u32[]{:S(2)}, u32[]{:S(2)}) collective-permute-start(bf16[304,128]{1,0:T(8,128)(2,1)} %get-tuple-element.80), channel_id=1, source_target_pairs={{0,96},{32,0},{64,32},{96,64},{1,97},{33,1},{65,33},{97,65},{2,98}... | collective-permute-start | bytes 233480 | tf_op jit(solution)/shard_map/ppermute | solution.py:772
  152.5 1.8 %copy-start.9 = (bf16[304,128]{1,0:T(8,128)(2,1)}, bf16[304,128]{1,0:T(8,128)(2,1)S(1)}, u32[]{:S(2)}) copy-start(bf16[304,128]{1,0:T(8,128)(2,1)S(1)} %collective-permute-done.13.refs_2_) | copy-start | bytes 233476
  154.3 0.6 copy-start.10
  156.8 0.8 copy-start.11

commit v4 on v3

--- a/solution.py
+++ b/solution.py
@@ -168,7 +168,8 @@
         put_grad(rows, grad.astype(BF16))
 
 
-def phase_c(family, side, layer, upper_at, saved_ref, end_ref):
+def phase_c(family, side, layer, upper_at, saved_ref, end_ref, want):
+    grads = grad_step = small = None
     b_one, c_one = layer.b[side].astype(BF16), layer.c[side].astype(BF16)
     b_turned = jnp.transpose(layer.b[side]).astype(BF16)
     read = layer.read.astype(BF16)
@@ -193,33 +194,38 @@
             packed = pltpu.roll(packed, STATE, 1)
         saved = jnp.where((lanes < STATE) == (side == 0), packed, 0.0)
         x_saved = jnp.concatenate([x_one, saved.astype(BF16)], axis=1)
+        if "grads" in want:
+            left = left + dot(hat_one, x_saved, TN)
+            grad_in = grad_in + dot(x_one, ends, TN)
+        if "rates" not in want:
+            continue
         end_in = dot(ends, b_turned, NN)
         pulled = dot(hat_one, read, NN) + end_in
         forward = dot(x_saved, weights, NN)
-        left = left + dot(hat_one, x_saved, TN)
-        grad_in = grad_in + dot(x_one, ends, TN)
         x_pulled = x_hat * pulled
         worth.append(head_sums(x_pulled))
         flow.append(head_sums(hat * forward - x_pulled))
         ending.append(head_sums(x_hat * end_in + ends.astype(F32) * saved))
         skips.append(head_sums(x * upstream))
-    flow, worth, ending, skips = (jnp.concatenate(part, axis=0) for part in (flow, worth, ending, skips))
-    pairs, grad_out = left[:, 0:ROWS], left[:, ROWS:]
-    pairs = jnp.where(layer.row >= layer.col, pairs, 0.0).astype(BF16)
-    grad_out = grad_out + dot(pairs, b_one, NN)
-    grad_in = grad_in + dot(pairs, c_one, TN)
-    lanes = lane_ids((ROWS, LANES))
-    if side == 0:
-        grads = jnp.where(lanes < STATE, grad_in, pltpu.roll(grad_out, STATE, 1))
-    else:
-        grads = jnp.where(lanes < STATE, pltpu.roll(grad_in, STATE, 1), grad_out)
-    later = jnp.where(layer.row >= layer.col, 1.0, 0.0).astype(BF16)
-    rate = dot2(split(flow), later, NN) + jnp.sum(ending, axis=1, keepdims=True)
-    grad_step = worth / layer.step - layer.decay * rate
-    decay_part = jnp.sum(-layer.step * rate, axis=1, keepdims=True)
-    skip_part = jnp.sum(skips, axis=1, keepdims=True)
-    place = lane_ids((GROUP, LANES))
-    small = jnp.where(place == 0, decay_part, jnp.where(place == 1, skip_part, 0.0))
+    if "grads" in want:
+        pairs, grad_out = left[:, 0:ROWS], left[:, ROWS:]
+        pairs = jnp.where(layer.row >= layer.col, pairs, 0.0).astype(BF16)
+        grad_out = grad_out + dot(pairs, b_one, NN)
+        grad_in = grad_in + dot(pairs, c_one, TN)
+        lanes = lane_ids((ROWS, LANES))
+        if side == 0:
+            grads = jnp.where(lanes < STATE, grad_in, pltpu.roll(grad_out, STATE, 1))
+        else:
+            grads = jnp.where(lanes < STATE, pltpu.roll(grad_in, STATE, 1), grad_out)
+    if "rates" in want:
+        flow, worth, ending, skips = (jnp.concatenate(part, axis=0) for part in (flow, worth, ending, skips))
+        later = jnp.where(layer.row >= layer.col, 1.0, 0.0).astype(BF16)
+        rate = dot2(split(flow), later, NN) + jnp.sum(ending, axis=1, keepdims=True)
+        grad_step = worth / layer.step - layer.decay * rate
+        decay_part = jnp.sum(-layer.step * rate, axis=1, keepdims=True)
+        skip_part = jnp.sum(skips, axis=1, keepdims=True)
+        place = lane_ids((GROUP, LANES))
+        small = jnp.where(place == 0, decay_part, jnp.where(place == 1, skip_part, 0.0))
     return grads, grad_step, small
 
 
@@ -235,6 +241,7 @@
     copy = pltpu.make_async_copy(cot_ref.at[:, :, pl.ds(at, COLS)], cot_buf, sems.at[3])
     copy.start()
     wait_packs(layers, pack_refs, pack_ref, pack_sem)
+    ready = [[Layer(pack_ref, at, family) for at in layers] for family in range(FAMILIES)]
     copy.wait()
     copies = []
     for family in range(FAMILIES):
@@ -247,9 +254,7 @@
             up_buf[family, rows, :] = value.astype(BF16)
             return value
 
-        high = Layer(pack_ref, high_at, family)
-        low = Layer(pack_ref, high_at - 1, family)
-        phase_a(family, upper_at, high, low, send_buf)
+        phase_a(family, upper_at, *ready[family], send_buf)
         heads = pl.ds(family * GROUP, GROUP)
         copies.append(pltpu.make_async_copy(send_buf.at[heads], send_ref.at[heads], sems.at[family]))
         copies[-1].start()
@@ -280,6 +285,7 @@
     fetch_packs(layers[2:], pack_refs, pack_ref, pack_sem)
     mine = lax.axis_index("section")
     wait_packs(layers[:2], pack_refs, pack_ref, pack_sem)
+    ready = {at: Layer(pack_ref, high_at - at[0], at[1]) for at in ((0, 0), (0, 1))}
     for copy in ins:
         copy.wait()
     for side in range(2):
@@ -294,7 +300,7 @@
             def put_grad(rows, value):
                 grad_buf[side, family, rows, :] = value
 
-            layer = Layer(pack_ref, layer_at, family)
+            layer = ready.get((side, family)) or Layer(pack_ref, layer_at, family)
             phase_b(family, side, layer, upper_at, end_buf, put_grad)
         ahead = lax.rem(layer_at - mine + SECTIONS, SECTIONS)
         for k in range(SECTIONS):
@@ -325,16 +331,20 @@
         pltpu.make_async_copy(grad_buf.at[side], grad_refs[0], grad_sem.at[side]).wait()
 
 
-def other_kernel(high_at, sides, after, *refs):
+def other_kernel(high_at, sides, want, after, *refs):
     pack_refs, up_refs, end_ref, saved_refs = refs[:4], refs[4:6], refs[6], refs[7:11]
     refs = refs[11:]
-    final = len(sides) == 2
+    final = want == ("grads",)
     if final:
-        held_refs, small_refs, refs = refs[0:2], refs[2:4], refs[4:]
+        held_refs, steps_ref, refs = refs[0:2], refs[2], refs[3:]
+    elif len(sides) == 2:
+        small_refs, refs = refs[0:2], refs[2:]
     refs = refs[after:]
     part_refs, refs = (refs[:4], refs[4:]) if final else (refs[:1], refs[1:])
-    rate_ref, saved_buf, up_buf, end_buf, part_buf, pack_ref = refs[:6]
-    saved_sem, up_sem, part_sem, end_sem, pack_sem = refs[6:]
+    if not final:
+        rate_ref, refs = refs[0], refs[1:]
+    saved_buf, up_buf, end_buf, part_buf, pack_ref = refs[:5]
+    saved_sem, up_sem, part_sem, end_sem, pack_sem = refs[5:]
     mine = lax.axis_index("section")
     layers = [high_at - side for side in sides]
     fetch_packs(layers, pack_refs, pack_ref, pack_sem)
@@ -364,10 +374,13 @@
         moved.append(copies[0])
 
     moved = []
+    steps = slice(FAMILIES * ROWS, GRAD_ROWS)
     if final:
         for side in range(2):
             hand_on(held_refs[side], high_at + 2 - side)
+            pltpu.make_async_copy(steps_ref.at[side], part_buf.at[side, steps], end_sem.at[1 + side]).start()
     wait_packs(layers, pack_refs, pack_ref, pack_sem)
+    ready = [Layer(pack_ref, layers[0], family) for family in range(FAMILIES)]
     ends.wait()
     smalls_of = []
     for side in sides:
@@ -379,15 +392,25 @@
             def upper_at(rows):
                 return up_buf[side, family, rows, :].astype(F32)
 
-            layer = Layer(pack_ref, high_at - side, family)
-            grads, grad_step, small = phase_c(family, side, layer, upper_at, saved_buf.at[side], end_buf)
-            part_buf[side, family * ROWS : (family + 1) * ROWS, :] = grads.astype(BF16)
-            below = FAMILIES * ROWS + family * GROUP
-            part_buf[side, below : below + GROUP, :] = grad_step.astype(BF16)
-            smalls = smalls + small
-        hand_on(part_buf.at[side], high_at - side)
+            layer = ready[family] if side == sides[0] else Layer(pack_ref, high_at - side, family)
+            grads, grad_step, small = phase_c(family, side, layer, upper_at, saved_buf.at[side], end_buf, want)
+            if "grads" in want:
+                part_buf[side, family * ROWS : (family + 1) * ROWS, :] = grads.astype(BF16)
+            if "rates" in want:
+                below = FAMILIES * ROWS + family * GROUP
+                part_buf[side, below : below + GROUP, :] = grad_step.astype(BF16)
+                smalls = smalls + small
+        if final:
+            pltpu.make_async_copy(steps_ref.at[side], part_buf.at[side, steps], end_sem.at[1 + side]).wait()
+        if "grads" in want:
+            hand_on(part_buf.at[side], high_at - side)
+        else:
+            moved.append(pltpu.make_async_copy(part_buf.at[side, steps], part_refs[0].at[side], part_sem.at[side]))
+            moved[-1].start()
         smalls_of.append(smalls)
     if final:
+        pass
+    elif len(sides) == 2:
         blocks = smalls_of[::-1] + [small_refs[1][...], small_refs[0][...]]
         turned = jnp.transpose(jnp.concatenate(blocks + [jnp.zeros((STATE, LANES), F32)], axis=0))
         row = turned[0:1] + pltpu.roll(turned[1:2], STATE, 1)
@@ -483,7 +506,7 @@
 
 def home_small_kernel(*refs):
     piece_refs = refs[:4]
-    in_ref, out_ref, step_ref, decay_ref, skip_ref, part_ref, part_sem = refs[4:]
+    in_ref, out_ref, step_ref, decay_ref, skip_ref, part_ref, part_sem = refs[-7:]
     mine = lax.axis_index("section")
     for k in range(SECTIONS):
         source = lax.rem(mine - k + SECTIONS, SECTIONS)
@@ -553,6 +576,7 @@
         copy.wait()
 
 
+ALL = ("grads", "rates")
 VM = pl.BlockSpec(memory_space=pltpu.VMEM)
 SM = pl.BlockSpec(memory_space=pltpu.SMEM)
 ANY = pl.BlockSpec(memory_space=pl.ANY)
@@ -674,17 +698,21 @@
     )(*packs, upstream, ends, *after)
 
 
-def other_phase(high_at, sides, packs, ups, ends, saved, held, after):
-    final = len(sides) == 2
-    if final:
-        outs = [shape((HOME_ROWS, LANES), BF16)] * SECTIONS + [shape((BRANCHES, 1, LANES), F32)]
+def other_phase(high_at, sides, want, packs, ups, ends, saved, held, after):
+    if want == ("grads",):
+        outs = [shape((HOME_ROWS, LANES), BF16)] * SECTIONS
+        extra, specs = [ANY] * 3, [HBM] * SECTIONS
+    elif len(sides) == 2:
+        outs = [shape((2, FAMILIES * GROUP, LANES), BF16), shape((BRANCHES, 1, LANES), F32)]
+        extra, specs = [VM] * 2, [HBM, VM]
     else:
         outs = [shape((GRAD_ROWS, LANES), BF16), shape((GROUP, LANES), F32)]
+        extra, specs = [], [HBM, VM]
     return pl.pallas_call(
-        functools.partial(other_kernel, high_at, sides, len(after)),
+        functools.partial(other_kernel, high_at, sides, want, len(after)),
         out_shape=outs,
-        in_specs=[ANY] * 11 + ([ANY, ANY, VM, VM] if final else []) + [ANY] * len(after),
-        out_specs=[HBM] * (len(outs) - 1) + [VM],
+        in_specs=[ANY] * 11 + extra + [ANY] * len(after),
+        out_specs=specs,
         scratch_shapes=[
             pltpu.VMEM((2, FAMILIES, SAVED_ROWS, LANES), BF16),
             pltpu.VMEM((2, FAMILIES, COLS, ROWS), BF16),
@@ -694,11 +722,11 @@
             sems(2),
             sems(2),
             sems(4),
-            sems(1),
+            sems(3),
             sems(4),
         ],
         compiler_params=PARAMS,
-        cost_estimate=cost(6_000_000_000 * len(sides)),
+        cost_estimate=cost(6_000_000_000 if len(want) == 2 else 5_000_000_000),
         name="other_phase",
     )(*packs, *ups, ends, *saved, *held, *after)
 
@@ -714,7 +742,7 @@
     )(got, *after)
 
 
-def home_small(parts):
+def home_small(parts, after):
     return pl.pallas_call(
         home_small_kernel,
         out_shape=[
@@ -724,12 +752,12 @@
             shape((1, SECTIONS * GROUP), F32),
             shape((1, SECTIONS * GROUP), F32),
         ],
-        in_specs=[ANY] * 4,
+        in_specs=[ANY] * (4 + len(after)),
         out_specs=[VM] * 5,
         scratch_shapes=[pltpu.VMEM((SECTIONS, HOME_ROWS, LANES), BF16), sems(SECTIONS)],
         compiler_params=PARAMS,
         name="home_small",
-    )(*parts)
+    )(*parts, *after)
 
 
 def home_grad(early, late):
@@ -802,17 +830,19 @@
     early = later_phase(3, True, packs, upstream, ends, [saved[1], saved[3]])
     early_grads = send_home(early[:4], (2, 3))
     ups = (upstream, early[4])
-    part_a, small_a = other_phase(3, (0,), packs, ups, ends, saved, [], [])
-    next_ends = exchange(early[6], [part_a])
-    part_b, small_b = other_phase(3, (1,), packs, ups, ends, saved, [], [])
+    part_a, small_a = other_phase(3, (0,), ALL, packs, ups, ends, saved, [], [])
+    next_ends = exchange(early[6], [])
+    part_b, small_b = other_phase(3, (1,), ALL, packs, ups, ends, saved, [], [])
     late = later_phase(1, False, packs, early[5], next_ends, early_grads[1:] + [part_b])
     late_grads = send_home(late[:4], (0, 1))
     ups = (early[5], late[4])
-    *parts, rates = other_phase(1, (0, 1), packs, ups, next_ends, saved, [part_a, part_b, small_a, small_b], [])
+    steps, rates = other_phase(1, (0, 1), ("rates",), packs, ups, next_ends, saved, [small_a, small_b], [])
+    parts = other_phase(1, (0, 1), ("grads",), packs, ups, next_ends, saved, [part_a, part_b, steps], [])
     parts = send_home(rate_sum(swap(rates, "branch"), parts, grad_scale), everyone)
-    *others, decay_sum, skip_sum = home_small(parts)
+    grad = home_grad(early_grads, late_grads)
+    *others, decay_sum, skip_sum = home_small(parts, [grad])
     others = tuple(jnp.transpose(value, (0, 1, 3, 2)) for value in others)
-    return (home_grad(early_grads, late_grads),) + others + (decay_sum, skip_sum)
+    return (grad,) + others + (decay_sum, skip_sum)
 
 
 def solution(mesh):

time: 163 us -> 155 us (0.951)
  blocking collectives: 11.6 us -> 0 us
  Pallas kernels: 50.7 us -> 54.7 us
  starting transfers between devices: 57.4 us -> 60.7 us
    all_to_all x1 -> x0, blocking collectives: 11.6 us -> none  [swap(): return lax.all_to_all(value, axis, 0, 0, tiled=True)]
    pallas_call x3 -> x4, Pallas kernels: 17.3 us -> 21.7 us  [other_phase(): pl.pallas_call(functools.partial(other_kernel, high_at, sides, want, len(...]
    all_to_all x4 -> x5, starting transfers between devices: 21.8 us -> 25.3 us  [swap(): return lax.all_to_all(value, axis, 0, 0, tiled=True)]
    ppermute x15, waiting for transfers between devices: 5.69 us -> 2.94 us  [send_on(): return lax.ppermute(value, 'section', pairs)]
    all_to_all x4 -> x5, waiting for transfers between devices: 29.8 us -> 31.2 us  [swap(): return lax.all_to_all(value, axis, 0, 0, tiled=True)]
  transfers between devices with their start and end apart: 19 -> 20, of which waited for: 8 -> 7; matrix products, arithmetic and copies ran while one was open for 0% -> 0% of each run, Pallas kernels for 21% -> 26%
where the time goes in v4:
time: 155 us; the launch traced here: 154 us
  starting transfers between devices  60.7 us (39%)
  Pallas kernels  54.7 us (35%)
  waiting for transfers between devices  34.2 us (22%)
  local copies, waits for them, and re-layouts  3.59 us (2%)
    ppermute x15, starting transfers between devices, send_on(): return lax.ppermute(value, 'section', pairs)  35.4 us
    all_to_all x5, waiting for transfers between devices, swap(): return lax.all_to_all(value, axis, 0, 0, tiled=True)  31.2 us
    all_to_all x5, starting transfers between devices, swap(): return lax.all_to_all(value, axis, 0, 0, tiled=True)  25.3 us
    pallas_call x4, Pallas kernels, other_phase(): pl.pallas_call(functools.partial(other_kernel, high_at, sides, want, len(...  21.7 us
    pallas_call x2, Pallas kernels, later_phase(): pl.pallas_call(functools.partial(later_kernel, high_at, goes_on, len(afte...  11.7 us
    pallas_call x1, Pallas kernels, first_phase(): pl.pallas_call(functools.partial(first_kernel, high_at, len(after)), out_...  5.63 us
    pallas_call x1, Pallas kernels, sort_heads(): pl.pallas_call(sort_kernel, grid_spec=pltpu.PrefetchScalarGridSpec(num_sc...  4.45 us
    unnamed x24, local copies, waits for them, and re-layouts  3.59 us
  transfers between devices with their start and end apart: 20, of which 7 were waited for; matrix products, arithmetic and copies ran while one was open for 0% of the time, Pallas kernels for 26%

profile of v4, /device:TPU:0, one launch (start us, length us, event | category | flops | bytes accessed | tf_op | source)
XLA Modules:
  0.0 154.2 jit_solution(4181567913113420500)
XLA Ops:
  0.6 2.6 %pack_small.1 = (f32[320,128]{1,0:T(8,128)}, f32[320,128]{1,0:T(8,128)}, f32[320,128]{1,0:T(8,128)}, f32[320,128]{1,0:T(8,128)}) custom-call(f32[1,2,64,128]{3,2,1,0:T(8,128)} %bitcast.7, f32[1,2,64,128]{3,2,1,0:T(8,128)} %bitcast.8, f32[1,2,64,128]{3,2,1,0:T(8,128)} %bitcast.9, f32[1,64]{1,0:T(1,128)} %refs_3_.2, f32[1,64]{1,0:T(1,128)} %refs_4_.2), custom_call_target="tpu_custom_call" | custom-call | tf_op jit(solution)/shard_map/pack_small/pallas_call | solution.py:605
  3.2 2.1 %collective-permute-start = (f32[320,128]{1,0:T(8,128)}, f32[320,128]{1,0:T(8,128)S(1)}, u32[]{:S(2)}, u32[]{:S(2)}) collective-permute-start(f32[320,128]{1,0:T(8,128)} %get-tuple-element.48), channel_id=1, source_target_pairs={{0,32},{32,64},{64,96},{96,0},{1,33},{33,65},{65,97},{97,1},{2,34}... | collective-permute-start | bytes 491528 | tf_op jit(solution)/shard_map/ppermute | solution.py:800
  5.3 3.6 %collective-permute-start.1 = (f32[320,128]{1,0:T(8,128)}, f32[320,128]{1,0:T(8,128)S(1)}, u32[]{:S(2)}, u32[]{:S(2)}) collective-permute-start(f32[320,128]{1,0:T(8,128)} %get-tuple-element.49), channel_id=1, source_target_pairs={{0,64},{32,96},{64,0},{96,32},{1,65},{33,97},{65,1},{97,33},{2,66}... | collective-permute-start | bytes 491528 | tf_op jit(solution)/shard_map/ppermute | solution.py:800
  8.9 1.0 collective-permute-start.2
  9.9 4.4 %sort_heads.1 = (bf16[2,1536,128]{2,1,0:T(8,128)(2,1)}, bf16[2,1536,128]{2,1,0:T(8,128)(2,1)}, bf16[2,1536,128]{2,1,0:T(8,128)(2,1)}, bf16[2,1536,128]{2,1,0:T(8,128)(2,1)}) custom-call(s32[1]{0:T(128)} %bitcast.3.at_ref, bf16[1,2,128,4096]{3,2,1,0:T(8,128)(2,1)} %refs_3_.3, bf16[1,2,128,4096]{3,2,1,0:T(8,128)(2,1)} %refs_3_.3, ...), custom_call_target="tpu_custom_call" | custom-call | flops 4000000000 | bytes 4000000 | tf_op jit(solution)/shard_map/sort_heads/pallas_call | solution.py:637
  14.3 0.0 collective-permute-done.refs_3_.refs_1_
  14.3 2.2 %collective-permute-done.1.refs_4_.refs_2_ = f32[320,128]{1,0:T(8,128)S(1)} collective-permute-done((f32[320,128]{1,0:T(8,128)}, f32[320,128]{1,0:T(8,128)S(1)}, u32[]{:S(2)}, u32[]{:S(2)}) %collective-permute-start.1) | collective-permute-done | bytes 163872 | tf_op jit(solution)/shard_map/ppermute | solution.py:800
  16.5 0.0 collective-permute-done.2.refs_5_.refs_3_
  16.5 0.7 copy-done.3
  17.2 0.1 copy-done.4
  17.2 5.6 %first_phase.1 = (bf16[32,112,128]{2,1,0:T(8,128)(2,1)}, bf16[2,1024,128]{2,1,0:T(8,128)(2,1)}) custom-call(s32[2,16]{1,0:T(2,128)} %refs_0_.3, bf16[2,128,4096]{2,1,0:T(8,128)(2,1)} %refs_1_.3, f32[320,128]{1,0:T(8,128)} %get-tuple-element.47.refs_2_.refs_0_, f32[320,128]{1,0:T(8,128)} %copy-done.2, f32[320,128]{1,0:T(8,128)} %copy-done.3, ...), custom_call_target="tpu_custom_call" | custom-call | tf_op jit(solution)/shard_map/first_phase/pallas_call | solution.py:653
  22.9 7.3 %all-to-all-start = ((bf16[32,112,128]{2,1,0:T(8,128)(2,1)}), bf16[32,112,128]{2,1,0:T(8,128)(2,1)S(1)}, u32[]{:S(2)}, u32[]{:S(2)}) async-start(bf16[32,112,128]{2,1,0:T(8,128)(2,1)} %get-tuple-element.53), calls=%async_computation | async-start | bytes 1835008 | tf_op jit(solution)/shard_map/all_to_all | solution.py:795
  30.2 1.2 collective-permute-start.3
  31.4 2.1 %collective-permute-start.4 = (bf16[2,1536,128]{2,1,0:T(8,128)(2,1)}, bf16[2,1536,128]{2,1,0:T(8,128)(2,1)S(1)}, u32[]{:S(2)}, u32[]{:S(2)}) collective-permute-start(bf16[2,1536,128]{2,1,0:T(8,128)(2,1)} %get-tuple-element.55), channel_id=1, source_target_pairs={{0,96},{32,0},{64,32},{96,64},{1,97},{33,1},{65,33},{97,65},{2,98}... | collective-permute-start | bytes 2359304 | tf_op jit(solution)/shard_map/ppermute | solution.py:800
  33.5 12.6 %all-to-all-done.refs_0_ = bf16[32,112,128]{2,1,0:T(8,128)(2,1)S(1)} async-done(((bf16[32,112,128]{2,1,0:T(8,128)(2,1)}), bf16[32,112,128]{2,1,0:T(8,128)(2,1)S(1)}, u32[]{:S(2)}, u32[]{:S(2)}) %all-to-all-start) | async-done | bytes 917536 | tf_op jit(solution)/shard_map/all_to_all | solution.py:795
  46.1 1.2 chain.2
  47.3 3.9 %all-to-all-start.1 = ((bf16[32,64,128]{2,1,0:T(8,128)(2,1)}), bf16[32,64,128]{2,1,0:T(8,128)(2,1)S(1)}, u32[]{:S(2)}, u32[]{:S(2)}) async-start(bf16[32,64,128]{2,1,0:T(8,128)(2,1)} %chain.2), calls=%async_computation.1 | async-start | bytes 1048576 | tf_op jit(solution)/shard_map/all_to_all | solution.py:795
  51.2 2.3 %collective-permute-start.8 = (bf16[2,1536,128]{2,1,0:T(8,128)(2,1)}, bf16[2,1536,128]{2,1,0:T(8,128)(2,1)}, u32[]{:S(2)}, u32[]{:S(2)}) collective-permute-start(bf16[2,1536,128]{2,1,0:T(8,128)(2,1)} %get-tuple-element.63), channel_id=1, source_target_pairs={{0,64},{32,96},{64,0},{96,32},{1,65},{33,97},{65,1},{97,33},{2,66}... | collective-permute-start | bytes 2359304 | tf_op jit(solution)/shard_map/ppermute | solution.py:800
  53.4 0.0 collective-permute-done.3.refs_6_.refs_8_
  53.4 0.0 collective-permute-done.4.refs_7_.refs_10_
  53.4 0.0 copy-start.6
  53.4 9.5 %all-to-all-done.1.refs_5_.refs_6_ = bf16[32,64,128]{2,1,0:T(8,128)(2,1)S(1)} async-done(((bf16[32,64,128]{2,1,0:T(8,128)(2,1)}), bf16[32,64,128]{2,1,0:T(8,128)(2,1)S(1)}, u32[]{:S(2)}, u32[]{:S(2)}) %all-to-all-start.1) | async-done | bytes 524320 | tf_op jit(solution)/shard_map/all_to_all | solution.py:795
  62.9 0.0 copy-done.6
  62.9 0.8 copy-done.1
  63.8 7.1 %later_phase.2 = (bf16[2,1024,128]{2,1,0:T(8,128)(2,1)}, bf16[2,1024,128]{2,1,0:T(8,128)(2,1)}, bf16[2,1024,128]{2,1,0:T(8,128)(2,1)}, bf16[2,1024,128]{2,1,0:T(...) custom-call(f32[320,128]{1,0:T(8,128)} %get-tuple-element.47.refs_2_.refs_0, ...), custom_call_target="tpu_custom_call" | custom-call | tf_op jit(solution)/shard_map/later_phase/pallas_call | solution.py:690
  70.9 3.9 %all-to-all-start.2 = ((bf16[32,112,128]{2,1,0:T(8,128)(2,1)}), bf16[32,112,128]{2,1,0:T(8,128)(2,1)S(1)}, u32[]{:S(2)}, u32[]{:S(2)}) async-start(bf16[32,112,128]{2,1,0:T(8,128)(2,1)} %get-tuple-element.61), calls=%async_computation.2 | async-start | bytes 1835008 | tf_op jit(solution)/shard_map/all_to_all | solution.py:795
  74.8 1.5 collective-permute-start.5
  76.3 6.7 %collective-permute-start.6 = (bf16[2,1024,128]{2,1,0:T(8,128)(2,1)}, bf16[2,1024,128]{2,1,0:T(8,128)(2,1)}, u32[]{:S(2)}, u32[]{:S(2)}) collective-permute-start(bf16[2,1024,128]{2,1,0:T(8,128)(2,1)} %get-tuple-element.58), channel_id=1, source_target_pairs={{0,64},{32,96},{1,65},{33,97},{2,66},{34,98},{3,67},{35,99},{4,68}... | collective-permute-start | bytes 1572872 | tf_op jit(solution)/shard_map/ppermute | solution.py:800
  83.0 2.1 %collective-permute-start.7 = (bf16[2,1024,128]{2,1,0:T(8,128)(2,1)}, bf16[2,1024,128]{2,1,0:T(8,128)(2,1)}, u32[]{:S(2)}, u32[]{:S(2)}) collective-permute-start(bf16[2,1024,128]{2,1,0:T(8,128)(2,1)} %get-tuple-element.59), channel_id=1, source_target_pairs={{0,96},{96,64},{1,97},{97,65},{2,98},{98,66},{3,99},{99,67},{4,100... | collective-permute-start | bytes 1572872 | tf_op jit(solution)/shard_map/ppermute | solution.py:800
  85.1 0.0 collective-permute-done.8.refs_9_
  85.1 4.5 %other_phase.5 = (bf16[288,128]{1,0:T(8,128)(2,1)}, f32[16,128]{1,0:T(8,128)}) custom-call(f32[320,128]{1,0:T(8,128)} %get-tuple-element.47.refs_2_.refs_0_, f32[320,128]{1,0:T(8,128)} %copy-done.2, f32[320,128]{1,0:T(8,128)} %copy-done.3, f32[320,128]{1,0:T(8,128)} %copy-done.4, bf16[2,1024,128]{2,1,0:T(8,128)(2,1)} %get-tuple-element.52.refs_4_, ...), custom_call_target="tpu_custom_call" | custom-call | flops 6000000000 | bytes 4000000 | tf_op jit(solution)/shard_map/other_phase/pallas_call | solution.py:711
  89.6 1.1 all-to-all-done.2.refs_0_
  90.7 1.2 chain.3
  91.9 6.3 %all-to-all-start.3 = ((bf16[32,64,128]{2,1,0:T(8,128)(2,1)}), bf16[32,64,128]{2,1,0:T(8,128)(2,1)S(1)}, u32[]{:S(2)}, u32[]{:S(2)}) async-start(bf16[32,64,128]{2,1,0:T(8,128)(2,1)} %chain.3), calls=%async_computation.3 | async-start | bytes 1048576 | tf_op jit(solution)/shard_map/all_to_all | solution.py:795
  98.2 4.5 %other_phase.4 = (bf16[288,128]{1,0:T(8,128)(2,1)}, f32[16,128]{1,0:T(8,128)}) custom-call(f32[320,128]{1,0:T(8,128)} %get-tuple-element.47.refs_2_.refs_0_, f32[320,128]{1,0:T(8,128)} %copy-done.2, f32[320,128]{1,0:T(8,128)} %copy-done.3, f32[320,128]{1,0:T(8,128)} %copy-done.4, bf16[2,1024,128]{2,1,0:T(8,128)(2,1)} %get-tuple-element.52.refs_4_, ...), custom_call_target="tpu_custom_call" | custom-call | flops 6000000000 | bytes 4000000 | tf_op jit(solution)/shard_map/other_phase/pallas_call | solution.py:711
  102.7 0.0 collective-permute-done.5.refs_6_.refs_1_
  102.7 0.0 collective-permute-done.6.refs_7_.refs_2_
  102.7 0.7 collective-permute-done.7.refs_8_.refs_3_
  103.4 6.5 %all-to-all-done.3.refs_5_.refs_6_ = bf16[32,64,128]{2,1,0:T(8,128)(2,1)S(1)} async-done(((bf16[32,64,128]{2,1,0:T(8,128)(2,1)}), bf16[32,64,128]{2,1,0:T(8,128)(2,1)S(1)}, u32[]{:S(2)}, u32[]{:S(2)}) %all-to-all-start.3) | async-done | bytes 524320 | tf_op jit(solution)/shard_map/all_to_all | solution.py:795
  109.9 0.8 copy-done
  110.7 4.6 %later_phase.3 = (bf16[2,1024,128]{2,1,0:T(8,128)(2,1)}, bf16[2,1024,128]{2,1,0:T(8,128)(2,1)}, bf16[2,1024,128]{2,1,0:T(8,128)(2,1)}, bf16[2,1024,128]{2,1,0:T(...) custom-call(f32[320,128]{1,0:T(8,128)} %get-tuple-element.47.refs_2_.refs_0_, ...), custom_call_target="tpu_custom_call" | custom-call | tf_op jit(solution)/shard_map/later_phase/pallas_call | solution.py:690
  115.3 1.9 %collective-permute-start.9 = (bf16[2,1024,128]{2,1,0:T(8,128)(2,1)}, bf16[2,1024,128]{2,1,0:T(8,128)(2,1)S(1)}, u32[]{:S(2)}, u32[]{:S(2)}) collective-permute-start(bf16[2,1024,128]{2,1,0:T(8,128)(2,1)} %get-tuple-element.66), channel_id=1, source_target_pairs={{0,32},{96,0},{1,33},{97,1},{2,34},{98,2},{3,35},{99,3},{4,36},{10... | collective-permute-start | bytes 1572872 | tf_op jit(solution)/shard_map/ppermute | solution.py:800
  117.2 1.3 collective-permute-start.10
  118.5 1.3 collective-permute-start.11
  119.8 7.0 %other_phase.6 = (bf16[2,32,128]{2,1,0:T(8,128)(2,1)}, f32[32,1,128]{2,1,0:T(1,128)}) custom-call(f32[320,128]{1,0:T(8,128)} %get-tuple-element.47.refs_2_.refs_0_, f32[320,128]{1,0:T(8,128)} %copy-done.2, f32[320,128]{1,0:T(8,128)} %copy-done.3, f32[320,128]{1,0:T(8,128)} %copy-done.4, bf16[2,1024,128]{2,1,0:T(8,128)(2,1)} %get-tuple-element.60.refs_4_, ...), custom_call_target="tpu_custom_call" | custom-call | flops 5000000000 | bytes 4000000 | tf_op jit(solution)/shard_map/other_phase/pallas_call | solution.py:711
  126.8 3.8 %all-to-all-start.4 = ((f32[32,1,128]{2,1,0:T(1,128)}), f32[32,1,128]{2,1,0:T(1,128)S(1)}, u32[]{:S(2)}, u32[]{:S(2)}) async-start(f32[32,1,128]{2,1,0:T(1,128)} %get-tuple-element.72), calls=%async_computation.4 | async-start | bytes 32768 | tf_op jit(solution)/shard_map/all_to_all | solution.py:795
  130.6 5.7 %other_phase.7 = (bf16[304,128]{1,0:T(8,128)(2,1)}, bf16[304,128]{1,0:T(8,128)(2,1)}, bf16[304,128]{1,0:T(8,128)(2,1)}, bf16[304,128]{1,0:T(8,128)(2,1)}) custom-call(f32[320,128]{1,0:T(8,128)} %get-tuple-element.47.refs_2_.refs_0_, f32[320,128]{1,0:T(8,128)} %copy-done.2, f32[320,128]{1,0:T(8,128)} %copy-done.3, f32[320,128]{1,0:T(8,128)} %copy-done.4, ...), custom_call_target="tpu_custom_call" | custom-call | flops 5000000000 | bytes 4000000 | tf_op jit(solution)/shard_map/other_phase/pallas_call | solution.py:711
  136.4 1.5 all-to-all-done.4.refs_0_
  137.9 0.6 copy-done.10
  138.5 1.4 rate_sum.1
  139.9 2.7 %collective-permute-start.12 = (bf16[304,128]{1,0:T(8,128)(2,1)}, bf16[304,128]{1,0:T(8,128)(2,1)S(1)}, u32[]{:S(2)}, u32[]{:S(2)}) collective-permute-start(bf16[304,128]{1,0:T(8,128)(2,1)} %get-tuple-element.80), channel_id=1, source_target_pairs={{0,32},{32,64},{64,96},{96,0},{1,33},{33,65},{65,97},{97,1},{2,34}... | collective-permute-start | bytes 233480 | tf_op jit(solution)/shard_map/ppermute | solution.py:800
  142.6 3.2 %collective-permute-start.13 = (bf16[304,128]{1,0:T(8,128)(2,1)}, bf16[304,128]{1,0:T(8,128)(2,1)S(1)}, u32[]{:S(2)}, u32[]{:S(2)}) collective-permute-start(bf16[304,128]{1,0:T(8,128)(2,1)} %get-tuple-element.81), channel_id=1, source_target_pairs={{0,64},{32,96},{64,0},{96,32},{1,65},{33,97},{65,1},{97,33},{2,66}... | collective-permute-start | bytes 233480 | tf_op jit(solution)/shard_map/ppermute | solution.py:800
  145.8 0.0 collective-permute-done.9.refs_5_
  145.8 2.5 %collective-permute-start.14 = (bf16[304,128]{1,0:T(8,128)(2,1)}, bf16[304,128]{1,0:T(8,128)(2,1)S(1)}, u32[]{:S(2)}, u32[]{:S(2)}) collective-permute-start(bf16[304,128]{1,0:T(8,128)(2,1)} %get-tuple-element.82), channel_id=1, source_target_pairs={{0,96},{32,0},{64,32},{96,64},{1,97},{33,1},{65,33},{97,65},{2,98}... | collective-permute-start | bytes 233480 | tf_op jit(solution)/shard_map/ppermute | solution.py:800
  148.4 0.0 collective-permute-done.10.refs_6_
  148.4 0.0 collective-permute-done.11.refs_7_
  148.4 3.1 %home_grad.1.refs_4_ = bf16[1,2,128,4096]{3,2,1,0:T(8,128)(2,1)} custom-call(bf16[2,1024,128]{2,1,0:T(8,128)(2,1)} %get-tuple-element.56.refs_0_, bf16[2,1024,128]{2,1,0:T(8,128)(2,1)} %collective-permute-done.5.refs_6_.refs_1_, bf16[2,1024,128]{2,1,0:T(8,128)(2,1)} %collective-permute-done.6.refs_7_.refs_2_, ...), custom_call_target="tpu_custom_call" | custom-call | flops 3000000000 | bytes 4000000 | tf_op jit(solution)/shard_map/home_grad/pallas_call | solution.py:764
  151.5 0.0 collective-permute-done.12.refs_1_
  151.5 0.0 collective-permute-done.13.refs_2_
  151.5 0.0 collective-permute-done.14.refs_3_
  151.5 0.6 copy-done.7
  152.1 0.0 copy-done.8
  152.1 0.0 copy-done.9
  152.2 1.8 %home_small.1 = (f32[1,2,64,128]{3,2,1,0:T(8,128)}, f32[1,2,64,128]{3,2,1,0:T(8,128)}, f32[1,2,64,128]{3,2,1,0:T(8,128)}, f32[1,64]{1,0:T(1,128)}, f32[1,64]{1,0:T(1,128)}) custom-call(bf16[304,128]{1,0:T(8,128)(2,1)} %get-tuple-element.79.refs_0_, bf16[304,128]{1,0:T(8,128)(2,1)} %copy-done.7, bf16[304,128]{1,0:T(8,128)(2,1)} %copy-done.8, ...), custom_call_target="tpu_custom_call" | custom-call | tf_op jit(solution)/shard_map/home_small/pallas_call | solution.py:746
  (14 shorter events, 0.0 us)
Async XLA Ops:
  3.2 11.1 %collective-permute-start = (f32[320,128]{1,0:T(8,128)}, f32[320,128]{1,0:T(8,128)S(1)}, u32[]{:S(2)}, u32[]{:S(2)}) collective-permute-start(f32[320,128]{1,0:T(8,128)} %get-tuple-element.48), channel_id=1, source_target_pairs={{0,32},{32,64},{64,96},{96,0},{1,33},{33,65},{65,97},{97,1},{2,34}... | collective-permute-start | bytes 491528 | tf_op jit(solution)/shard_map/ppermute | solution.py:800
  5.3 11.2 %collective-permute-start.1 = (f32[320,128]{1,0:T(8,128)}, f32[320,128]{1,0:T(8,128)S(1)}, u32[]{:S(2)}, u32[]{:S(2)}) collective-permute-start(f32[320,128]{1,0:T(8,128)} %get-tuple-element.49), channel_id=1, source_target_pairs={{0,64},{32,96},{64,0},{96,32},{1,65},{33,97},{65,1},{97,33},{2,66}... | collective-permute-start | bytes 491528 | tf_op jit(solution)/shard_map/ppermute | solution.py:800
  8.9 7.6 %collective-permute-start.2 = (f32[320,128]{1,0:T(8,128)}, f32[320,128]{1,0:T(8,128)S(1)}, u32[]{:S(2)}, u32[]{:S(2)}) collective-permute-start(f32[320,128]{1,0:T(8,128)} %get-tuple-element.50), channel_id=1, source_target_pairs={{0,96},{32,0},{64,32},{96,64},{1,97},{33,1},{65,33},{97,65},{2,98}... | collective-permute-start | bytes 491528 | tf_op jit(solution)/shard_map/ppermute | solution.py:800
  14.3 2.2 %copy-start.2 = (f32[320,128]{1,0:T(8,128)}, f32[320,128]{1,0:T(8,128)S(1)}, u32[]{:S(2)}) copy-start(f32[320,128]{1,0:T(8,128)S(1)} %collective-permute-done.refs_3_.refs_1_) | copy-start | bytes 491524
  16.5 0.7 copy-start.3
  16.5 0.7 copy-start.4
  22.9 23.3 %all-to-all-start = ((bf16[32,112,128]{2,1,0:T(8,128)(2,1)}), bf16[32,112,128]{2,1,0:T(8,128)(2,1)S(1)}, u32[]{:S(2)}, u32[]{:S(2)}) async-start(bf16[32,112,128]{2,1,0:T(8,128)(2,1)} %get-tuple-element.53), calls=%async_computation | async-start | bytes 1835008 | tf_op jit(solution)/shard_map/all_to_all | solution.py:795
  30.2 23.2 %collective-permute-start.3 = (bf16[2,1536,128]{2,1,0:T(8,128)(2,1)}, bf16[2,1536,128]{2,1,0:T(8,128)(2,1)S(1)}, u32[]{:S(2)}, u32[]{:S(2)}) collective-permute-start(bf16[2,1536,128]{2,1,0:T(8,128)(2,1)} %get-tuple-element.54), channel_id=1, source_target_pairs={{0,32},{32,64},{64,96},{96,0},{1,33},{33,65},{65,97},{97,1},{2,34}... | collective-permute-start | bytes 2359304 | tf_op jit(solution)/shard_map/ppermute | solution.py:800
  31.4 22.0 %collective-permute-start.4 = (bf16[2,1536,128]{2,1,0:T(8,128)(2,1)}, bf16[2,1536,128]{2,1,0:T(8,128)(2,1)S(1)}, u32[]{:S(2)}, u32[]{:S(2)}) collective-permute-start(bf16[2,1536,128]{2,1,0:T(8,128)(2,1)} %get-tuple-element.55), channel_id=1, source_target_pairs={{0,96},{32,0},{64,32},{96,64},{1,97},{33,1},{65,33},{97,65},{2,98}... | collective-permute-start | bytes 2359304 | tf_op jit(solution)/shard_map/ppermute | solution.py:800
  47.3 15.7 %all-to-all-start.1 = ((bf16[32,64,128]{2,1,0:T(8,128)(2,1)}), bf16[32,64,128]{2,1,0:T(8,128)(2,1)S(1)}, u32[]{:S(2)}, u32[]{:S(2)}) async-start(bf16[32,64,128]{2,1,0:T(8,128)(2,1)} %chain.2), calls=%async_computation.1 | async-start | bytes 1048576 | tf_op jit(solution)/shard_map/all_to_all | solution.py:795
  51.2 33.9 %collective-permute-start.8 = (bf16[2,1536,128]{2,1,0:T(8,128)(2,1)}, bf16[2,1536,128]{2,1,0:T(8,128)(2,1)}, u32[]{:S(2)}, u32[]{:S(2)}) collective-permute-start(bf16[2,1536,128]{2,1,0:T(8,128)(2,1)} %get-tuple-element.63), channel_id=1, source_target_pairs={{0,64},{32,96},{64,0},{96,32},{1,65},{33,97},{65,1},{97,33},{2,66}... | collective-permute-start | bytes 2359304 | tf_op jit(solution)/shard_map/ppermute | solution.py:800
  53.4 9.5 %copy-start.5 = (bf16[2,1536,128]{2,1,0:T(8,128)(2,1)}, bf16[2,1536,128]{2,1,0:T(8,128)(2,1)S(1)}, u32[]{:S(2)}) copy-start(bf16[2,1536,128]{2,1,0:T(8,128)(2,1)S(1)} %collective-permute-done.3.refs_6_.refs_8_) | copy-start | bytes 2359300
  53.4 9.5 %copy-start.6 = (bf16[2,1536,128]{2,1,0:T(8,128)(2,1)}, bf16[2,1536,128]{2,1,0:T(8,128)(2,1)S(1)}, u32[]{:S(2)}) copy-start(bf16[2,1536,128]{2,1,0:T(8,128)(2,1)S(1)} %collective-permute-done.4.refs_7_.refs_10_) | copy-start | bytes 2359300
  62.9 0.8 copy-start.1
  70.9 19.9 %all-to-all-start.2 = ((bf16[32,112,128]{2,1,0:T(8,128)(2,1)}), bf16[32,112,128]{2,1,0:T(8,128)(2,1)S(1)}, u32[]{:S(2)}, u32[]{:S(2)}) async-start(bf16[32,112,128]{2,1,0:T(8,128)(2,1)} %get-tuple-element.61), calls=%async_computation.2 | async-start | bytes 1835008 | tf_op jit(solution)/shard_map/all_to_all | solution.py:795
  74.8 27.9 %collective-permute-start.5 = (bf16[2,1024,128]{2,1,0:T(8,128)(2,1)}, bf16[2,1024,128]{2,1,0:T(8,128)(2,1)}, u32[]{:S(2)}, u32[]{:S(2)}) collective-permute-start(bf16[2,1024,128]{2,1,0:T(8,128)(2,1)} %get-tuple-element.57), channel_id=1, source_target_pairs={{32,64},{64,96},{33,65},{65,97},{34,66},{66,98},{35,67},{67,99},{3... | collective-permute-start | bytes 1572872 | tf_op jit(solution)/shard_map/ppermute | solution.py:800
  76.3 26.4 %collective-permute-start.6 = (bf16[2,1024,128]{2,1,0:T(8,128)(2,1)}, bf16[2,1024,128]{2,1,0:T(8,128)(2,1)}, u32[]{:S(2)}, u32[]{:S(2)}) collective-permute-start(bf16[2,1024,128]{2,1,0:T(8,128)(2,1)} %get-tuple-element.58), channel_id=1, source_target_pairs={{0,64},{32,96},{1,65},{33,97},{2,66},{34,98},{3,67},{35,99},{4,68}... | collective-permute-start | bytes 1572872 | tf_op jit(solution)/shard_map/ppermute | solution.py:800
  83.0 20.4 %collective-permute-start.7 = (bf16[2,1024,128]{2,1,0:T(8,128)(2,1)}, bf16[2,1024,128]{2,1,0:T(8,128)(2,1)}, u32[]{:S(2)}, u32[]{:S(2)}) collective-permute-start(bf16[2,1024,128]{2,1,0:T(8,128)(2,1)} %get-tuple-element.59), channel_id=1, source_target_pairs={{0,96},{96,64},{1,97},{97,65},{2,98},{98,66},{3,99},{99,67},{4,100... | collective-permute-start | bytes 1572872 | tf_op jit(solution)/shard_map/ppermute | solution.py:800
  91.9 18.0 %all-to-all-start.3 = ((bf16[32,64,128]{2,1,0:T(8,128)(2,1)}), bf16[32,64,128]{2,1,0:T(8,128)(2,1)S(1)}, u32[]{:S(2)}, u32[]{:S(2)}) async-start(bf16[32,64,128]{2,1,0:T(8,128)(2,1)} %chain.3), calls=%async_computation.3 | async-start | bytes 1048576 | tf_op jit(solution)/shard_map/all_to_all | solution.py:795
  109.9 0.8 copy-start
  115.3 30.5 %collective-permute-start.9 = (bf16[2,1024,128]{2,1,0:T(8,128)(2,1)}, bf16[2,1024,128]{2,1,0:T(8,128)(2,1)S(1)}, u32[]{:S(2)}, u32[]{:S(2)}) collective-permute-start(bf16[2,1024,128]{2,1,0:T(8,128)(2,1)} %get-tuple-element.66), channel_id=1, source_target_pairs={{0,32},{96,0},{1,33},{97,1},{2,34},{98,2},{3,35},{99,3},{4,36},{10... | collective-permute-start | bytes 1572872 | tf_op jit(solution)/shard_map/ppermute | solution.py:800
  117.2 31.1 %collective-permute-start.10 = (bf16[2,1024,128]{2,1,0:T(8,128)(2,1)}, bf16[2,1024,128]{2,1,0:T(8,128)(2,1)}, u32[]{:S(2)}, u32[]{:S(2)}) collective-permute-start(bf16[2,1024,128]{2,1,0:T(8,128)(2,1)} %get-tuple-element.67), channel_id=1, source_target_pairs={{64,0},{96,32},{65,1},{97,33},{66,2},{98,34},{67,3},{99,35},{68,4}... | collective-permute-start | bytes 1572872 | tf_op jit(solution)/shard_map/ppermute | solution.py:800
  118.5 29.9 %collective-permute-start.11 = (bf16[2,1024,128]{2,1,0:T(8,128)(2,1)}, bf16[2,1024,128]{2,1,0:T(8,128)(2,1)}, u32[]{:S(2)}, u32[]{:S(2)}) collective-permute-start(bf16[2,1024,128]{2,1,0:T(8,128)(2,1)} %get-tuple-element.68), channel_id=1, source_target_pairs={{32,0},{64,32},{33,1},{65,33},{34,2},{66,34},{35,3},{67,35},{36,4}... | collective-permute-start | bytes 1572872 | tf_op jit(solution)/shard_map/ppermute | solution.py:800
  126.8 11.1 %all-to-all-start.4 = ((f32[32,1,128]{2,1,0:T(1,128)}), f32[32,1,128]{2,1,0:T(1,128)S(1)}, u32[]{:S(2)}, u32[]{:S(2)}) async-start(f32[32,1,128]{2,1,0:T(1,128)} %get-tuple-element.72), calls=%async_computation.4 | async-start | bytes 32768 | tf_op jit(solution)/shard_map/all_to_all | solution.py:795
  137.9 0.6 copy-start.10
  139.9 11.6 %collective-permute-start.12 = (bf16[304,128]{1,0:T(8,128)(2,1)}, bf16[304,128]{1,0:T(8,128)(2,1)S(1)}, u32[]{:S(2)}, u32[]{:S(2)}) collective-permute-start(bf16[304,128]{1,0:T(8,128)(2,1)} %get-tuple-element.80), channel_id=1, source_target_pairs={{0,32},{32,64},{64,96},{96,0},{1,33},{33,65},{65,97},{97,1},{2,34}... | collective-permute-start | bytes 233480 | tf_op jit(solution)/shard_map/ppermute | solution.py:800
  142.6 8.9 %collective-permute-start.13 = (bf16[304,128]{1,0:T(8,128)(2,1)}, bf16[304,128]{1,0:T(8,128)(2,1)S(1)}, u32[]{:S(2)}, u32[]{:S(2)}) collective-permute-start(bf16[304,128]{1,0:T(8,128)(2,1)} %get-tuple-element.81), channel_id=1, source_target_pairs={{0,64},{32,96},{64,0},{96,32},{1,65},{33,97},{65,1},{97,33},{2,66}... | collective-permute-start | bytes 233480 | tf_op jit(solution)/shard_map/ppermute | solution.py:800
  145.8 2.6 %copy-start.11 = (bf16[2,1024,128]{2,1,0:T(8,128)(2,1)}, bf16[2,1024,128]{2,1,0:T(8,128)(2,1)S(1)}, u32[]{:S(2)}) copy-start(bf16[2,1024,128]{2,1,0:T(8,128)(2,1)S(1)} %collective-permute-done.9.refs_5_) | copy-start | bytes 1572868
  145.8 5.7 %collective-permute-start.14 = (bf16[304,128]{1,0:T(8,128)(2,1)}, bf16[304,128]{1,0:T(8,128)(2,1)S(1)}, u32[]{:S(2)}, u32[]{:S(2)}) collective-permute-start(bf16[304,128]{1,0:T(8,128)(2,1)} %get-tuple-element.82), channel_id=1, source_target_pairs={{0,96},{32,0},{64,32},{96,64},{1,97},{33,1},{65,33},{97,65},{2,98}... | collective-permute-start | bytes 233480 | tf_op jit(solution)/shard_map/ppermute | solution.py:800
  151.5 0.6 copy-start.7
  151.5 0.6 copy-start.8
  151.5 0.7 copy-start.9

commit v5 on v4

--- a/solution.py
+++ b/solution.py
@@ -87,6 +87,14 @@
 def wait_packs(layers, pack_refs, pack_buf, sems):
     for at in layers:
         pltpu.make_async_copy(pack_refs[0], pack_buf.at[at], sems.at[at]).wait()
+
+
+def wide(a, b):
+    return jnp.concatenate([a, b], axis=1)
+
+
+def folded(value):
+    return value[:, 0:LANES] + value[:, LANES:]
 
 
 class Layer:
@@ -121,6 +129,7 @@
 def phase_a(family, upper_at, high, low, send_ref):
     c_pair = split(jnp.concatenate([high.c[0], low.c[1]], axis=0))
     c_both = split(low.c[0] + low.c[1])
+    c_pair_wide, c_both_wide = wide(*c_pair), wide(*c_both)
     b_turned = jnp.transpose(high.b[0])[0:STATE]
     b_tile = jnp.concatenate([b_turned] * PER_CHUNK, axis=0)
     read = high.read.astype(BF16)
@@ -134,8 +143,9 @@
         low_up = by_head(high.gain, chunk) * upstream + by_head(high.scale, chunk) * pulled
         low_hat2 = split(by_head(low.carried, chunk) * low_up)
         both = tuple(jnp.concatenate([a, b], axis=1) for a, b in zip(hat2, low_hat2))
-        begin = dot3(both, c_pair, NN).astype(BF16)
-        move = dot3(split(by_head(mixed, chunk) * b_tile), c_both, NN)
+        begin = (folded(dot(both[0], c_pair_wide, NN)) + dot(both[1], c_pair[0], NN)).astype(BF16)
+        response = split(by_head(mixed, chunk) * b_tile)
+        move = folded(dot(response[0], c_both_wide, NN)) + dot(response[1], c_both[0], NN)
         for inner in range(PER_CHUNK):
             head = family * GROUP + chunk * PER_CHUNK + inner
             top = inner * HEADDIM
@@ -156,14 +166,15 @@
 
 def phase_b(family, side, layer, upper_at, end_ref, put_grad):
     b2 = split(jnp.transpose(layer.b[side]))
-    weights = jnp.concatenate([layer.read.astype(BF16), b2[0]], axis=0)
+    read = layer.read.astype(BF16)
+    weights = jnp.concatenate([wide(read, jnp.zeros_like(read)), wide(*b2)], axis=0)
     for chunk in range(COLS // CHUNK):
         rows = slice(chunk * CHUNK, (chunk + 1) * CHUNK)
         upstream = upper_at(rows)
         first = family * GROUP + chunk * PER_CHUNK
         ends = end_ref[first : first + PER_CHUNK].reshape(CHUNK, LANES)
         hat = (by_head(layer.carried, chunk) * upstream).astype(BF16)
-        pulled = dot(jnp.concatenate([hat, ends], axis=1), weights, NN) + dot(ends, b2[1], NN)
+        pulled = folded(dot(wide(hat, ends), weights, NN))
         grad = by_head(layer.gain, chunk) * upstream + by_head(layer.scale, chunk) * pulled
         put_grad(rows, grad.astype(BF16))
 
@@ -174,6 +185,7 @@
     b_turned = jnp.transpose(layer.b[side]).astype(BF16)
     read = layer.read.astype(BF16)
     weights = jnp.concatenate([jnp.transpose(layer.read), jnp.transpose(layer.c[side])], axis=0).astype(BF16)
+    pulls = jnp.concatenate([wide(read, jnp.zeros_like(read)), wide(b_turned, b_turned)], axis=0)
     left = jnp.zeros((ROWS, ROWS + LANES), F32)
     grad_in = jnp.zeros((ROWS, LANES), F32)
     flow, worth, ending, skips = [], [], [], []
@@ -199,8 +211,8 @@
             grad_in = grad_in + dot(x_one, ends, TN)
         if "rates" not in want:
             continue
-        end_in = dot(ends, b_turned, NN)
-        pulled = dot(hat_one, read, NN) + end_in
+        both = dot(wide(hat_one, ends), pulls, NN)
+        pulled, end_in = both[:, 0:LANES], both[:, LANES:]
         forward = dot(x_saved, weights, NN)
         x_pulled = x_hat * pulled
         worth.append(head_sums(x_pulled))

time: 155 us -> 154 us (level)
  no operation moved by 1% of the time
where the time goes in v5:
time: 154 us; the launch traced here: 153 us
  starting transfers between devices  60.6 us (39%)
  Pallas kernels  53.5 us (35%)
  waiting for transfers between devices  34.3 us (22%)
  local copies, waits for them, and re-layouts  3.59 us (2%)
    ppermute x15, starting transfers between devices, send_on(): return lax.ppermute(value, 'section', pairs)  35.4 us
    all_to_all x5, waiting for transfers between devices, swap(): return lax.all_to_all(value, axis, 0, 0, tiled=True)  31.2 us
    all_to_all x5, starting transfers between devices, swap(): return lax.all_to_all(value, axis, 0, 0, tiled=True)  25.2 us
    pallas_call x4, Pallas kernels, other_phase(): pl.pallas_call(functools.partial(other_kernel, high_at, sides, want, len(...  21.4 us
    pallas_call x2, Pallas kernels, later_phase(): pl.pallas_call(functools.partial(later_kernel, high_at, goes_on, len(afte...  11 us
    pallas_call x1, Pallas kernels, first_phase(): pl.pallas_call(functools.partial(first_kernel, high_at, len(after)), out_...  5.37 us
    pallas_call x1, Pallas kernels, sort_heads(): pl.pallas_call(sort_kernel, grid_spec=pltpu.PrefetchScalarGridSpec(num_sc...  4.45 us
    unnamed x24, local copies, waits for them, and re-layouts  3.59 us
  transfers between devices with their start and end apart: 20, of which 7 were waited for; matrix products, arithmetic and copies ran while one was open for 0% of the time, Pallas kernels for 26%

profile of v5, /device:TPU:0, one launch (start us, length us, event | category | flops | bytes accessed | tf_op | source)
XLA Modules:
  0.0 153.1 jit_solution(14729799591831878997)
XLA Ops:
  0.6 2.6 %pack_small.1 = (f32[320,128]{1,0:T(8,128)}, f32[320,128]{1,0:T(8,128)}, f32[320,128]{1,0:T(8,128)}, f32[320,128]{1,0:T(8,128)}) custom-call(f32[1,2,64,128]{3,2,1,0:T(8,128)} %bitcast.7, f32[1,2,64,128]{3,2,1,0:T(8,128)} %bitcast.8, f32[1,2,64,128]{3,2,1,0:T(8,128)} %bitcast.9, f32[1,64]{1,0:T(1,128)} %refs_3_.2, f32[1,64]{1,0:T(1,128)} %refs_4_.2), custom_call_target="tpu_custom_call" | custom-call | tf_op jit(solution)/shard_map/pack_small/pallas_call | solution.py:617
  3.2 2.1 %collective-permute-start = (f32[320,128]{1,0:T(8,128)}, f32[320,128]{1,0:T(8,128)S(1)}, u32[]{:S(2)}, u32[]{:S(2)}) collective-permute-start(f32[320,128]{1,0:T(8,128)} %get-tuple-element.48), channel_id=1, source_target_pairs={{0,32},{32,64},{64,96},{96,0},{1,33},{33,65},{65,97},{97,1},{2,34}... | collective-permute-start | bytes 491528 | tf_op jit(solution)/shard_map/ppermute | solution.py:812
  5.3 3.6 %collective-permute-start.1 = (f32[320,128]{1,0:T(8,128)}, f32[320,128]{1,0:T(8,128)S(1)}, u32[]{:S(2)}, u32[]{:S(2)}) collective-permute-start(f32[320,128]{1,0:T(8,128)} %get-tuple-element.49), channel_id=1, source_target_pairs={{0,64},{32,96},{64,0},{96,32},{1,65},{33,97},{65,1},{97,33},{2,66}... | collective-permute-start | bytes 491528 | tf_op jit(solution)/shard_map/ppermute | solution.py:812
  8.9 1.0 collective-permute-start.2
  9.9 4.4 %sort_heads.1 = (bf16[2,1536,128]{2,1,0:T(8,128)(2,1)}, bf16[2,1536,128]{2,1,0:T(8,128)(2,1)}, bf16[2,1536,128]{2,1,0:T(8,128)(2,1)}, bf16[2,1536,128]{2,1,0:T(8,128)(2,1)}) custom-call(s32[1]{0:T(128)} %bitcast.3.at_ref, bf16[1,2,128,4096]{3,2,1,0:T(8,128)(2,1)} %refs_3_.3, bf16[1,2,128,4096]{3,2,1,0:T(8,128)(2,1)} %refs_3_.3, ...), custom_call_target="tpu_custom_call" | custom-call | flops 4000000000 | bytes 4000000 | tf_op jit(solution)/shard_map/sort_heads/pallas_call | solution.py:649
  14.3 0.0 collective-permute-done.refs_3_.refs_1_
  14.3 0.0 copy-start.2
  14.3 2.2 %collective-permute-done.1.refs_4_.refs_2_ = f32[320,128]{1,0:T(8,128)S(1)} collective-permute-done((f32[320,128]{1,0:T(8,128)}, f32[320,128]{1,0:T(8,128)S(1)}, u32[]{:S(2)}, u32[]{:S(2)}) %collective-permute-start.1) | collective-permute-done | bytes 163872 | tf_op jit(solution)/shard_map/ppermute | solution.py:812
  16.5 0.0 collective-permute-done.2.refs_5_.refs_3_
  16.5 0.7 copy-done.3
  17.2 0.1 copy-done.4
  17.2 5.4 %first_phase.1 = (bf16[32,112,128]{2,1,0:T(8,128)(2,1)}, bf16[2,1024,128]{2,1,0:T(8,128)(2,1)}) custom-call(s32[2,16]{1,0:T(2,128)} %refs_0_.3, bf16[2,128,4096]{2,1,0:T(8,128)(2,1)} %refs_1_.3, f32[320,128]{1,0:T(8,128)} %get-tuple-element.47.refs_2_.refs_0_, f32[320,128]{1,0:T(8,128)} %copy-done.2, f32[320,128]{1,0:T(8,128)} %copy-done.3, ...), custom_call_target="tpu_custom_call" | custom-call | tf_op jit(solution)/shard_map/first_phase/pallas_call | solution.py:665
  22.6 7.3 %all-to-all-start = ((bf16[32,112,128]{2,1,0:T(8,128)(2,1)}), bf16[32,112,128]{2,1,0:T(8,128)(2,1)S(1)}, u32[]{:S(2)}, u32[]{:S(2)}) async-start(bf16[32,112,128]{2,1,0:T(8,128)(2,1)} %get-tuple-element.53), calls=%async_computation | async-start | bytes 1835008 | tf_op jit(solution)/shard_map/all_to_all | solution.py:807
  29.9 1.2 collective-permute-start.3
  31.2 2.1 %collective-permute-start.4 = (bf16[2,1536,128]{2,1,0:T(8,128)(2,1)}, bf16[2,1536,128]{2,1,0:T(8,128)(2,1)S(1)}, u32[]{:S(2)}, u32[]{:S(2)}) collective-permute-start(bf16[2,1536,128]{2,1,0:T(8,128)(2,1)} %get-tuple-element.55), channel_id=1, source_target_pairs={{0,96},{32,0},{64,32},{96,64},{1,97},{33,1},{65,33},{97,65},{2,98}... | collective-permute-start | bytes 2359304 | tf_op jit(solution)/shard_map/ppermute | solution.py:812
  33.3 12.6 %all-to-all-done.refs_0_ = bf16[32,112,128]{2,1,0:T(8,128)(2,1)S(1)} async-done(((bf16[32,112,128]{2,1,0:T(8,128)(2,1)}), bf16[32,112,128]{2,1,0:T(8,128)(2,1)S(1)}, u32[]{:S(2)}, u32[]{:S(2)}) %all-to-all-start) | async-done | bytes 917536 | tf_op jit(solution)/shard_map/all_to_all | solution.py:807
  45.9 1.2 chain.2
  47.0 3.9 %all-to-all-start.1 = ((bf16[32,64,128]{2,1,0:T(8,128)(2,1)}), bf16[32,64,128]{2,1,0:T(8,128)(2,1)S(1)}, u32[]{:S(2)}, u32[]{:S(2)}) async-start(bf16[32,64,128]{2,1,0:T(8,128)(2,1)} %chain.2), calls=%async_computation.1 | async-start | bytes 1048576 | tf_op jit(solution)/shard_map/all_to_all | solution.py:807
  50.9 2.2 %collective-permute-start.8 = (bf16[2,1536,128]{2,1,0:T(8,128)(2,1)}, bf16[2,1536,128]{2,1,0:T(8,128)(2,1)}, u32[]{:S(2)}, u32[]{:S(2)}) collective-permute-start(bf16[2,1536,128]{2,1,0:T(8,128)(2,1)} %get-tuple-element.63), channel_id=1, source_target_pairs={{0,64},{32,96},{64,0},{96,32},{1,65},{33,97},{65,1},{97,33},{2,66}... | collective-permute-start | bytes 2359304 | tf_op jit(solution)/shard_map/ppermute | solution.py:812
  53.2 0.0 collective-permute-done.3.refs_6_.refs_8_
  53.2 0.0 collective-permute-done.4.refs_7_.refs_10_
  53.2 9.5 %all-to-all-done.1.refs_5_.refs_6_ = bf16[32,64,128]{2,1,0:T(8,128)(2,1)S(1)} async-done(((bf16[32,64,128]{2,1,0:T(8,128)(2,1)}), bf16[32,64,128]{2,1,0:T(8,128)(2,1)S(1)}, u32[]{:S(2)}, u32[]{:S(2)}) %all-to-all-start.1) | async-done | bytes 524320 | tf_op jit(solution)/shard_map/all_to_all | solution.py:807
  62.7 0.8 copy-done.1
  63.5 6.7 %later_phase.2 = (bf16[2,1024,128]{2,1,0:T(8,128)(2,1)}, bf16[2,1024,128]{2,1,0:T(8,128)(2,1)}, bf16[2,1024,128]{2,1,0:T(8,128)(2,1)}, bf16[2,1024,128]{2,1,0:T(...) custom-call(f32[320,128]{1,0:T(8,128)} %get-tuple-element.47.refs_2_.refs_0, ...), custom_call_target="tpu_custom_call" | custom-call | tf_op jit(solution)/shard_map/later_phase/pallas_call | solution.py:702
  70.2 3.9 %all-to-all-start.2 = ((bf16[32,112,128]{2,1,0:T(8,128)(2,1)}), bf16[32,112,128]{2,1,0:T(8,128)(2,1)S(1)}, u32[]{:S(2)}, u32[]{:S(2)}) async-start(bf16[32,112,128]{2,1,0:T(8,128)(2,1)} %get-tuple-element.61), calls=%async_computation.2 | async-start | bytes 1835008 | tf_op jit(solution)/shard_map/all_to_all | solution.py:807
  74.1 1.5 collective-permute-start.5
  75.6 6.7 %collective-permute-start.6 = (bf16[2,1024,128]{2,1,0:T(8,128)(2,1)}, bf16[2,1024,128]{2,1,0:T(8,128)(2,1)}, u32[]{:S(2)}, u32[]{:S(2)}) collective-permute-start(bf16[2,1024,128]{2,1,0:T(8,128)(2,1)} %get-tuple-element.58), channel_id=1, source_target_pairs={{0,64},{32,96},{1,65},{33,97},{2,66},{34,98},{3,67},{35,99},{4,68}... | collective-permute-start | bytes 1572872 | tf_op jit(solution)/shard_map/ppermute | solution.py:812
  82.3 2.1 %collective-permute-start.7 = (bf16[2,1024,128]{2,1,0:T(8,128)(2,1)}, bf16[2,1024,128]{2,1,0:T(8,128)(2,1)}, u32[]{:S(2)}, u32[]{:S(2)}) collective-permute-start(bf16[2,1024,128]{2,1,0:T(8,128)(2,1)} %get-tuple-element.59), channel_id=1, source_target_pairs={{0,96},{96,64},{1,97},{97,65},{2,98},{98,66},{3,99},{99,67},{4,100... | collective-permute-start | bytes 1572872 | tf_op jit(solution)/shard_map/ppermute | solution.py:812
  84.4 0.0 collective-permute-done.8.refs_9_
  84.4 4.4 %other_phase.5 = (bf16[288,128]{1,0:T(8,128)(2,1)}, f32[16,128]{1,0:T(8,128)}) custom-call(f32[320,128]{1,0:T(8,128)} %get-tuple-element.47.refs_2_.refs_0_, f32[320,128]{1,0:T(8,128)} %copy-done.2, f32[320,128]{1,0:T(8,128)} %copy-done.3, f32[320,128]{1,0:T(8,128)} %copy-done.4, bf16[2,1024,128]{2,1,0:T(8,128)(2,1)} %get-tuple-element.52.refs_4_, ...), custom_call_target="tpu_custom_call" | custom-call | flops 6000000000 | bytes 4000000 | tf_op jit(solution)/shard_map/other_phase/pallas_call | solution.py:723
  88.8 1.2 all-to-all-done.2.refs_0_
  90.0 1.2 chain.3
  91.2 6.2 %all-to-all-start.3 = ((bf16[32,64,128]{2,1,0:T(8,128)(2,1)}), bf16[32,64,128]{2,1,0:T(8,128)(2,1)S(1)}, u32[]{:S(2)}, u32[]{:S(2)}) async-start(bf16[32,64,128]{2,1,0:T(8,128)(2,1)} %chain.3), calls=%async_computation.3 | async-start | bytes 1048576 | tf_op jit(solution)/shard_map/all_to_all | solution.py:807
  97.4 4.4 %other_phase.4 = (bf16[288,128]{1,0:T(8,128)(2,1)}, f32[16,128]{1,0:T(8,128)}) custom-call(f32[320,128]{1,0:T(8,128)} %get-tuple-element.47.refs_2_.refs_0_, f32[320,128]{1,0:T(8,128)} %copy-done.2, f32[320,128]{1,0:T(8,128)} %copy-done.3, f32[320,128]{1,0:T(8,128)} %copy-done.4, bf16[2,1024,128]{2,1,0:T(8,128)(2,1)} %get-tuple-element.52.refs_4_, ...), custom_call_target="tpu_custom_call" | custom-call | flops 6000000000 | bytes 4000000 | tf_op jit(solution)/shard_map/other_phase/pallas_call | solution.py:723
  101.8 0.0 collective-permute-done.5.refs_6_.refs_1_
  101.8 0.0 collective-permute-done.6.refs_7_.refs_2_
  101.8 0.9 collective-permute-done.7.refs_8_.refs_3_
  102.7 6.4 %all-to-all-done.3.refs_5_.refs_6_ = bf16[32,64,128]{2,1,0:T(8,128)(2,1)S(1)} async-done(((bf16[32,64,128]{2,1,0:T(8,128)(2,1)}), bf16[32,64,128]{2,1,0:T(8,128)(2,1)S(1)}, u32[]{:S(2)}, u32[]{:S(2)}) %all-to-all-start.3) | async-done | bytes 524320 | tf_op jit(solution)/shard_map/all_to_all | solution.py:807
  109.2 0.8 copy-done
  109.9 4.4 %later_phase.3 = (bf16[2,1024,128]{2,1,0:T(8,128)(2,1)}, bf16[2,1024,128]{2,1,0:T(8,128)(2,1)}, bf16[2,1024,128]{2,1,0:T(8,128)(2,1)}, bf16[2,1024,128]{2,1,0:T(...) custom-call(f32[320,128]{1,0:T(8,128)} %get-tuple-element.47.refs_2_.refs_0_, ...), custom_call_target="tpu_custom_call" | custom-call | tf_op jit(solution)/shard_map/later_phase/pallas_call | solution.py:702
  114.3 1.9 %collective-permute-start.9 = (bf16[2,1024,128]{2,1,0:T(8,128)(2,1)}, bf16[2,1024,128]{2,1,0:T(8,128)(2,1)S(1)}, u32[]{:S(2)}, u32[]{:S(2)}) collective-permute-start(bf16[2,1024,128]{2,1,0:T(8,128)(2,1)} %get-tuple-element.66), channel_id=1, source_target_pairs={{0,32},{96,0},{1,33},{97,1},{2,34},{98,2},{3,35},{99,3},{4,36},{10... | collective-permute-start | bytes 1572872 | tf_op jit(solution)/shard_map/ppermute | solution.py:812
  116.3 1.3 collective-permute-start.10
  117.6 1.3 collective-permute-start.11
  118.9 6.8 %other_phase.6 = (bf16[2,32,128]{2,1,0:T(8,128)(2,1)}, f32[32,1,128]{2,1,0:T(1,128)}) custom-call(f32[320,128]{1,0:T(8,128)} %get-tuple-element.47.refs_2_.refs_0_, f32[320,128]{1,0:T(8,128)} %copy-done.2, f32[320,128]{1,0:T(8,128)} %copy-done.3, f32[320,128]{1,0:T(8,128)} %copy-done.4, bf16[2,1024,128]{2,1,0:T(8,128)(2,1)} %get-tuple-element.60.refs_4_, ...), custom_call_target="tpu_custom_call" | custom-call | flops 5000000000 | bytes 4000000 | tf_op jit(solution)/shard_map/other_phase/pallas_call | solution.py:723
  125.7 3.8 %all-to-all-start.4 = ((f32[32,1,128]{2,1,0:T(1,128)}), f32[32,1,128]{2,1,0:T(1,128)S(1)}, u32[]{:S(2)}, u32[]{:S(2)}) async-start(f32[32,1,128]{2,1,0:T(1,128)} %get-tuple-element.72), calls=%async_computation.4 | async-start | bytes 32768 | tf_op jit(solution)/shard_map/all_to_all | solution.py:807
  129.6 5.7 %other_phase.7 = (bf16[304,128]{1,0:T(8,128)(2,1)}, bf16[304,128]{1,0:T(8,128)(2,1)}, bf16[304,128]{1,0:T(8,128)(2,1)}, bf16[304,128]{1,0:T(8,128)(2,1)}) custom-call(f32[320,128]{1,0:T(8,128)} %get-tuple-element.47.refs_2_.refs_0_, f32[320,128]{1,0:T(8,128)} %copy-done.2, f32[320,128]{1,0:T(8,128)} %copy-done.3, f32[320,128]{1,0:T(8,128)} %copy-done.4, ...), custom_call_target="tpu_custom_call" | custom-call | flops 5000000000 | bytes 4000000 | tf_op jit(solution)/shard_map/other_phase/pallas_call | solution.py:723
  135.3 1.5 all-to-all-done.4.refs_0_
  136.8 0.6 copy-done.10
  137.4 1.4 rate_sum.1
  138.9 2.7 %collective-permute-start.12 = (bf16[304,128]{1,0:T(8,128)(2,1)}, bf16[304,128]{1,0:T(8,128)(2,1)S(1)}, u32[]{:S(2)}, u32[]{:S(2)}) collective-permute-start(bf16[304,128]{1,0:T(8,128)(2,1)} %get-tuple-element.80), channel_id=1, source_target_pairs={{0,32},{32,64},{64,96},{96,0},{1,33},{33,65},{65,97},{97,1},{2,34}... | collective-permute-start | bytes 233480 | tf_op jit(solution)/shard_map/ppermute | solution.py:812
  141.5 3.2 %collective-permute-start.13 = (bf16[304,128]{1,0:T(8,128)(2,1)}, bf16[304,128]{1,0:T(8,128)(2,1)S(1)}, u32[]{:S(2)}, u32[]{:S(2)}) collective-permute-start(bf16[304,128]{1,0:T(8,128)(2,1)} %get-tuple-element.81), channel_id=1, source_target_pairs={{0,64},{32,96},{64,0},{96,32},{1,65},{33,97},{65,1},{97,33},{2,66}... | collective-permute-start | bytes 233480 | tf_op jit(solution)/shard_map/ppermute | solution.py:812
  144.7 0.0 collective-permute-done.9.refs_5_
  144.7 2.5 %collective-permute-start.14 = (bf16[304,128]{1,0:T(8,128)(2,1)}, bf16[304,128]{1,0:T(8,128)(2,1)S(1)}, u32[]{:S(2)}, u32[]{:S(2)}) collective-permute-start(bf16[304,128]{1,0:T(8,128)(2,1)} %get-tuple-element.82), channel_id=1, source_target_pairs={{0,96},{32,0},{64,32},{96,64},{1,97},{33,1},{65,33},{97,65},{2,98}... | collective-permute-start | bytes 233480 | tf_op jit(solution)/shard_map/ppermute | solution.py:812
  147.3 0.0 collective-permute-done.10.refs_6_
  147.3 0.0 collective-permute-done.11.refs_7_
  147.3 0.0 copy-done.11
  147.3 3.1 %home_grad.1.refs_4_ = bf16[1,2,128,4096]{3,2,1,0:T(8,128)(2,1)} custom-call(bf16[2,1024,128]{2,1,0:T(8,128)(2,1)} %get-tuple-element.56.refs_0_, bf16[2,1024,128]{2,1,0:T(8,128)(2,1)} %collective-permute-done.5.refs_6_.refs_1_, bf16[2,1024,128]{2,1,0:T(8,128)(2,1)} %collective-permute-done.6.refs_7_.refs_2_, ...), custom_call_target="tpu_custom_call" | custom-call | flops 3000000000 | bytes 4000000 | tf_op jit(solution)/shard_map/home_grad/pallas_call | solution.py:776
  150.4 0.0 collective-permute-done.12.refs_1_
  150.4 0.0 collective-permute-done.13.refs_2_
  150.4 0.0 collective-permute-done.14.refs_3_
  150.4 0.6 copy-done.7
  151.0 0.0 copy-done.8
  151.1 0.0 copy-done.9
  151.1 1.8 %home_small.1 = (f32[1,2,64,128]{3,2,1,0:T(8,128)}, f32[1,2,64,128]{3,2,1,0:T(8,128)}, f32[1,2,64,128]{3,2,1,0:T(8,128)}, f32[1,64]{1,0:T(1,128)}, f32[1,64]{1,0:T(1,128)}) custom-call(bf16[304,128]{1,0:T(8,128)(2,1)} %get-tuple-element.79.refs_0_, bf16[304,128]{1,0:T(8,128)(2,1)} %copy-done.7, bf16[304,128]{1,0:T(8,128)(2,1)} %copy-done.8, ...), custom_call_target="tpu_custom_call" | custom-call | tf_op jit(solution)/shard_map/home_small/pallas_call | solution.py:758
  (14 shorter events, 0.0 us)
Async XLA Ops:
  3.2 11.1 %collective-permute-start = (f32[320,128]{1,0:T(8,128)}, f32[320,128]{1,0:T(8,128)S(1)}, u32[]{:S(2)}, u32[]{:S(2)}) collective-permute-start(f32[320,128]{1,0:T(8,128)} %get-tuple-element.48), channel_id=1, source_target_pairs={{0,32},{32,64},{64,96},{96,0},{1,33},{33,65},{65,97},{97,1},{2,34}... | collective-permute-start | bytes 491528 | tf_op jit(solution)/shard_map/ppermute | solution.py:812
  5.3 11.2 %collective-permute-start.1 = (f32[320,128]{1,0:T(8,128)}, f32[320,128]{1,0:T(8,128)S(1)}, u32[]{:S(2)}, u32[]{:S(2)}) collective-permute-start(f32[320,128]{1,0:T(8,128)} %get-tuple-element.49), channel_id=1, source_target_pairs={{0,64},{32,96},{64,0},{96,32},{1,65},{33,97},{65,1},{97,33},{2,66}... | collective-permute-start | bytes 491528 | tf_op jit(solution)/shard_map/ppermute | solution.py:812
  8.9 7.6 %collective-permute-start.2 = (f32[320,128]{1,0:T(8,128)}, f32[320,128]{1,0:T(8,128)S(1)}, u32[]{:S(2)}, u32[]{:S(2)}) collective-permute-start(f32[320,128]{1,0:T(8,128)} %get-tuple-element.50), channel_id=1, source_target_pairs={{0,96},{32,0},{64,32},{96,64},{1,97},{33,1},{65,33},{97,65},{2,98}... | collective-permute-start | bytes 491528 | tf_op jit(solution)/shard_map/ppermute | solution.py:812
  14.3 2.2 %copy-start.2 = (f32[320,128]{1,0:T(8,128)}, f32[320,128]{1,0:T(8,128)S(1)}, u32[]{:S(2)}) copy-start(f32[320,128]{1,0:T(8,128)S(1)} %collective-permute-done.refs_3_.refs_1_) | copy-start | bytes 491524
  16.5 0.7 copy-start.3
  16.5 0.7 copy-start.4
  22.6 23.3 %all-to-all-start = ((bf16[32,112,128]{2,1,0:T(8,128)(2,1)}), bf16[32,112,128]{2,1,0:T(8,128)(2,1)S(1)}, u32[]{:S(2)}, u32[]{:S(2)}) async-start(bf16[32,112,128]{2,1,0:T(8,128)(2,1)} %get-tuple-element.53), calls=%async_computation | async-start | bytes 1835008 | tf_op jit(solution)/shard_map/all_to_all | solution.py:807
  29.9 23.2 %collective-permute-start.3 = (bf16[2,1536,128]{2,1,0:T(8,128)(2,1)}, bf16[2,1536,128]{2,1,0:T(8,128)(2,1)S(1)}, u32[]{:S(2)}, u32[]{:S(2)}) collective-permute-start(bf16[2,1536,128]{2,1,0:T(8,128)(2,1)} %get-tuple-element.54), channel_id=1, source_target_pairs={{0,32},{32,64},{64,96},{96,0},{1,33},{33,65},{65,97},{97,1},{2,34}... | collective-permute-start | bytes 2359304 | tf_op jit(solution)/shard_map/ppermute | solution.py:812
  31.2 22.0 %collective-permute-start.4 = (bf16[2,1536,128]{2,1,0:T(8,128)(2,1)}, bf16[2,1536,128]{2,1,0:T(8,128)(2,1)S(1)}, u32[]{:S(2)}, u32[]{:S(2)}) collective-permute-start(bf16[2,1536,128]{2,1,0:T(8,128)(2,1)} %get-tuple-element.55), channel_id=1, source_target_pairs={{0,96},{32,0},{64,32},{96,64},{1,97},{33,1},{65,33},{97,65},{2,98}... | collective-permute-start | bytes 2359304 | tf_op jit(solution)/shard_map/ppermute | solution.py:812
  47.0 15.7 %all-to-all-start.1 = ((bf16[32,64,128]{2,1,0:T(8,128)(2,1)}), bf16[32,64,128]{2,1,0:T(8,128)(2,1)S(1)}, u32[]{:S(2)}, u32[]{:S(2)}) async-start(bf16[32,64,128]{2,1,0:T(8,128)(2,1)} %chain.2), calls=%async_computation.1 | async-start | bytes 1048576 | tf_op jit(solution)/shard_map/all_to_all | solution.py:807
  50.9 33.5 %collective-permute-start.8 = (bf16[2,1536,128]{2,1,0:T(8,128)(2,1)}, bf16[2,1536,128]{2,1,0:T(8,128)(2,1)}, u32[]{:S(2)}, u32[]{:S(2)}) collective-permute-start(bf16[2,1536,128]{2,1,0:T(8,128)(2,1)} %get-tuple-element.63), channel_id=1, source_target_pairs={{0,64},{32,96},{64,0},{96,32},{1,65},{33,97},{65,1},{97,33},{2,66}... | collective-permute-start | bytes 2359304 | tf_op jit(solution)/shard_map/ppermute | solution.py:812
  53.2 9.5 %copy-start.5 = (bf16[2,1536,128]{2,1,0:T(8,128)(2,1)}, bf16[2,1536,128]{2,1,0:T(8,128)(2,1)S(1)}, u32[]{:S(2)}) copy-start(bf16[2,1536,128]{2,1,0:T(8,128)(2,1)S(1)} %collective-permute-done.3.refs_6_.refs_8_) | copy-start | bytes 2359300
  53.2 9.5 %copy-start.6 = (bf16[2,1536,128]{2,1,0:T(8,128)(2,1)}, bf16[2,1536,128]{2,1,0:T(8,128)(2,1)S(1)}, u32[]{:S(2)}) copy-start(bf16[2,1536,128]{2,1,0:T(8,128)(2,1)S(1)} %collective-permute-done.4.refs_7_.refs_10_) | copy-start | bytes 2359300
  62.7 0.8 copy-start.1
  70.2 19.9 %all-to-all-start.2 = ((bf16[32,112,128]{2,1,0:T(8,128)(2,1)}), bf16[32,112,128]{2,1,0:T(8,128)(2,1)S(1)}, u32[]{:S(2)}, u32[]{:S(2)}) async-start(bf16[32,112,128]{2,1,0:T(8,128)(2,1)} %get-tuple-element.61), calls=%async_computation.2 | async-start | bytes 1835008 | tf_op jit(solution)/shard_map/all_to_all | solution.py:807
  74.1 27.7 %collective-permute-start.5 = (bf16[2,1024,128]{2,1,0:T(8,128)(2,1)}, bf16[2,1024,128]{2,1,0:T(8,128)(2,1)}, u32[]{:S(2)}, u32[]{:S(2)}) collective-permute-start(bf16[2,1024,128]{2,1,0:T(8,128)(2,1)} %get-tuple-element.57), channel_id=1, source_target_pairs={{32,64},{64,96},{33,65},{65,97},{34,66},{66,98},{35,67},{67,99},{3... | collective-permute-start | bytes 1572872 | tf_op jit(solution)/shard_map/ppermute | solution.py:812
  75.6 26.3 %collective-permute-start.6 = (bf16[2,1024,128]{2,1,0:T(8,128)(2,1)}, bf16[2,1024,128]{2,1,0:T(8,128)(2,1)}, u32[]{:S(2)}, u32[]{:S(2)}) collective-permute-start(bf16[2,1024,128]{2,1,0:T(8,128)(2,1)} %get-tuple-element.58), channel_id=1, source_target_pairs={{0,64},{32,96},{1,65},{33,97},{2,66},{34,98},{3,67},{35,99},{4,68}... | collective-permute-start | bytes 1572872 | tf_op jit(solution)/shard_map/ppermute | solution.py:812
  82.3 20.4 %collective-permute-start.7 = (bf16[2,1024,128]{2,1,0:T(8,128)(2,1)}, bf16[2,1024,128]{2,1,0:T(8,128)(2,1)}, u32[]{:S(2)}, u32[]{:S(2)}) collective-permute-start(bf16[2,1024,128]{2,1,0:T(8,128)(2,1)} %get-tuple-element.59), channel_id=1, source_target_pairs={{0,96},{96,64},{1,97},{97,65},{2,98},{98,66},{3,99},{99,67},{4,100... | collective-permute-start | bytes 1572872 | tf_op jit(solution)/shard_map/ppermute | solution.py:812
  91.2 18.0 %all-to-all-start.3 = ((bf16[32,64,128]{2,1,0:T(8,128)(2,1)}), bf16[32,64,128]{2,1,0:T(8,128)(2,1)S(1)}, u32[]{:S(2)}, u32[]{:S(2)}) async-start(bf16[32,64,128]{2,1,0:T(8,128)(2,1)} %chain.3), calls=%async_computation.3 | async-start | bytes 1048576 | tf_op jit(solution)/shard_map/all_to_all | solution.py:807
  109.2 0.8 copy-start
  114.3 30.4 %collective-permute-start.9 = (bf16[2,1024,128]{2,1,0:T(8,128)(2,1)}, bf16[2,1024,128]{2,1,0:T(8,128)(2,1)S(1)}, u32[]{:S(2)}, u32[]{:S(2)}) collective-permute-start(bf16[2,1024,128]{2,1,0:T(8,128)(2,1)} %get-tuple-element.66), channel_id=1, source_target_pairs={{0,32},{96,0},{1,33},{97,1},{2,34},{98,2},{3,35},{99,3},{4,36},{10... | collective-permute-start | bytes 1572872 | tf_op jit(solution)/shard_map/ppermute | solution.py:812
  116.3 31.0 %collective-permute-start.10 = (bf16[2,1024,128]{2,1,0:T(8,128)(2,1)}, bf16[2,1024,128]{2,1,0:T(8,128)(2,1)}, u32[]{:S(2)}, u32[]{:S(2)}) collective-permute-start(bf16[2,1024,128]{2,1,0:T(8,128)(2,1)} %get-tuple-element.67), channel_id=1, source_target_pairs={{64,0},{96,32},{65,1},{97,33},{66,2},{98,34},{67,3},{99,35},{68,4}... | collective-permute-start | bytes 1572872 | tf_op jit(solution)/shard_map/ppermute | solution.py:812
  117.6 29.7 %collective-permute-start.11 = (bf16[2,1024,128]{2,1,0:T(8,128)(2,1)}, bf16[2,1024,128]{2,1,0:T(8,128)(2,1)}, u32[]{:S(2)}, u32[]{:S(2)}) collective-permute-start(bf16[2,1024,128]{2,1,0:T(8,128)(2,1)} %get-tuple-element.68), channel_id=1, source_target_pairs={{32,0},{64,32},{33,1},{65,33},{34,2},{66,34},{35,3},{67,35},{36,4}... | collective-permute-start | bytes 1572872 | tf_op jit(solution)/shard_map/ppermute | solution.py:812
  125.7 11.1 %all-to-all-start.4 = ((f32[32,1,128]{2,1,0:T(1,128)}), f32[32,1,128]{2,1,0:T(1,128)S(1)}, u32[]{:S(2)}, u32[]{:S(2)}) async-start(f32[32,1,128]{2,1,0:T(1,128)} %get-tuple-element.72), calls=%async_computation.4 | async-start | bytes 32768 | tf_op jit(solution)/shard_map/all_to_all | solution.py:807
  136.8 0.6 copy-start.10
  138.9 11.5 %collective-permute-start.12 = (bf16[304,128]{1,0:T(8,128)(2,1)}, bf16[304,128]{1,0:T(8,128)(2,1)S(1)}, u32[]{:S(2)}, u32[]{:S(2)}) collective-permute-start(bf16[304,128]{1,0:T(8,128)(2,1)} %get-tuple-element.80), channel_id=1, source_target_pairs={{0,32},{32,64},{64,96},{96,0},{1,33},{33,65},{65,97},{97,1},{2,34}... | collective-permute-start | bytes 233480 | tf_op jit(solution)/shard_map/ppermute | solution.py:812
  141.5 8.9 %collective-permute-start.13 = (bf16[304,128]{1,0:T(8,128)(2,1)}, bf16[304,128]{1,0:T(8,128)(2,1)S(1)}, u32[]{:S(2)}, u32[]{:S(2)}) collective-permute-start(bf16[304,128]{1,0:T(8,128)(2,1)} %get-tuple-element.81), channel_id=1, source_target_pairs={{0,64},{32,96},{64,0},{96,32},{1,65},{33,97},{65,1},{97,33},{2,66}... | collective-permute-start | bytes 233480 | tf_op jit(solution)/shard_map/ppermute | solution.py:812
  144.7 2.6 %copy-start.11 = (bf16[2,1024,128]{2,1,0:T(8,128)(2,1)}, bf16[2,1024,128]{2,1,0:T(8,128)(2,1)S(1)}, u32[]{:S(2)}) copy-start(bf16[2,1024,128]{2,1,0:T(8,128)(2,1)S(1)} %collective-permute-done.9.refs_5_) | copy-start | bytes 1572868
  144.7 5.7 %collective-permute-start.14 = (bf16[304,128]{1,0:T(8,128)(2,1)}, bf16[304,128]{1,0:T(8,128)(2,1)S(1)}, u32[]{:S(2)}, u32[]{:S(2)}) collective-permute-start(bf16[304,128]{1,0:T(8,128)(2,1)} %get-tuple-element.82), channel_id=1, source_target_pairs={{0,96},{32,0},{64,32},{96,64},{1,97},{33,1},{65,33},{97,65},{2,98}... | collective-permute-start | bytes 233480 | tf_op jit(solution)/shard_map/ppermute | solution.py:812
  150.4 0.6 copy-start.7
  150.4 0.6 copy-start.8
  150.4 0.7 copy-start.9

commit v6 on v5

--- a/solution.py
+++ b/solution.py
@@ -19,7 +19,7 @@
 GROUP = 16
 COLS = GROUP * HEADDIM
 LANES = 128
-CHUNK = 256
+CHUNK = 512
 PER_CHUNK = CHUNK // HEADDIM
 BRANCHES = 32
 SEND_ROWS = 112
@@ -200,9 +200,9 @@
         x_one = x_hat.astype(BF16)
         first = family * GROUP + chunk * PER_CHUNK
         ends = end_ref[first : first + PER_CHUNK].reshape(CHUNK, LANES)
-        top = COLS + (chunk % 2) * CHUNK
+        top = COLS + chunk * CHUNK % (COLS // 2)
         packed = saved_ref[family, top : top + CHUNK, :].astype(F32)
-        if (chunk < 2) != (side == 0):
+        if (chunk * CHUNK < COLS // 2) != (side == 0):
             packed = pltpu.roll(packed, STATE, 1)
         saved = jnp.where((lanes < STATE) == (side == 0), packed, 0.0)
         x_saved = jnp.concatenate([x_one, saved.astype(BF16)], axis=1)

time: 154 us -> 153 us (level)
  no operation moved by 1% of the time
where the time goes in v6:
time: 153 us; the launch traced here: 152 us
  starting transfers between devices  60.8 us (40%)
  Pallas kernels  52.4 us (34%)
  waiting for transfers between devices  34.3 us (22%)
  local copies, waits for them, and re-layouts  3.59 us (2%)
    ppermute x15, starting transfers between devices, send_on(): return lax.ppermute(value, 'section', pairs)  35.4 us
    all_to_all x5, waiting for transfers between devices, swap(): return lax.all_to_all(value, axis, 0, 0, tiled=True)  31.4 us
    all_to_all x5, starting transfers between devices, swap(): return lax.all_to_all(value, axis, 0, 0, tiled=True)  25.4 us
    pallas_call x4, Pallas kernels, other_phase(): pl.pallas_call(functools.partial(other_kernel, high_at, sides, want, len(...  21.4 us
    pallas_call x2, Pallas kernels, later_phase(): pl.pallas_call(functools.partial(later_kernel, high_at, goes_on, len(afte...  10.5 us
    pallas_call x1, Pallas kernels, first_phase(): pl.pallas_call(functools.partial(first_kernel, high_at, len(after)), out_...  4.85 us
    pallas_call x1, Pallas kernels, sort_heads(): pl.pallas_call(sort_kernel, grid_spec=pltpu.PrefetchScalarGridSpec(num_sc...  4.45 us
    unnamed x24, local copies, waits for them, and re-layouts  3.59 us
  transfers between devices with their start and end apart: 20, of which 7 were waited for; matrix products, arithmetic and copies ran while one was open for 0% of the time, Pallas kernels for 26%

profile of v6, /device:TPU:0, one launch (start us, length us, event | category | flops | bytes accessed | tf_op | source)
XLA Modules:
  0.0 152.2 jit_solution(17374020542956062231)
XLA Ops:
  0.6 2.6 %pack_small.1 = (f32[320,128]{1,0:T(8,128)}, f32[320,128]{1,0:T(8,128)}, f32[320,128]{1,0:T(8,128)}, f32[320,128]{1,0:T(8,128)}) custom-call(f32[1,2,64,128]{3,2,1,0:T(8,128)} %bitcast.7, f32[1,2,64,128]{3,2,1,0:T(8,128)} %bitcast.8, f32[1,2,64,128]{3,2,1,0:T(8,128)} %bitcast.9, f32[1,64]{1,0:T(1,128)} %refs_3_.2, f32[1,64]{1,0:T(1,128)} %refs_4_.2), custom_call_target="tpu_custom_call" | custom-call | tf_op jit(solution)/shard_map/pack_small/pallas_call | solution.py:617
  3.2 2.1 %collective-permute-start = (f32[320,128]{1,0:T(8,128)}, f32[320,128]{1,0:T(8,128)S(1)}, u32[]{:S(2)}, u32[]{:S(2)}) collective-permute-start(f32[320,128]{1,0:T(8,128)} %get-tuple-element.48), channel_id=1, source_target_pairs={{0,32},{32,64},{64,96},{96,0},{1,33},{33,65},{65,97},{97,1},{2,34}... | collective-permute-start | bytes 491528 | tf_op jit(solution)/shard_map/ppermute | solution.py:812
  5.3 3.6 %collective-permute-start.1 = (f32[320,128]{1,0:T(8,128)}, f32[320,128]{1,0:T(8,128)S(1)}, u32[]{:S(2)}, u32[]{:S(2)}) collective-permute-start(f32[320,128]{1,0:T(8,128)} %get-tuple-element.49), channel_id=1, source_target_pairs={{0,64},{32,96},{64,0},{96,32},{1,65},{33,97},{65,1},{97,33},{2,66}... | collective-permute-start | bytes 491528 | tf_op jit(solution)/shard_map/ppermute | solution.py:812
  8.9 1.0 collective-permute-start.2
  9.9 4.4 %sort_heads.1 = (bf16[2,1536,128]{2,1,0:T(8,128)(2,1)}, bf16[2,1536,128]{2,1,0:T(8,128)(2,1)}, bf16[2,1536,128]{2,1,0:T(8,128)(2,1)}, bf16[2,1536,128]{2,1,0:T(8,128)(2,1)}) custom-call(s32[1]{0:T(128)} %bitcast.3.at_ref, bf16[1,2,128,4096]{3,2,1,0:T(8,128)(2,1)} %refs_3_.3, bf16[1,2,128,4096]{3,2,1,0:T(8,128)(2,1)} %refs_3_.3, ...), custom_call_target="tpu_custom_call" | custom-call | flops 4000000000 | bytes 4000000 | tf_op jit(solution)/shard_map/sort_heads/pallas_call | solution.py:649
  14.3 0.0 collective-permute-done.refs_3_.refs_1_
  14.3 2.2 %collective-permute-done.1.refs_4_.refs_2_ = f32[320,128]{1,0:T(8,128)S(1)} collective-permute-done((f32[320,128]{1,0:T(8,128)}, f32[320,128]{1,0:T(8,128)S(1)}, u32[]{:S(2)}, u32[]{:S(2)}) %collective-permute-start.1) | collective-permute-done | bytes 163872 | tf_op jit(solution)/shard_map/ppermute | solution.py:812
  16.5 0.0 collective-permute-done.2.refs_5_.refs_3_
  16.5 0.7 copy-done.3
  17.2 0.1 copy-done.4
  17.2 4.9 %first_phase.1 = (bf16[32,112,128]{2,1,0:T(8,128)(2,1)}, bf16[2,1024,128]{2,1,0:T(8,128)(2,1)}) custom-call(s32[2,16]{1,0:T(2,128)} %refs_0_.3, bf16[2,128,4096]{2,1,0:T(8,128)(2,1)} %refs_1_.3, f32[320,128]{1,0:T(8,128)} %get-tuple-element.47.refs_2_.refs_0_, f32[320,128]{1,0:T(8,128)} %copy-done.2, f32[320,128]{1,0:T(8,128)} %copy-done.3, ...), custom_call_target="tpu_custom_call" | custom-call | tf_op jit(solution)/shard_map/first_phase/pallas_call | solution.py:665
  22.1 7.3 %all-to-all-start = ((bf16[32,112,128]{2,1,0:T(8,128)(2,1)}), bf16[32,112,128]{2,1,0:T(8,128)(2,1)S(1)}, u32[]{:S(2)}, u32[]{:S(2)}) async-start(bf16[32,112,128]{2,1,0:T(8,128)(2,1)} %get-tuple-element.53), calls=%async_computation | async-start | bytes 1835008 | tf_op jit(solution)/shard_map/all_to_all | solution.py:807
  29.4 1.2 collective-permute-start.3
  30.7 2.1 %collective-permute-start.4 = (bf16[2,1536,128]{2,1,0:T(8,128)(2,1)}, bf16[2,1536,128]{2,1,0:T(8,128)(2,1)S(1)}, u32[]{:S(2)}, u32[]{:S(2)}) collective-permute-start(bf16[2,1536,128]{2,1,0:T(8,128)(2,1)} %get-tuple-element.55), channel_id=1, source_target_pairs={{0,96},{32,0},{64,32},{96,64},{1,97},{33,1},{65,33},{97,65},{2,98}... | collective-permute-start | bytes 2359304 | tf_op jit(solution)/shard_map/ppermute | solution.py:812
  32.7 12.6 %all-to-all-done.refs_0_ = bf16[32,112,128]{2,1,0:T(8,128)(2,1)S(1)} async-done(((bf16[32,112,128]{2,1,0:T(8,128)(2,1)}), bf16[32,112,128]{2,1,0:T(8,128)(2,1)S(1)}, u32[]{:S(2)}, u32[]{:S(2)}) %all-to-all-start) | async-done | bytes 917536 | tf_op jit(solution)/shard_map/all_to_all | solution.py:807
  45.4 1.2 chain.2
  46.5 3.9 %all-to-all-start.1 = ((bf16[32,64,128]{2,1,0:T(8,128)(2,1)}), bf16[32,64,128]{2,1,0:T(8,128)(2,1)S(1)}, u32[]{:S(2)}, u32[]{:S(2)}) async-start(bf16[32,64,128]{2,1,0:T(8,128)(2,1)} %chain.2), calls=%async_computation.1 | async-start | bytes 1048576 | tf_op jit(solution)/shard_map/all_to_all | solution.py:807
  50.4 2.2 %collective-permute-start.8 = (bf16[2,1536,128]{2,1,0:T(8,128)(2,1)}, bf16[2,1536,128]{2,1,0:T(8,128)(2,1)}, u32[]{:S(2)}, u32[]{:S(2)}) collective-permute-start(bf16[2,1536,128]{2,1,0:T(8,128)(2,1)} %get-tuple-element.63), channel_id=1, source_target_pairs={{0,64},{32,96},{64,0},{96,32},{1,65},{33,97},{65,1},{97,33},{2,66}... | collective-permute-start | bytes 2359304 | tf_op jit(solution)/shard_map/ppermute | solution.py:812
  52.7 0.0 collective-permute-done.3.refs_6_.refs_8_
  52.7 0.0 collective-permute-done.4.refs_7_.refs_10_
  52.7 9.5 %all-to-all-done.1.refs_5_.refs_6_ = bf16[32,64,128]{2,1,0:T(8,128)(2,1)S(1)} async-done(((bf16[32,64,128]{2,1,0:T(8,128)(2,1)}), bf16[32,64,128]{2,1,0:T(8,128)(2,1)S(1)}, u32[]{:S(2)}, u32[]{:S(2)}) %all-to-all-start.1) | async-done | bytes 524320 | tf_op jit(solution)/shard_map/all_to_all | solution.py:807
  62.2 0.8 copy-done.1
  63.0 6.1 %later_phase.2 = (bf16[2,1024,128]{2,1,0:T(8,128)(2,1)}, bf16[2,1024,128]{2,1,0:T(8,128)(2,1)}, bf16[2,1024,128]{2,1,0:T(8,128)(2,1)}, bf16[2,1024,128]{2,1,0:T(...) custom-call(f32[320,128]{1,0:T(8,128)} %get-tuple-element.47.refs_2_.refs_0, ...), custom_call_target="tpu_custom_call" | custom-call | tf_op jit(solution)/shard_map/later_phase/pallas_call | solution.py:702
  69.1 3.9 %all-to-all-start.2 = ((bf16[32,112,128]{2,1,0:T(8,128)(2,1)}), bf16[32,112,128]{2,1,0:T(8,128)(2,1)S(1)}, u32[]{:S(2)}, u32[]{:S(2)}) async-start(bf16[32,112,128]{2,1,0:T(8,128)(2,1)} %get-tuple-element.61), calls=%async_computation.2 | async-start | bytes 1835008 | tf_op jit(solution)/shard_map/all_to_all | solution.py:807
  73.0 1.5 collective-permute-start.5
  74.5 6.7 %collective-permute-start.6 = (bf16[2,1024,128]{2,1,0:T(8,128)(2,1)}, bf16[2,1024,128]{2,1,0:T(8,128)(2,1)}, u32[]{:S(2)}, u32[]{:S(2)}) collective-permute-start(bf16[2,1024,128]{2,1,0:T(8,128)(2,1)} %get-tuple-element.58), channel_id=1, source_target_pairs={{0,64},{32,96},{1,65},{33,97},{2,66},{34,98},{3,67},{35,99},{4,68}... | collective-permute-start | bytes 1572872 | tf_op jit(solution)/shard_map/ppermute | solution.py:812
  81.2 2.1 %collective-permute-start.7 = (bf16[2,1024,128]{2,1,0:T(8,128)(2,1)}, bf16[2,1024,128]{2,1,0:T(8,128)(2,1)}, u32[]{:S(2)}, u32[]{:S(2)}) collective-permute-start(bf16[2,1024,128]{2,1,0:T(8,128)(2,1)} %get-tuple-element.59), channel_id=1, source_target_pairs={{0,96},{96,64},{1,97},{97,65},{2,98},{98,66},{3,99},{99,67},{4,100... | collective-permute-start | bytes 1572872 | tf_op jit(solution)/shard_map/ppermute | solution.py:812
  83.3 0.0 collective-permute-done.8.refs_9_
  83.3 4.4 %other_phase.5 = (bf16[288,128]{1,0:T(8,128)(2,1)}, f32[16,128]{1,0:T(8,128)}) custom-call(f32[320,128]{1,0:T(8,128)} %get-tuple-element.47.refs_2_.refs_0_, f32[320,128]{1,0:T(8,128)} %copy-done.2, f32[320,128]{1,0:T(8,128)} %copy-done.3, f32[320,128]{1,0:T(8,128)} %copy-done.4, bf16[2,1024,128]{2,1,0:T(8,128)(2,1)} %get-tuple-element.52.refs_4_, ...), custom_call_target="tpu_custom_call" | custom-call | flops 6000000000 | bytes 4000000 | tf_op jit(solution)/shard_map/other_phase/pallas_call | solution.py:723
  87.8 1.2 all-to-all-done.2.refs_0_
  89.0 1.2 chain.3
  90.1 6.4 %all-to-all-start.3 = ((bf16[32,64,128]{2,1,0:T(8,128)(2,1)}), bf16[32,64,128]{2,1,0:T(8,128)(2,1)S(1)}, u32[]{:S(2)}, u32[]{:S(2)}) async-start(bf16[32,64,128]{2,1,0:T(8,128)(2,1)} %chain.3), calls=%async_computation.3 | async-start | bytes 1048576 | tf_op jit(solution)/shard_map/all_to_all | solution.py:807
  96.5 4.4 %other_phase.4 = (bf16[288,128]{1,0:T(8,128)(2,1)}, f32[16,128]{1,0:T(8,128)}) custom-call(f32[320,128]{1,0:T(8,128)} %get-tuple-element.47.refs_2_.refs_0_, f32[320,128]{1,0:T(8,128)} %copy-done.2, f32[320,128]{1,0:T(8,128)} %copy-done.3, f32[320,128]{1,0:T(8,128)} %copy-done.4, bf16[2,1024,128]{2,1,0:T(8,128)(2,1)} %get-tuple-element.52.refs_4_, ...), custom_call_target="tpu_custom_call" | custom-call | flops 6000000000 | bytes 4000000 | tf_op jit(solution)/shard_map/other_phase/pallas_call | solution.py:723
  101.0 0.0 collective-permute-done.5.refs_6_.refs_1_
  101.0 0.0 collective-permute-done.6.refs_7_.refs_2_
  101.0 0.7 collective-permute-done.7.refs_8_.refs_3_
  101.7 6.6 %all-to-all-done.3.refs_5_.refs_6_ = bf16[32,64,128]{2,1,0:T(8,128)(2,1)S(1)} async-done(((bf16[32,64,128]{2,1,0:T(8,128)(2,1)}), bf16[32,64,128]{2,1,0:T(8,128)(2,1)S(1)}, u32[]{:S(2)}, u32[]{:S(2)}) %all-to-all-start.3) | async-done | bytes 524320 | tf_op jit(solution)/shard_map/all_to_all | solution.py:807
  108.3 0.8 copy-done
  109.1 4.4 %later_phase.3 = (bf16[2,1024,128]{2,1,0:T(8,128)(2,1)}, bf16[2,1024,128]{2,1,0:T(8,128)(2,1)}, bf16[2,1024,128]{2,1,0:T(8,128)(2,1)}, bf16[2,1024,128]{2,1,0:T(...) custom-call(f32[320,128]{1,0:T(8,128)} %get-tuple-element.47.refs_2_.refs_0_, ...), custom_call_target="tpu_custom_call" | custom-call | tf_op jit(solution)/shard_map/later_phase/pallas_call | solution.py:702
  113.5 1.9 %collective-permute-start.9 = (bf16[2,1024,128]{2,1,0:T(8,128)(2,1)}, bf16[2,1024,128]{2,1,0:T(8,128)(2,1)S(1)}, u32[]{:S(2)}, u32[]{:S(2)}) collective-permute-start(bf16[2,1024,128]{2,1,0:T(8,128)(2,1)} %get-tuple-element.66), channel_id=1, source_target_pairs={{0,32},{96,0},{1,33},{97,1},{2,34},{98,2},{3,35},{99,3},{4,36},{10... | collective-permute-start | bytes 1572872 | tf_op jit(solution)/shard_map/ppermute | solution.py:812
  115.4 1.3 collective-permute-start.10
  116.7 1.3 collective-permute-start.11
  118.0 6.8 %other_phase.6 = (bf16[2,32,128]{2,1,0:T(8,128)(2,1)}, f32[32,1,128]{2,1,0:T(1,128)}) custom-call(f32[320,128]{1,0:T(8,128)} %get-tuple-element.47.refs_2_.refs_0_, f32[320,128]{1,0:T(8,128)} %copy-done.2, f32[320,128]{1,0:T(8,128)} %copy-done.3, f32[320,128]{1,0:T(8,128)} %copy-done.4, bf16[2,1024,128]{2,1,0:T(8,128)(2,1)} %get-tuple-element.60.refs_4_, ...), custom_call_target="tpu_custom_call" | custom-call | flops 5000000000 | bytes 4000000 | tf_op jit(solution)/shard_map/other_phase/pallas_call | solution.py:723
  124.8 3.8 %all-to-all-start.4 = ((f32[32,1,128]{2,1,0:T(1,128)}), f32[32,1,128]{2,1,0:T(1,128)S(1)}, u32[]{:S(2)}, u32[]{:S(2)}) async-start(f32[32,1,128]{2,1,0:T(1,128)} %get-tuple-element.72), calls=%async_computation.4 | async-start | bytes 32768 | tf_op jit(solution)/shard_map/all_to_all | solution.py:807
  128.7 5.7 %other_phase.7 = (bf16[304,128]{1,0:T(8,128)(2,1)}, bf16[304,128]{1,0:T(8,128)(2,1)}, bf16[304,128]{1,0:T(8,128)(2,1)}, bf16[304,128]{1,0:T(8,128)(2,1)}) custom-call(f32[320,128]{1,0:T(8,128)} %get-tuple-element.47.refs_2_.refs_0_, f32[320,128]{1,0:T(8,128)} %copy-done.2, f32[320,128]{1,0:T(8,128)} %copy-done.3, f32[320,128]{1,0:T(8,128)} %copy-done.4, ...), custom_call_target="tpu_custom_call" | custom-call | flops 5000000000 | bytes 4000000 | tf_op jit(solution)/shard_map/other_phase/pallas_call | solution.py:723
  134.4 1.5 all-to-all-done.4.refs_0_
  135.9 0.6 copy-done.10
  136.6 1.4 rate_sum.1
  138.0 2.7 %collective-permute-start.12 = (bf16[304,128]{1,0:T(8,128)(2,1)}, bf16[304,128]{1,0:T(8,128)(2,1)S(1)}, u32[]{:S(2)}, u32[]{:S(2)}) collective-permute-start(bf16[304,128]{1,0:T(8,128)(2,1)} %get-tuple-element.80), channel_id=1, source_target_pairs={{0,32},{32,64},{64,96},{96,0},{1,33},{33,65},{65,97},{97,1},{2,34}... | collective-permute-start | bytes 233480 | tf_op jit(solution)/shard_map/ppermute | solution.py:812
  140.7 3.2 %collective-permute-start.13 = (bf16[304,128]{1,0:T(8,128)(2,1)}, bf16[304,128]{1,0:T(8,128)(2,1)S(1)}, u32[]{:S(2)}, u32[]{:S(2)}) collective-permute-start(bf16[304,128]{1,0:T(8,128)(2,1)} %get-tuple-element.81), channel_id=1, source_target_pairs={{0,64},{32,96},{64,0},{96,32},{1,65},{33,97},{65,1},{97,33},{2,66}... | collective-permute-start | bytes 233480 | tf_op jit(solution)/shard_map/ppermute | solution.py:812
  143.8 0.0 collective-permute-done.9.refs_5_
  143.8 2.5 %collective-permute-start.14 = (bf16[304,128]{1,0:T(8,128)(2,1)}, bf16[304,128]{1,0:T(8,128)(2,1)S(1)}, u32[]{:S(2)}, u32[]{:S(2)}) collective-permute-start(bf16[304,128]{1,0:T(8,128)(2,1)} %get-tuple-element.82), channel_id=1, source_target_pairs={{0,96},{32,0},{64,32},{96,64},{1,97},{33,1},{65,33},{97,65},{2,98}... | collective-permute-start | bytes 233480 | tf_op jit(solution)/shard_map/ppermute | solution.py:812
  146.4 0.0 collective-permute-done.10.refs_6_
  146.4 0.0 collective-permute-done.11.refs_7_
  146.4 0.0 copy-done.11
  146.4 3.1 %home_grad.1.refs_4_ = bf16[1,2,128,4096]{3,2,1,0:T(8,128)(2,1)} custom-call(bf16[2,1024,128]{2,1,0:T(8,128)(2,1)} %get-tuple-element.56.refs_0_, bf16[2,1024,128]{2,1,0:T(8,128)(2,1)} %collective-permute-done.5.refs_6_.refs_1_, bf16[2,1024,128]{2,1,0:T(8,128)(2,1)} %collective-permute-done.6.refs_7_.refs_2_, ...), custom_call_target="tpu_custom_call" | custom-call | flops 3000000000 | bytes 4000000 | tf_op jit(solution)/shard_map/home_grad/pallas_call | solution.py:776
  149.5 0.0 collective-permute-done.12.refs_1_
  149.5 0.0 copy-start.7
  149.5 0.0 collective-permute-done.13.refs_2_
  149.5 0.0 collective-permute-done.14.refs_3_
  149.6 0.6 copy-done.7
  150.1 0.0 copy-done.8
  150.2 0.0 copy-done.9
  150.2 1.8 %home_small.1 = (f32[1,2,64,128]{3,2,1,0:T(8,128)}, f32[1,2,64,128]{3,2,1,0:T(8,128)}, f32[1,2,64,128]{3,2,1,0:T(8,128)}, f32[1,64]{1,0:T(1,128)}, f32[1,64]{1,0:T(1,128)}) custom-call(bf16[304,128]{1,0:T(8,128)(2,1)} %get-tuple-element.79.refs_0_, bf16[304,128]{1,0:T(8,128)(2,1)} %copy-done.7, bf16[304,128]{1,0:T(8,128)(2,1)} %copy-done.8, ...), custom_call_target="tpu_custom_call" | custom-call | tf_op jit(solution)/shard_map/home_small/pallas_call | solution.py:758
  (14 shorter events, 0.0 us)
Async XLA Ops:
  3.2 11.1 %collective-permute-start = (f32[320,128]{1,0:T(8,128)}, f32[320,128]{1,0:T(8,128)S(1)}, u32[]{:S(2)}, u32[]{:S(2)}) collective-permute-start(f32[320,128]{1,0:T(8,128)} %get-tuple-element.48), channel_id=1, source_target_pairs={{0,32},{32,64},{64,96},{96,0},{1,33},{33,65},{65,97},{97,1},{2,34}... | collective-permute-start | bytes 491528 | tf_op jit(solution)/shard_map/ppermute | solution.py:812
  5.3 11.2 %collective-permute-start.1 = (f32[320,128]{1,0:T(8,128)}, f32[320,128]{1,0:T(8,128)S(1)}, u32[]{:S(2)}, u32[]{:S(2)}) collective-permute-start(f32[320,128]{1,0:T(8,128)} %get-tuple-element.49), channel_id=1, source_target_pairs={{0,64},{32,96},{64,0},{96,32},{1,65},{33,97},{65,1},{97,33},{2,66}... | collective-permute-start | bytes 491528 | tf_op jit(solution)/shard_map/ppermute | solution.py:812
  8.9 7.6 %collective-permute-start.2 = (f32[320,128]{1,0:T(8,128)}, f32[320,128]{1,0:T(8,128)S(1)}, u32[]{:S(2)}, u32[]{:S(2)}) collective-permute-start(f32[320,128]{1,0:T(8,128)} %get-tuple-element.50), channel_id=1, source_target_pairs={{0,96},{32,0},{64,32},{96,64},{1,97},{33,1},{65,33},{97,65},{2,98}... | collective-permute-start | bytes 491528 | tf_op jit(solution)/shard_map/ppermute | solution.py:812
  14.3 2.2 %copy-start.2 = (f32[320,128]{1,0:T(8,128)}, f32[320,128]{1,0:T(8,128)S(1)}, u32[]{:S(2)}) copy-start(f32[320,128]{1,0:T(8,128)S(1)} %collective-permute-done.refs_3_.refs_1_) | copy-start | bytes 491524
  16.5 0.7 copy-start.3
  16.5 0.7 copy-start.4
  22.1 23.3 %all-to-all-start = ((bf16[32,112,128]{2,1,0:T(8,128)(2,1)}), bf16[32,112,128]{2,1,0:T(8,128)(2,1)S(1)}, u32[]{:S(2)}, u32[]{:S(2)}) async-start(bf16[32,112,128]{2,1,0:T(8,128)(2,1)} %get-tuple-element.53), calls=%async_computation | async-start | bytes 1835008 | tf_op jit(solution)/shard_map/all_to_all | solution.py:807
  29.4 23.2 %collective-permute-start.3 = (bf16[2,1536,128]{2,1,0:T(8,128)(2,1)}, bf16[2,1536,128]{2,1,0:T(8,128)(2,1)S(1)}, u32[]{:S(2)}, u32[]{:S(2)}) collective-permute-start(bf16[2,1536,128]{2,1,0:T(8,128)(2,1)} %get-tuple-element.54), channel_id=1, source_target_pairs={{0,32},{32,64},{64,96},{96,0},{1,33},{33,65},{65,97},{97,1},{2,34}... | collective-permute-start | bytes 2359304 | tf_op jit(solution)/shard_map/ppermute | solution.py:812
  30.7 22.0 %collective-permute-start.4 = (bf16[2,1536,128]{2,1,0:T(8,128)(2,1)}, bf16[2,1536,128]{2,1,0:T(8,128)(2,1)S(1)}, u32[]{:S(2)}, u32[]{:S(2)}) collective-permute-start(bf16[2,1536,128]{2,1,0:T(8,128)(2,1)} %get-tuple-element.55), channel_id=1, source_target_pairs={{0,96},{32,0},{64,32},{96,64},{1,97},{33,1},{65,33},{97,65},{2,98}... | collective-permute-start | bytes 2359304 | tf_op jit(solution)/shard_map/ppermute | solution.py:812
  46.5 15.7 %all-to-all-start.1 = ((bf16[32,64,128]{2,1,0:T(8,128)(2,1)}), bf16[32,64,128]{2,1,0:T(8,128)(2,1)S(1)}, u32[]{:S(2)}, u32[]{:S(2)}) async-start(bf16[32,64,128]{2,1,0:T(8,128)(2,1)} %chain.2), calls=%async_computation.1 | async-start | bytes 1048576 | tf_op jit(solution)/shard_map/all_to_all | solution.py:807
  50.4 32.9 %collective-permute-start.8 = (bf16[2,1536,128]{2,1,0:T(8,128)(2,1)}, bf16[2,1536,128]{2,1,0:T(8,128)(2,1)}, u32[]{:S(2)}, u32[]{:S(2)}) collective-permute-start(bf16[2,1536,128]{2,1,0:T(8,128)(2,1)} %get-tuple-element.63), channel_id=1, source_target_pairs={{0,64},{32,96},{64,0},{96,32},{1,65},{33,97},{65,1},{97,33},{2,66}... | collective-permute-start | bytes 2359304 | tf_op jit(solution)/shard_map/ppermute | solution.py:812
  52.7 9.5 %copy-start.5 = (bf16[2,1536,128]{2,1,0:T(8,128)(2,1)}, bf16[2,1536,128]{2,1,0:T(8,128)(2,1)S(1)}, u32[]{:S(2)}) copy-start(bf16[2,1536,128]{2,1,0:T(8,128)(2,1)S(1)} %collective-permute-done.3.refs_6_.refs_8_) | copy-start | bytes 2359300
  52.7 9.5 %copy-start.6 = (bf16[2,1536,128]{2,1,0:T(8,128)(2,1)}, bf16[2,1536,128]{2,1,0:T(8,128)(2,1)S(1)}, u32[]{:S(2)}) copy-start(bf16[2,1536,128]{2,1,0:T(8,128)(2,1)S(1)} %collective-permute-done.4.refs_7_.refs_10_) | copy-start | bytes 2359300
  62.2 0.8 copy-start.1
  69.1 19.9 %all-to-all-start.2 = ((bf16[32,112,128]{2,1,0:T(8,128)(2,1)}), bf16[32,112,128]{2,1,0:T(8,128)(2,1)S(1)}, u32[]{:S(2)}, u32[]{:S(2)}) async-start(bf16[32,112,128]{2,1,0:T(8,128)(2,1)} %get-tuple-element.61), calls=%async_computation.2 | async-start | bytes 1835008 | tf_op jit(solution)/shard_map/all_to_all | solution.py:807
  73.0 27.9 %collective-permute-start.5 = (bf16[2,1024,128]{2,1,0:T(8,128)(2,1)}, bf16[2,1024,128]{2,1,0:T(8,128)(2,1)}, u32[]{:S(2)}, u32[]{:S(2)}) collective-permute-start(bf16[2,1024,128]{2,1,0:T(8,128)(2,1)} %get-tuple-element.57), channel_id=1, source_target_pairs={{32,64},{64,96},{33,65},{65,97},{34,66},{66,98},{35,67},{67,99},{3... | collective-permute-start | bytes 1572872 | tf_op jit(solution)/shard_map/ppermute | solution.py:812
  74.5 26.5 %collective-permute-start.6 = (bf16[2,1024,128]{2,1,0:T(8,128)(2,1)}, bf16[2,1024,128]{2,1,0:T(8,128)(2,1)}, u32[]{:S(2)}, u32[]{:S(2)}) collective-permute-start(bf16[2,1024,128]{2,1,0:T(8,128)(2,1)} %get-tuple-element.58), channel_id=1, source_target_pairs={{0,64},{32,96},{1,65},{33,97},{2,66},{34,98},{3,67},{35,99},{4,68}... | collective-permute-start | bytes 1572872 | tf_op jit(solution)/shard_map/ppermute | solution.py:812
  81.2 20.4 %collective-permute-start.7 = (bf16[2,1024,128]{2,1,0:T(8,128)(2,1)}, bf16[2,1024,128]{2,1,0:T(8,128)(2,1)}, u32[]{:S(2)}, u32[]{:S(2)}) collective-permute-start(bf16[2,1024,128]{2,1,0:T(8,128)(2,1)} %get-tuple-element.59), channel_id=1, source_target_pairs={{0,96},{96,64},{1,97},{97,65},{2,98},{98,66},{3,99},{99,67},{4,100... | collective-permute-start | bytes 1572872 | tf_op jit(solution)/shard_map/ppermute | solution.py:812
  90.1 18.2 %all-to-all-start.3 = ((bf16[32,64,128]{2,1,0:T(8,128)(2,1)}), bf16[32,64,128]{2,1,0:T(8,128)(2,1)S(1)}, u32[]{:S(2)}, u32[]{:S(2)}) async-start(bf16[32,64,128]{2,1,0:T(8,128)(2,1)} %chain.3), calls=%async_computation.3 | async-start | bytes 1048576 | tf_op jit(solution)/shard_map/all_to_all | solution.py:807
  108.3 0.8 copy-start
  113.5 30.4 %collective-permute-start.9 = (bf16[2,1024,128]{2,1,0:T(8,128)(2,1)}, bf16[2,1024,128]{2,1,0:T(8,128)(2,1)S(1)}, u32[]{:S(2)}, u32[]{:S(2)}) collective-permute-start(bf16[2,1024,128]{2,1,0:T(8,128)(2,1)} %get-tuple-element.66), channel_id=1, source_target_pairs={{0,32},{96,0},{1,33},{97,1},{2,34},{98,2},{3,35},{99,3},{4,36},{10... | collective-permute-start | bytes 1572872 | tf_op jit(solution)/shard_map/ppermute | solution.py:812
  115.4 31.0 %collective-permute-start.10 = (bf16[2,1024,128]{2,1,0:T(8,128)(2,1)}, bf16[2,1024,128]{2,1,0:T(8,128)(2,1)}, u32[]{:S(2)}, u32[]{:S(2)}) collective-permute-start(bf16[2,1024,128]{2,1,0:T(8,128)(2,1)} %get-tuple-element.67), channel_id=1, source_target_pairs={{64,0},{96,32},{65,1},{97,33},{66,2},{98,34},{67,3},{99,35},{68,4}... | collective-permute-start | bytes 1572872 | tf_op jit(solution)/shard_map/ppermute | solution.py:812
  116.7 29.7 %collective-permute-start.11 = (bf16[2,1024,128]{2,1,0:T(8,128)(2,1)}, bf16[2,1024,128]{2,1,0:T(8,128)(2,1)}, u32[]{:S(2)}, u32[]{:S(2)}) collective-permute-start(bf16[2,1024,128]{2,1,0:T(8,128)(2,1)} %get-tuple-element.68), channel_id=1, source_target_pairs={{32,0},{64,32},{33,1},{65,33},{34,2},{66,34},{35,3},{67,35},{36,4}... | collective-permute-start | bytes 1572872 | tf_op jit(solution)/shard_map/ppermute | solution.py:812
  124.8 11.1 %all-to-all-start.4 = ((f32[32,1,128]{2,1,0:T(1,128)}), f32[32,1,128]{2,1,0:T(1,128)S(1)}, u32[]{:S(2)}, u32[]{:S(2)}) async-start(f32[32,1,128]{2,1,0:T(1,128)} %get-tuple-element.72), calls=%async_computation.4 | async-start | bytes 32768 | tf_op jit(solution)/shard_map/all_to_all | solution.py:807
  135.9 0.6 copy-start.10
  138.0 11.5 %collective-permute-start.12 = (bf16[304,128]{1,0:T(8,128)(2,1)}, bf16[304,128]{1,0:T(8,128)(2,1)S(1)}, u32[]{:S(2)}, u32[]{:S(2)}) collective-permute-start(bf16[304,128]{1,0:T(8,128)(2,1)} %get-tuple-element.80), channel_id=1, source_target_pairs={{0,32},{32,64},{64,96},{96,0},{1,33},{33,65},{65,97},{97,1},{2,34}... | collective-permute-start | bytes 233480 | tf_op jit(solution)/shard_map/ppermute | solution.py:812
  140.7 8.9 %collective-permute-start.13 = (bf16[304,128]{1,0:T(8,128)(2,1)}, bf16[304,128]{1,0:T(8,128)(2,1)S(1)}, u32[]{:S(2)}, u32[]{:S(2)}) collective-permute-start(bf16[304,128]{1,0:T(8,128)(2,1)} %get-tuple-element.81), channel_id=1, source_target_pairs={{0,64},{32,96},{64,0},{96,32},{1,65},{33,97},{65,1},{97,33},{2,66}... | collective-permute-start | bytes 233480 | tf_op jit(solution)/shard_map/ppermute | solution.py:812
  143.8 2.6 %copy-start.11 = (bf16[2,1024,128]{2,1,0:T(8,128)(2,1)}, bf16[2,1024,128]{2,1,0:T(8,128)(2,1)S(1)}, u32[]{:S(2)}) copy-start(bf16[2,1024,128]{2,1,0:T(8,128)(2,1)S(1)} %collective-permute-done.9.refs_5_) | copy-start | bytes 1572868
  143.8 5.7 %collective-permute-start.14 = (bf16[304,128]{1,0:T(8,128)(2,1)}, bf16[304,128]{1,0:T(8,128)(2,1)S(1)}, u32[]{:S(2)}, u32[]{:S(2)}) collective-permute-start(bf16[304,128]{1,0:T(8,128)(2,1)} %get-tuple-element.82), channel_id=1, source_target_pairs={{0,96},{32,0},{64,32},{96,64},{1,97},{33,1},{65,33},{97,65},{2,98}... | collective-permute-start | bytes 233480 | tf_op jit(solution)/shard_map/ppermute | solution.py:812
  149.5 0.6 copy-start.7
  149.5 0.6 copy-start.8
  149.6 0.7 copy-start.9
